TPU v7x, 32 devices: a whole 2x2x4 slice. The times are simulated.
32 devices in a mesh: groups: 2 (over y), curve: 4 (over z), sub: 2 (over x), pair: 2 (over core).
Axes of the slice: x: 2, y: 2, z: 4, core: 2. Of those that a mesh axis runs over, the one named last changes fastest.
Arguments:
- state: float32 [16384, 512], P(('groups', 'curve', 'sub', 'pair')), parts along dimension 0, may hold values from -6 to 6
- velocity: float32 [3, 16384], P(None, ('groups', 'curve', 'sub', 'pair')), parts along dimension 1, may hold values from -4 to 4
- levels: int32 [16384], P(('groups', 'curve', 'sub', 'pair')), parts along dimension 0, may hold values from 0 to 3
- neighbours: int32 [6, 16384], P(None, ('groups', 'curve', 'sub', 'pair')), parts along dimension 1, may hold values from -1 to 8191, as said below
- records: int32 [4, 8192], P(None, ('groups', 'curve', 'sub', 'pair')), parts along dimension 1, may hold values from 0 to 511, as said below
- counts: int32 [32, 8], P(('groups', 'curve', 'sub', 'pair')), parts along dimension 0, may hold values from 0 to 32, as said below
- stiffness: bfloat16 [512, 1536], replicated, may hold values from -0.25 to 0.25
- trace_map: bfloat16 [512, 384], replicated, may hold values from -0.25 to 0.25
- lift: bfloat16 [384, 512], replicated, may hold values from -0.75 to 0.75
- projection: bfloat16 [64, 512], replicated, may hold values from -0.75 to 0.75
Outputs:
- stepped: float32 [16384, 512], P(('groups', 'curve', 'sub', 'pair')), parts along dimension 0
There are 2 independent parts, one for each index of `groups`. A program takes and returns all parts, laid end to end along the dimension named above; an argument that names none is the same for every part. Nothing has to cross between parts.
Inputs may be any that keep to these rules, and one draw needn't show every extreme that they name: `neighbours`: A neighbour is -1 or an element of the same partition, one of the last 64 elements of the partition before it, or one of the first 64 elements of the partition after it; both ends are reached. `records`: rows 0 and 3 hold element numbers within a partition, row 1 a face 0 to 5, row 2 a projection id 0 to 7. The columns of partition s are its slots ordered by offset index j, then slot k. counts[s, j] is 0 exactly where s + o_j lies outside 0 to 15, else 1 to 32; some partition receives 32 live records from each of its nearby partitions.
All inputs are finite; a program needn't handle non-finite values.
Results may differ from a plain program's by a relative error of at most 0.0046.
Values may be sent and summed in bfloat16 or wider, within the bound.
No kernel may reach another device: no remote copies, remote signals or barrier semaphores. Data moves between devices by JAX's collectives and lax.ppermute only.
A program may use at most 64 MiB of HBM per device.

v0:
```python
import jax
import jax.numpy as jnp
from jax import lax
from jax.sharding import PartitionSpec as P

time_step = 0.3


def passed_along(x, axis, by):
    length = lax.axis_size(axis)
    pairs = [(i, i + by) for i in range(length) if 0 <= i + by < length]
    return lax.ppermute(x, axis, pairs)


def padded_2(cells, sides, width):
    for axis, dim in sides:
        count = lax.axis_size(axis)
        ends = count - 1
        head = lax.slice_in_dim(cells, 0, width, axis=dim)
        tail = lax.slice_in_dim(cells, cells.shape[dim] - width, cells.shape[dim], axis=dim)
        cells = jnp.concatenate(
            [
                lax.ppermute(tail, axis, [(i, (i + 1) % count) for i in range(ends)]),
                cells,
                lax.ppermute(head, axis, [((i + 1) % count, i) for i in range(ends)]),
            ],
            axis=dim,
        )
    return cells


def inflow_speeds(velocity):
    ahead = jnp.maximum(velocity, 0.0)
    behind = jnp.maximum(-velocity, 0.0)
    return jnp.stack([ahead[0], behind[0], ahead[1], behind[1], ahead[2], behind[2]], axis=1)


def tendency(
    field, velocity, levels, neighbours, records, counts, stiffness, trace_map, lift, projection
):
    elements = field.shape[0]
    face_modes = projection.shape[0]
    width = 6 * face_modes
    position = lax.axis_index(("curve", "sub", "pair"))
    offset_count = counts.shape[1]
    reach = offset_count // 2
    slots = records.shape[1]
    capacity = slots // offset_count
    rim = elements // 8
    lowered = field.astype(jnp.bfloat16)
    moved = jnp.dot(lowered, stiffness, preferred_element_type=jnp.float32).reshape(elements, 3, -1)
    volume = (
        velocity[0][:, None] * moved[:, 0]
        + velocity[1][:, None] * moved[:, 1]
        + velocity[2][:, None] * moved[:, 2]
    )
    traces = jnp.dot(lowered, trace_map, preferred_element_type=jnp.float32).astype(jnp.bfloat16)
    slot_ids = jnp.arange(slots, dtype=jnp.int32)
    kinds = jnp.arange(8, dtype=jnp.int32)[None, :]
    face_ids = jnp.arange(6, dtype=jnp.int32)[None, :]
    element_ids = jnp.arange(elements, dtype=jnp.int32)
    source_hot = (records[0][:, None] == element_ids[None, :]).astype(jnp.bfloat16)
    source_rows = jnp.dot(source_hot, traces, preferred_element_type=jnp.float32).reshape(
        slots, 6, face_modes
    )
    face_pick = (records[1][:, None] == face_ids).astype(jnp.float32)
    rows = jnp.sum(source_rows * face_pick[:, :, None], axis=1).astype(jnp.bfloat16)
    every = jnp.dot(rows, projection, preferred_element_type=jnp.float32).reshape(
        slots, 8, face_modes
    )
    select = (records[2][:, None] == kinds).astype(jnp.float32)
    piece = jnp.sum(every * select[:, :, None], axis=1).astype(jnp.bfloat16)
    live = slot_ids % capacity < counts[0][slot_ids // capacity]
    code = jnp.where(live, records[3] * 6 + jnp.bitwise_xor(records[1], 1) + 1, 0)
    blocks = piece.reshape(offset_count, capacity, face_modes)
    codes = code.reshape(offset_count, capacity)
    offsets = [j - reach if j < reach else j - reach + 1 for j in range(offset_count)]
    got_pieces = []
    got_codes = []
    for j in range(offset_count):
        got_piece, got_code = passed_along(
            (blocks[j], codes[j]), ("curve", "sub", "pair"), offsets[j]
        )
        got_pieces.append(got_piece)
        got_codes.append(got_code)
    arrived = jnp.stack(got_pieces, axis=0).reshape(-1, face_modes)
    aimed = jnp.stack(got_codes, axis=0).reshape(-1)
    target_element = jnp.where(aimed > 0, (aimed - 1) // 6, -1).astype(jnp.int32)
    target_face = jnp.where(aimed > 0, (aimed - 1) % 6, 0).astype(jnp.int32)
    face_hot = (target_face[:, None] == face_ids).astype(jnp.bfloat16)
    placed = (arrived[:, None, :] * face_hot[:, :, None]).reshape(-1, width)
    element_hot = (element_ids[:, None] == target_element[None, :]).astype(jnp.bfloat16)
    mortar = jnp.dot(element_hot, placed, preferred_element_type=jnp.float32)
    padded = padded_2(traces, ((("curve", "sub", "pair"), 0),), rim)
    window = jnp.arange(elements + 2 * rim, dtype=jnp.int32)[None, :]
    valid = neighbours >= 0
    shifted = jnp.where(valid, neighbours - position * elements + rim, -1)
    pieces = []
    for face in range(6):
        other = face ^ 1
        picker = (shifted[face][:, None] == window).astype(jnp.bfloat16)
        column = padded[:, other * face_modes : (other + 1) * face_modes]
        pieces.append(jnp.dot(picker, column, preferred_element_type=jnp.float32))
    conforming = jnp.concatenate(pieces, axis=1)
    own = traces.astype(jnp.float32)
    speeds = jnp.repeat(inflow_speeds(velocity), face_modes, axis=1)
    flux = (speeds * (conforming + mortar - own)).astype(jnp.bfloat16)
    lifted = jnp.dot(flux, lift, preferred_element_type=jnp.float32)
    scale = jnp.exp2(levels.astype(jnp.float32)) * 0.25
    return scale[:, None] * (volume + lifted)


def body(
    state, velocity, levels, neighbours, records, counts, stiffness, trace_map, lift, projection
):
    extra = (velocity, levels, neighbours, records, counts, stiffness, trace_map, lift, projection)
    first = state + time_step * tendency(state, *extra)
    second = first + time_step * tendency(first, *extra)
    return 0.5 * state + 0.5 * second


def solution(mesh):
    placed = (
        P(("groups", "curve", "sub", "pair"), None),
        P(None, ("groups", "curve", "sub", "pair")),
        P(("groups", "curve", "sub", "pair")),
        P(None, ("groups", "curve", "sub", "pair")),
        P(None, ("groups", "curve", "sub", "pair")),
        P(("groups", "curve", "sub", "pair"), None),
        P(),
        P(),
        P(),
        P(),
    )
    return jax.shard_map(
        body,
        mesh=mesh,
        in_specs=placed,
        out_specs=P(("groups", "curve", "sub", "pair"), None),
        check_vma=False,
    )
```

profile of v0, /device:TPU:0, one launch (start us, length us, event | category | flops | bytes accessed | tf_op | source)
XLA Modules:
  0.0 164.1 jit_solution(13083426517795056399)
XLA Ops:
  3.2 3.0 %collective-permute-start = (bf16[64,384]{1,0:T(8,128)(2,1)S(1)}, bf16[64,384]{1,0:T(8,128)(2,1)S(1)}, u32[]{:S(2)}, u32[]{:S(2)}) collective-permute-start(bf16[64,384]{1,0:T(8,128)(2,1)S(1)} %get-tuple-element.13), channel_id=1, source_target_pairs={{0,1},{1,2},{2,3},{3,4},{4,5},{5,6},{6,7},{7,8},{8,9},{9,10},{10,1... | collective-permute-start | bytes 147464 | tf_op jit(solution)/shard_map/ppermute | solution.py:23
  7.0 4.3 %compare_select_fusion.1 = s32[256,1]{0,1:T(1,128)S(1)} fusion(s32[]{:T(128)} %bitcast.21, s32[]{:T(128)} %bitcast.22, s32[]{:T(128)} %bitcast.23, s32[]{:T(128)} %bitcast.24, s32[]{:T(128)} %bitcast.25, s32[]{:T(128)} %bitcast.27, s32[]{:T(128)} %bitcast.26), kind=kLoop, calls=%fused_computation.122 | loop fusion | flops 5888 | bytes 1052 | tf_op jit(solution)/shard_map/gather | solution.py:73
  18.9 2.6 %copy.126 = f32[512,1,512]{2,0,1:T(8,128)} copy(f32[512,1,512]{0,2,1:T(8,128)} %get-tuple-element.10) | data formatting | bytes 2097152
  21.5 2.6 %copy.125 = f32[512,1,512]{2,0,1:T(8,128)} copy(f32[512,1,512]{0,2,1:T(8,128)} %get-tuple-element.9) | data formatting | bytes 2097152
  24.0 2.6 %copy.124 = f32[512,1,512]{2,0,1:T(8,128)} copy(f32[512,1,512]{0,2,1:T(8,128)} %get-tuple-element.8) | data formatting | bytes 2097152
  33.4 5.1 %collective-permute-start.6 = (s32[32]{0:T(128)S(1)}, s32[32]{0:T(128)S(1)}, u32[]{:S(2)}, u32[]{:S(2)}) collective-permute-start(s32[32]{0:T(128)S(1)} %get-tuple-element.61), channel_id=1, source_target_pairs={{0,1},{1,2},{2,3},{3,4},{4,5},{5,6},{6,7},{7,8},{8,9},{9,10},{10,1... | collective-permute-start | bytes 392 | tf_op jit(solution)/shard_map/ppermute | solution.py:12
  38.5 5.5 %collective-permute-start.7 = (s32[32]{0:T(128)S(1)}, s32[32]{0:T(128)S(1)}, u32[]{:S(2)}, u32[]{:S(2)}) collective-permute-start(s32[32]{0:T(128)S(1)} %get-tuple-element.60), channel_id=1, source_target_pairs={{0,2},{1,3},{2,4},{3,5},{4,6},{5,7},{6,8},{7,9},{8,10},{9,11},{10,... | collective-permute-start | bytes 392 | tf_op jit(solution)/shard_map/ppermute | solution.py:12
  44.1 5.6 %collective-permute-start.8 = (s32[32]{0:T(128)S(1)}, s32[32]{0:T(128)S(1)}, u32[]{:S(2)}, u32[]{:S(2)}) collective-permute-start(s32[32]{0:T(128)S(1)} %get-tuple-element.59), channel_id=1, source_target_pairs={{0,3},{1,4},{2,5},{3,6},{4,7},{5,8},{6,9},{7,10},{8,11},{9,12},{10... | collective-permute-start | bytes 392 | tf_op jit(solution)/shard_map/ppermute | solution.py:12
  49.7 4.3 %collective-permute-start.9 = (s32[32]{0:T(128)S(1)}, s32[32]{0:T(128)S(1)}, u32[]{:S(2)}, u32[]{:S(2)}) collective-permute-start(s32[32]{0:T(128)S(1)} %get-tuple-element.58), channel_id=1, source_target_pairs={{0,4},{1,5},{2,6},{3,7},{4,8},{5,9},{6,10},{7,11},{8,12},{9,13},{1... | collective-permute-start | bytes 392 | tf_op jit(solution)/shard_map/ppermute | solution.py:12
  62.2 3.0 %collective-permute-start.14 = (bf16[32,64]{0,1:T(8,128)(2,1)S(1)}, bf16[32,64]{0,1:T(8,128)(2,1)S(1)}, u32[]{:S(2)}, u32[]{:S(2)}) collective-permute-start(bf16[32,64]{0,1:T(8,128)(2,1)S(1)} %get-tuple-element.26), channel_id=1, source_target_pairs={{0,1},{1,2},{2,3},{3,4},{4,5},{5,6},{6,7},{7,8},{8,9},{9,10},{10,1... | collective-permute-start | bytes 12296 | tf_op jit(solution)/shard_map/ppermute | solution.py:12
  66.0 3.6 %collective-permute-start.15 = (bf16[32,64]{0,1:T(8,128)(2,1)S(1)}, bf16[32,64]{0,1:T(8,128)(2,1)S(1)}, u32[]{:S(2)}, u32[]{:S(2)}) collective-permute-start(bf16[32,64]{0,1:T(8,128)(2,1)S(1)} %get-tuple-element.25), channel_id=1, source_target_pairs={{0,2},{1,3},{2,4},{3,5},{4,6},{5,7},{6,8},{7,9},{8,10},{9,11},{10,... | collective-permute-start | bytes 12296 | tf_op jit(solution)/shard_map/ppermute | solution.py:12
  70.4 5.5 %collective-permute-start.16 = (bf16[32,64]{0,1:T(8,128)(2,1)S(1)}, bf16[32,64]{0,1:T(8,128)(2,1)S(1)}, u32[]{:S(2)}, u32[]{:S(2)}) collective-permute-start(bf16[32,64]{0,1:T(8,128)(2,1)S(1)} %get-tuple-element.24), channel_id=1, source_target_pairs={{0,3},{1,4},{2,5},{3,6},{4,7},{5,8},{6,9},{7,10},{8,11},{9,12},{10... | collective-permute-start | bytes 12296 | tf_op jit(solution)/shard_map/ppermute | solution.py:12
  75.9 4.6 %collective-permute-start.17 = (bf16[32,64]{0,1:T(8,128)(2,1)S(1)}, bf16[32,64]{0,1:T(8,128)(2,1)S(1)}, u32[]{:S(2)}, u32[]{:S(2)}) collective-permute-start(bf16[32,64]{0,1:T(8,128)(2,1)S(1)} %get-tuple-element.23), channel_id=1, source_target_pairs={{0,4},{1,5},{2,6},{3,7},{4,8},{5,9},{6,10},{7,11},{8,12},{9,13},{1... | collective-permute-start | bytes 12296 | tf_op jit(solution)/shard_map/ppermute | solution.py:12
  91.0 2.4 %concatenate.13 = f32[512,384]{1,0:T(8,128)} concatenate(f32[512,64]{1,0:T(8,128)} %fusion.19, f32[512,64]{1,0:T(8,128)} %fusion.17, f32[512,64]{1,0:T(8,128)} %fusion.15, f32[512,64]{1,0:T(8,128)} %fusion.13, f32[512,64]{1,0:T(8,128)} %fusion.11, f32[512,64]{1,0:T(8,128)} %fusion.9), dimensions={1} | concatenate | bytes 1572864 | tf_op jit(solution)/shard_map/concatenate | solution.py:104
  93.4 4.1 %fusion.7 = f32[512,512]{1,0:T(8,128)} fusion(f32[512,512]{1,0:T(8,128)S(1)} %copy-done.1, bf16[384,512]{1,0:T(8,128)(2,1)S(1)} %copy-done.4, f32[512,1,512]{2,0,1:T(8,128)} %copy.126, f32[512,1,512]{2,0,1:T(8,128)} %copy.125, f32[512,1,512]{2,0,1:T(8,128)} %copy.124, f32[512]{0:T(512)S(1)} %bitcast.144, f32[512]{0:T(512)S(1)} %bitcast.146, ...), kind=kOutput, calls=%fused_computation.9 | convolution fusion | flops 305463296 | bytes 7808000 | tf_op jit(solution)/shard_map/dot_general | solution.py:108
  105.4 2.6 %copy.129 = f32[512,1,512]{2,0,1:T(8,128)} copy(f32[512,1,512]{0,2,1:T(8,128)} %get-tuple-element.7) | data formatting | bytes 2097152
  108.0 2.6 %copy.128 = f32[512,1,512]{2,0,1:T(8,128)} copy(f32[512,1,512]{0,2,1:T(8,128)} %get-tuple-element.6) | data formatting | bytes 2097152
  110.6 2.5 %copy.127 = f32[512,1,512]{2,0,1:T(8,128)} copy(f32[512,1,512]{0,2,1:T(8,128)} %get-tuple-element.5) | data formatting | bytes 2097152
  114.4 3.7 %collective-permute-start.18 = (bf16[64,384]{1,0:T(8,128)(2,1)S(1)}, bf16[64,384]{1,0:T(8,128)(2,1)}, u32[]{:S(2)}, u32[]{:S(2)}) collective-permute-start(bf16[64,384]{1,0:T(8,128)(2,1)S(1)} %get-tuple-element.11), channel_id=1, source_target_pairs={{0,1},{1,2},{2,3},{3,4},{4,5},{5,6},{6,7},{7,8},{8,9},{9,10},{10,1... | collective-permute-start | bytes 147464 | tf_op jit(solution)/shard_map/ppermute | solution.py:23
  124.6 3.0 %collective-permute-start.24 = (bf16[32,64]{0,1:T(8,128)(2,1)S(1)}, bf16[32,64]{0,1:T(8,128)(2,1)S(1)}, u32[]{:S(2)}, u32[]{:S(2)}) collective-permute-start(bf16[32,64]{0,1:T(8,128)(2,1)S(1)} %get-tuple-element.18), channel_id=1, source_target_pairs={{0,1},{1,2},{2,3},{3,4},{4,5},{5,6},{6,7},{7,8},{8,9},{9,10},{10,1... | collective-permute-start | bytes 12296 | tf_op jit(solution)/shard_map/ppermute | solution.py:12
  128.2 4.9 %collective-permute-start.25 = (bf16[32,64]{0,1:T(8,128)(2,1)S(1)}, bf16[32,64]{0,1:T(8,128)(2,1)S(1)}, u32[]{:S(2)}, u32[]{:S(2)}) collective-permute-start(bf16[32,64]{0,1:T(8,128)(2,1)S(1)} %get-tuple-element.17), channel_id=1, source_target_pairs={{0,2},{1,3},{2,4},{3,5},{4,6},{5,7},{6,8},{7,9},{8,10},{9,11},{10,... | collective-permute-start | bytes 12296 | tf_op jit(solution)/shard_map/ppermute | solution.py:12
  133.7 5.6 %collective-permute-start.26 = (bf16[32,64]{0,1:T(8,128)(2,1)S(1)}, bf16[32,64]{0,1:T(8,128)(2,1)S(1)}, u32[]{:S(2)}, u32[]{:S(2)}) collective-permute-start(bf16[32,64]{0,1:T(8,128)(2,1)S(1)} %get-tuple-element.16), channel_id=1, source_target_pairs={{0,3},{1,4},{2,5},{3,6},{4,7},{5,8},{6,9},{7,10},{8,11},{9,12},{10... | collective-permute-start | bytes 12296 | tf_op jit(solution)/shard_map/ppermute | solution.py:12
  139.9 3.9 %collective-permute-start.27 = (bf16[32,64]{0,1:T(8,128)(2,1)S(1)}, bf16[32,64]{0,1:T(8,128)(2,1)S(1)}, u32[]{:S(2)}, u32[]{:S(2)}) collective-permute-start(bf16[32,64]{0,1:T(8,128)(2,1)S(1)} %get-tuple-element.15), channel_id=1, source_target_pairs={{0,4},{1,5},{2,6},{3,7},{4,8},{5,9},{6,10},{7,11},{8,12},{9,13},{1... | collective-permute-start | bytes 12296 | tf_op jit(solution)/shard_map/ppermute | solution.py:12
  159.6 4.5 %fusion.4 = f32[512,512]{1,0:T(8,128)} fusion(f32[512,512]{1,0:T(8,128)S(1)} %copy-done.1, f32[512,512]{1,0:T(8,128)} %fusion.7, bf16[384,512]{1,0:T(8,128)(2,1)S(1)} %copy-done.4, f32[512,1,512]{2,0,1:T(8,128)} %copy.129, f32[512,1,512]{2,0,1:T(8,128)} %copy.128, f32[512,1,512]{2,0,1:T(8,128)} %copy.127, f32[512]{0:T(512)S(1)} %bitcast.145, ...), kind=kOutput, calls=%fused_computation.5 | convolution fusion | flops 305987584 | bytes 8856576 | tf_op jit(solution)/shard_map/dot_general | solution.py:108
  (186 shorter events, 71.3 us)
Async XLA Ops:
  1.9 80.8 %collective-permute-start.1 = (bf16[64,384]{1,0:T(8,128)(2,1)S(1)}, bf16[64,384]{1,0:T(8,128)(2,1)S(1)}, u32[]{:S(2)}, u32[]{:S(2)}) collective-permute-start(bf16[64,384]{1,0:T(8,128)(2,1)S(1)} %get-tuple-element.14), channel_id=1, source_target_pairs={{1,0},{2,1},{3,2},{4,3},{5,4},{6,5},{7,6},{8,7},{9,8},{10,9},{11,1... | collective-permute-start | bytes 147464 | tf_op jit(solution)/shard_map/ppermute | solution.py:25
  3.2 79.5 %collective-permute-start = (bf16[64,384]{1,0:T(8,128)(2,1)S(1)}, bf16[64,384]{1,0:T(8,128)(2,1)S(1)}, u32[]{:S(2)}, u32[]{:S(2)}) collective-permute-start(bf16[64,384]{1,0:T(8,128)(2,1)S(1)} %get-tuple-element.13), channel_id=1, source_target_pairs={{0,1},{1,2},{2,3},{3,4},{4,5},{5,6},{6,7},{7,8},{8,9},{9,10},{10,1... | collective-permute-start | bytes 147464 | tf_op jit(solution)/shard_map/ppermute | solution.py:23
  12.1 20.0 %collective-permute-start.2 = (s32[32]{0:T(128)S(1)}, s32[32]{0:T(128)S(1)}, u32[]{:S(2)}, u32[]{:S(2)}) collective-permute-start(s32[32]{0:T(128)S(1)} %get-tuple-element.65), channel_id=1, source_target_pairs={{4,0},{5,1},{6,2},{7,3},{8,4},{9,5},{10,6},{11,7},{12,8},{13,9},{1... | collective-permute-start | bytes 392 | tf_op jit(solution)/shard_map/ppermute | solution.py:12
  13.4 20.0 %collective-permute-start.3 = (s32[32]{0:T(128)S(1)}, s32[32]{0:T(128)S(1)}, u32[]{:S(2)}, u32[]{:S(2)}) collective-permute-start(s32[32]{0:T(128)S(1)} %get-tuple-element.64), channel_id=1, source_target_pairs={{3,0},{4,1},{5,2},{6,3},{7,4},{8,5},{9,6},{10,7},{11,8},{12,9},{13... | collective-permute-start | bytes 392 | tf_op jit(solution)/shard_map/ppermute | solution.py:12
  14.7 23.8 %collective-permute-start.4 = (s32[32]{0:T(128)S(1)}, s32[32]{0:T(128)S(1)}, u32[]{:S(2)}, u32[]{:S(2)}) collective-permute-start(s32[32]{0:T(128)S(1)} %get-tuple-element.63), channel_id=1, source_target_pairs={{2,0},{3,1},{4,2},{5,3},{6,4},{7,5},{8,6},{9,7},{10,8},{11,9},{12,... | collective-permute-start | bytes 392 | tf_op jit(solution)/shard_map/ppermute | solution.py:12
  32.1 11.9 %collective-permute-start.5 = (s32[32]{0:T(128)S(1)}, s32[32]{0:T(128)S(1)}, u32[]{:S(2)}, u32[]{:S(2)}) collective-permute-start(s32[32]{0:T(128)S(1)} %get-tuple-element.62), channel_id=1, source_target_pairs={{1,0},{2,1},{3,2},{4,3},{5,4},{6,5},{7,6},{8,7},{9,8},{10,9},{11,1... | collective-permute-start | bytes 392 | tf_op jit(solution)/shard_map/ppermute | solution.py:12
  33.4 16.3 %collective-permute-start.6 = (s32[32]{0:T(128)S(1)}, s32[32]{0:T(128)S(1)}, u32[]{:S(2)}, u32[]{:S(2)}) collective-permute-start(s32[32]{0:T(128)S(1)} %get-tuple-element.61), channel_id=1, source_target_pairs={{0,1},{1,2},{2,3},{3,4},{4,5},{5,6},{6,7},{7,8},{8,9},{9,10},{10,1... | collective-permute-start | bytes 392 | tf_op jit(solution)/shard_map/ppermute | solution.py:12
  38.5 15.4 %collective-permute-start.7 = (s32[32]{0:T(128)S(1)}, s32[32]{0:T(128)S(1)}, u32[]{:S(2)}, u32[]{:S(2)}) collective-permute-start(s32[32]{0:T(128)S(1)} %get-tuple-element.60), channel_id=1, source_target_pairs={{0,2},{1,3},{2,4},{3,5},{4,6},{5,7},{6,8},{7,9},{8,10},{9,11},{10,... | collective-permute-start | bytes 392 | tf_op jit(solution)/shard_map/ppermute | solution.py:12
  44.1 11.2 %collective-permute-start.8 = (s32[32]{0:T(128)S(1)}, s32[32]{0:T(128)S(1)}, u32[]{:S(2)}, u32[]{:S(2)}) collective-permute-start(s32[32]{0:T(128)S(1)} %get-tuple-element.59), channel_id=1, source_target_pairs={{0,3},{1,4},{2,5},{3,6},{4,7},{5,8},{6,9},{7,10},{8,11},{9,12},{10... | collective-permute-start | bytes 392 | tf_op jit(solution)/shard_map/ppermute | solution.py:12
  49.7 6.9 %collective-permute-start.9 = (s32[32]{0:T(128)S(1)}, s32[32]{0:T(128)S(1)}, u32[]{:S(2)}, u32[]{:S(2)}) collective-permute-start(s32[32]{0:T(128)S(1)} %get-tuple-element.58), channel_id=1, source_target_pairs={{0,4},{1,5},{2,6},{3,7},{4,8},{5,9},{6,10},{7,11},{8,12},{9,13},{1... | collective-permute-start | bytes 392 | tf_op jit(solution)/shard_map/ppermute | solution.py:12
  55.3 6.9 %collective-permute-start.11 = (bf16[32,64]{0,1:T(8,128)(2,1)}, bf16[32,64]{0,1:T(8,128)(2,1)}, u32[]{:S(2)}, u32[]{:S(2)}) collective-permute-start(bf16[32,64]{0,1:T(8,128)(2,1)} %get-tuple-element.29), channel_id=1, source_target_pairs={{3,0},{4,1},{5,2},{6,3},{7,4},{8,5},{9,6},{10,7},{11,8},{12,9},{13... | collective-permute-start | bytes 12296 | tf_op jit(solution)/shard_map/ppermute | solution.py:12
  56.6 9.4 %collective-permute-start.12 = (bf16[32,64]{0,1:T(8,128)(2,1)}, bf16[32,64]{0,1:T(8,128)(2,1)}, u32[]{:S(2)}, u32[]{:S(2)}) collective-permute-start(bf16[32,64]{0,1:T(8,128)(2,1)} %get-tuple-element.28), channel_id=1, source_target_pairs={{2,0},{3,1},{4,2},{5,3},{6,4},{7,5},{8,6},{9,7},{10,8},{11,9},{12,... | collective-permute-start | bytes 12296 | tf_op jit(solution)/shard_map/ppermute | solution.py:12
  60.2 10.2 %collective-permute-start.13 = (bf16[32,64]{0,1:T(8,128)(2,1)S(1)}, bf16[32,64]{0,1:T(8,128)(2,1)S(1)}, u32[]{:S(2)}, u32[]{:S(2)}) collective-permute-start(bf16[32,64]{0,1:T(8,128)(2,1)S(1)} %get-tuple-element.27), channel_id=1, source_target_pairs={{1,0},{2,1},{3,2},{4,3},{5,4},{6,5},{7,6},{8,7},{9,8},{10,9},{11,1... | collective-permute-start | bytes 12296 | tf_op jit(solution)/shard_map/ppermute | solution.py:12
  62.2 13.6 %collective-permute-start.14 = (bf16[32,64]{0,1:T(8,128)(2,1)S(1)}, bf16[32,64]{0,1:T(8,128)(2,1)S(1)}, u32[]{:S(2)}, u32[]{:S(2)}) collective-permute-start(bf16[32,64]{0,1:T(8,128)(2,1)S(1)} %get-tuple-element.26), channel_id=1, source_target_pairs={{0,1},{1,2},{2,3},{3,4},{4,5},{5,6},{6,7},{7,8},{8,9},{9,10},{10,1... | collective-permute-start | bytes 12296 | tf_op jit(solution)/shard_map/ppermute | solution.py:12
  66.0 14.5 %collective-permute-start.15 = (bf16[32,64]{0,1:T(8,128)(2,1)S(1)}, bf16[32,64]{0,1:T(8,128)(2,1)S(1)}, u32[]{:S(2)}, u32[]{:S(2)}) collective-permute-start(bf16[32,64]{0,1:T(8,128)(2,1)S(1)} %get-tuple-element.25), channel_id=1, source_target_pairs={{0,2},{1,3},{2,4},{3,5},{4,6},{5,7},{6,8},{7,9},{8,10},{9,11},{10,... | collective-permute-start | bytes 12296 | tf_op jit(solution)/shard_map/ppermute | solution.py:12
  70.4 10.1 %collective-permute-start.16 = (bf16[32,64]{0,1:T(8,128)(2,1)S(1)}, bf16[32,64]{0,1:T(8,128)(2,1)S(1)}, u32[]{:S(2)}, u32[]{:S(2)}) collective-permute-start(bf16[32,64]{0,1:T(8,128)(2,1)S(1)} %get-tuple-element.24), channel_id=1, source_target_pairs={{0,3},{1,4},{2,5},{3,6},{4,7},{5,8},{6,9},{7,10},{8,11},{9,12},{10... | collective-permute-start | bytes 12296 | tf_op jit(solution)/shard_map/ppermute | solution.py:12
  103.5 17.1 %collective-permute-start.20 = (bf16[32,64]{0,1:T(8,128)(2,1)}, bf16[32,64]{0,1:T(8,128)(2,1)}, u32[]{:S(2)}, u32[]{:S(2)}) collective-permute-start(bf16[32,64]{0,1:T(8,128)(2,1)} %get-tuple-element.22), channel_id=1, source_target_pairs={{4,0},{5,1},{6,2},{7,3},{8,4},{9,5},{10,6},{11,7},{12,8},{13,9},{1... | collective-permute-start | bytes 12296 | tf_op jit(solution)/shard_map/ppermute | solution.py:12
  113.1 35.7 %collective-permute-start.19 = (bf16[64,384]{1,0:T(8,128)(2,1)}, bf16[64,384]{1,0:T(8,128)(2,1)}, u32[]{:S(2)}, u32[]{:S(2)}) collective-permute-start(bf16[64,384]{1,0:T(8,128)(2,1)} %get-tuple-element.12), channel_id=1, source_target_pairs={{1,0},{2,1},{3,2},{4,3},{5,4},{6,5},{7,6},{8,7},{9,8},{10,9},{11,1... | collective-permute-start | bytes 147464 | tf_op jit(solution)/shard_map/ppermute | solution.py:25
  114.4 34.5 %collective-permute-start.18 = (bf16[64,384]{1,0:T(8,128)(2,1)S(1)}, bf16[64,384]{1,0:T(8,128)(2,1)}, u32[]{:S(2)}, u32[]{:S(2)}) collective-permute-start(bf16[64,384]{1,0:T(8,128)(2,1)S(1)} %get-tuple-element.11), channel_id=1, source_target_pairs={{0,1},{1,2},{2,3},{3,4},{4,5},{5,6},{6,7},{7,8},{8,9},{9,10},{10,1... | collective-permute-start | bytes 147464 | tf_op jit(solution)/shard_map/ppermute | solution.py:23
  119.3 8.9 %collective-permute-start.22 = (bf16[32,64]{0,1:T(8,128)(2,1)S(1)}, bf16[32,64]{0,1:T(8,128)(2,1)S(1)}, u32[]{:S(2)}, u32[]{:S(2)}) collective-permute-start(bf16[32,64]{0,1:T(8,128)(2,1)S(1)} %get-tuple-element.20), channel_id=1, source_target_pairs={{2,0},{3,1},{4,2},{5,3},{6,4},{7,5},{8,6},{9,7},{10,8},{11,9},{12,... | collective-permute-start | bytes 12296 | tf_op jit(solution)/shard_map/ppermute | solution.py:12
  120.6 13.1 %collective-permute-start.23 = (bf16[32,64]{0,1:T(8,128)(2,1)S(1)}, bf16[32,64]{0,1:T(8,128)(2,1)S(1)}, u32[]{:S(2)}, u32[]{:S(2)}) collective-permute-start(bf16[32,64]{0,1:T(8,128)(2,1)S(1)} %get-tuple-element.19), channel_id=1, source_target_pairs={{1,0},{2,1},{3,2},{4,3},{5,4},{6,5},{7,6},{8,7},{9,8},{10,9},{11,1... | collective-permute-start | bytes 12296 | tf_op jit(solution)/shard_map/ppermute | solution.py:12
  124.6 15.4 %collective-permute-start.24 = (bf16[32,64]{0,1:T(8,128)(2,1)S(1)}, bf16[32,64]{0,1:T(8,128)(2,1)S(1)}, u32[]{:S(2)}, u32[]{:S(2)}) collective-permute-start(bf16[32,64]{0,1:T(8,128)(2,1)S(1)} %get-tuple-element.18), channel_id=1, source_target_pairs={{0,1},{1,2},{2,3},{3,4},{4,5},{5,6},{6,7},{7,8},{8,9},{9,10},{10,1... | collective-permute-start | bytes 12296 | tf_op jit(solution)/shard_map/ppermute | solution.py:12
  128.2 16.3 %collective-permute-start.25 = (bf16[32,64]{0,1:T(8,128)(2,1)S(1)}, bf16[32,64]{0,1:T(8,128)(2,1)S(1)}, u32[]{:S(2)}, u32[]{:S(2)}) collective-permute-start(bf16[32,64]{0,1:T(8,128)(2,1)S(1)} %get-tuple-element.17), channel_id=1, source_target_pairs={{0,2},{1,3},{2,4},{3,5},{4,6},{5,7},{6,8},{7,9},{8,10},{9,11},{10,... | collective-permute-start | bytes 12296 | tf_op jit(solution)/shard_map/ppermute | solution.py:12
  133.7 11.4 %collective-permute-start.26 = (bf16[32,64]{0,1:T(8,128)(2,1)S(1)}, bf16[32,64]{0,1:T(8,128)(2,1)S(1)}, u32[]{:S(2)}, u32[]{:S(2)}) collective-permute-start(bf16[32,64]{0,1:T(8,128)(2,1)S(1)} %get-tuple-element.16), channel_id=1, source_target_pairs={{0,3},{1,4},{2,5},{3,6},{4,7},{5,8},{6,9},{7,10},{8,11},{9,12},{10... | collective-permute-start | bytes 12296 | tf_op jit(solution)/shard_map/ppermute | solution.py:12
  (36 other events, 576.9 us)
where the time goes:
time: 166 us; the launch traced here: 164 us
  starting transfers between devices  79.5 us (48%)
  local copies, waits for them, and re-layouts  40.5 us (24%)
  matrix products  31.1 us (19%)
  other arithmetic  8.26 us (5%)
  waiting for transfers between devices  3.85 us (2%)
    ppermute x24, starting transfers between devices, passed_along(): return lax.ppermute(x, axis, pairs)  70.3 us
    unnamed x84, local copies, waits for them, and re-layouts  23.3 us
    dot_general x12, matrix products, tendency(): pieces.append(jnp.dot(picker, column, preferred_element_type=jnp.float32))  15.5 us
    dot_general x2, matrix products, tendency(): lifted = jnp.dot(flux, lift, preferred_element_type=jnp.float32)  8.53 us
    ppermute x2, starting transfers between devices, padded_2(): lax.ppermute(tail, axis, [(i, (i + 1) % count) for i in range(ends)])  6.68 us
    concatenate x2, local copies, waits for them, and re-layouts, tendency(): conforming = jnp.concatenate(pieces, axis=1)  4.76 us
    gather x2, other arithmetic, tendency(): live = slot_ids % capacity < counts[0][slot_ids // capacity]  4.37 us
    ppermute x24, waiting for transfers between devices, passed_along(): return lax.ppermute(x, axis, pairs)  3.84 us
  transfers between devices with their start and end apart: 28, of which 3 were waited for; matrix products, arithmetic and copies ran while one was open for 25% of the time, Pallas kernels for 0%

commit v1 on v0

v1 whole, which is shorter than its diff:
```python
import functools

import jax
import jax.numpy as jnp
from jax import lax
from jax.experimental import pallas as pl
from jax.experimental.pallas import tpu as pltpu
from jax.sharding import PartitionSpec as P

time_step = 0.3
bf16 = jnp.bfloat16
f32 = jnp.float32
CURVE = ("curve", "sub", "pair")


def dot(a, b):
    return jnp.dot(a, b, preferred_element_type=f32)


def columns_of(*rows):
    stacked = jnp.concatenate([row.astype(f32) for row in rows], axis=0)
    pad = jnp.zeros((128 - stacked.shape[0], stacked.shape[1]), f32)
    return jnp.concatenate([stacked, pad], axis=0).T


def lanes(shape):
    return lax.broadcasted_iota(jnp.int32, shape, 1)


def rows_of(shape):
    return lax.broadcasted_iota(jnp.int32, shape, 0)


def swapped(tile):
    turned = pltpu.roll(tile.astype(f32), 64, 1)
    low = lanes(turned.shape) < 64
    top = jnp.where(low, turned, 0.0).astype(bf16)
    bottom = jnp.where(low, 0.0, turned).astype(bf16)
    return jnp.concatenate([top, bottom], axis=0)


def hot(column, width):
    rows = column.shape[0]
    picked = column.astype(jnp.int32) == lanes((rows, width))
    return jnp.where(picked, 1.0, 0.0).astype(bf16)


def send(traces, roles, counts, records, projection, traces_out, first_out, own_out, blocks):
    elements, width = traces.shape
    slots = records.shape[1]
    capacity = slots // 8
    rim = elements // 8
    traces_out[...] = traces
    column = columns_of(records[...])
    shape = (slots, 128)
    source = column[:, 0:1]
    face = jnp.broadcast_to(column[:, 1:2], shape).astype(jnp.int32)
    kind = jnp.broadcast_to(column[:, 2:3], shape).astype(jnp.int32)
    target = jnp.broadcast_to(column[:, 3:4], shape).astype(jnp.int32)
    picked = dot(hot(source, elements), traces)
    lane = lanes(shape)
    half = lane // 64
    parts = [
        jnp.where(half + 2 * t == face, picked[:, 128 * t : 128 * t + 128], 0.0).astype(bf16)
        for t in range(width // 128)
    ]
    rows = jnp.concatenate(parts, axis=1)
    every = dot(rows, jnp.concatenate([projection[...]] * (width // 64), axis=0))
    folded = jnp.zeros(shape, f32)
    for t in range(4):
        folded = jnp.where(half + 2 * t == kind, every[:, 128 * t : 128 * t + 128], folded)
    piece = folded + pltpu.roll(folded, 64, 1)
    slot = rows_of(shape)
    allowed = jnp.zeros(shape, jnp.int32)
    for j in range(8):
        allowed = jnp.where(slot // capacity == j, counts[0, j], allowed)
    live = slot % capacity < allowed
    facing = jnp.where(live, jnp.bitwise_xor(face, 1) + 1, 0)
    code = jnp.where(lane == 64, target // 16, jnp.where(lane == 65, target % 16, facing))
    code = jnp.where(lane < 67, code, 0).astype(f32)
    blocks[...] = jnp.where(lane < 64, piece, code).astype(bf16)

    def block(role):
        return blocks[pl.ds(pl.multiple_of(roles[role] * capacity, capacity), capacity), :]

    final_at = pl.multiple_of(roles[8] * rim, rim)
    other_at = pl.multiple_of(roles[9] * rim, rim)
    first_out[0:rim, :] = traces_out[pl.ds(final_at, rim), :]
    first_out[rim : 2 * rim, :] = traces_out[pl.ds(other_at, rim), :]
    at = 2 * rim
    for t in range(3):
        first_out[at : at + capacity, 128 * t : 128 * t + 128] = block(t)
    at += capacity
    first_out[at : at + capacity, 0:128] = block(3)
    first_out[at : at + capacity, 128:] = jnp.zeros((capacity, width - 128), bf16)
    for t in range(4):
        own_out[capacity * t : capacity * t + capacity, :] = block(4 + t)


def start_kernel(roles, counts, state, records, trace_map, projection, traces_out, first_out, own_out, blocks):
    traces = dot(state[...].astype(bf16), trace_map[...]).astype(bf16)
    send(traces, roles, counts, records, projection, traces_out, first_out, own_out, blocks)


def local_kernel(weights, roles, *refs):
    if len(weights) == 3:
        state, field, velocity, levels, neighbours, stiffness, traces, base_out, partial_out = refs
    else:
        field, velocity, levels, neighbours, stiffness, traces, base_out, partial_out = refs
        state = None
    elements, modes = field.shape
    column = columns_of(velocity[...], levels[...], neighbours[...])
    scale = jnp.exp2(column[:, 3:4]) * (0.25 * weights[-1])
    lowered = field[...].astype(bf16)
    step = 256
    for n in range(0, modes, step):
        volume = jnp.zeros((elements, step), f32)
        for d in range(3):
            volume += column[:, d : d + 1] * dot(lowered, stiffness[:, d * modes + n : d * modes + n + step])
        base = weights[-2] * field[:, n : n + step] + scale * volume
        if state is not None:
            base += weights[0] * state[:, n : n + step]
        base_out[:, n : n + step] = base
    start = (roles[10] * elements).astype(f32)
    for t in range(3):
        tile = traces[:, 128 * t : 128 * t + 128]
        picks = [hot(column[:, 4 + 2 * t + i : 5 + 2 * t + i] - start, elements) for i in range(2)]
        near = dot(jnp.concatenate(picks, axis=1), swapped(tile))
        partial_out[:, 128 * t : 128 * t + 128] = near - tile.astype(f32)


def finished(weight, roles, velocity, levels, neighbours, lift, base, partial, got, got_even, got_odd, got_a, got_b, arrived):
    elements = base.shape[0]
    rim = elements // 8
    capacity = arrived.shape[0] // 8
    at = 2 * rim
    column = columns_of(velocity[...], levels[...], neighbours[...])
    arrived[0:capacity, :] = got[at : at + capacity, 0:128]
    for i, ref in enumerate((got_even, got_odd)):
        for k in range(2):
            to = capacity * (1 + 2 * i + k)
            arrived[to : to + capacity, :] = ref[rim : rim + capacity, 128 * k : 128 * k + 128]
    arrived[5 * capacity : 6 * capacity, :] = got_a[0:capacity, :]
    arrived[6 * capacity : 7 * capacity, :] = got_b[0:capacity, :]
    far = jnp.where(roles[12] > 0, got_a[capacity : 2 * capacity, :], got_b[capacity : 2 * capacity, :])
    arrived[7 * capacity :, :] = far
    forward = jnp.where(roles[11] > 0, got_even[0:rim, :], got_odd[0:rim, :])
    window = jnp.concatenate([got[0:rim, :], forward], axis=0)
    pieces = arrived[...]
    shape = (128, 128)
    source_lane = rows_of(shape)
    face_of = jnp.where(source_lane == 66, 1.0, 0.0).astype(bf16)
    face = dot(pieces, face_of).astype(jnp.int32) - 1
    small = (8, 128)
    element_of = jnp.where(lanes(small) == 64, 16.0, jnp.where(lanes(small) == 65, 1.0, 0.0)).astype(bf16)
    target = lax.dot_general(element_of, pieces, (((1,), (1,)), ((), ())), preferred_element_type=f32)[0:1, :]
    slots = pieces.shape[0]
    element_hot = jnp.where(rows_of((elements, slots)) == target.astype(jnp.int32), 1.0, 0.0).astype(bf16)
    half = lanes((slots, 128)) // 64
    plain = jnp.where(half == 0, pieces.astype(f32), 0.0)
    both = plain + pltpu.roll(plain, 64, 1)
    placed = jnp.concatenate([jnp.where(half + 2 * t == face, both, 0.0).astype(bf16) for t in range(3)], axis=1)
    mortar = dot(element_hot, placed)
    start = (roles[10] * elements).astype(f32)
    before = roles[13].astype(f32)
    after = roles[14].astype(f32)
    low = lanes((elements, 128)) < 64
    fluxes = []
    for t in range(3):
        picks = []
        for i in range(2):
            raw = column[:, 4 + 2 * t + i : 5 + 2 * t + i]
            local = raw - start
            index = jnp.where(local < 0, local + before, jnp.where(local >= elements, local - after, -1.0))
            picks.append(hot(jnp.where(raw < 0, -1.0, index), 2 * rim))
        near = dot(jnp.concatenate(picks, axis=1), swapped(window[:, 128 * t : 128 * t + 128]))
        speed = column[:, t : t + 1]
        inflow = jnp.maximum(jnp.where(low, speed, -speed), 0.0)
        total = partial[:, 128 * t : 128 * t + 128] + near + mortar[:, 128 * t : 128 * t + 128]
        fluxes.append((inflow * total).astype(bf16))
    lifted = dot(jnp.concatenate(fluxes, axis=1), lift[...])
    scale = jnp.exp2(column[:, 3:4]) * (0.25 * weight)
    return base[...] + scale * lifted


def middle_kernel(
    roles, counts, velocity, levels, neighbours, lift, base, partial, got, got_even, got_odd, got_a, got_b,
    records, trace_map, projection, field_out, traces_out, first_out, own_out, arrived, blocks
):
    field = finished(
        time_step, roles, velocity, levels, neighbours, lift, base, partial, got, got_even, got_odd, got_a, got_b, arrived
    )
    field_out[...] = field
    traces = dot(field.astype(bf16), trace_map[...]).astype(bf16)
    send(traces, roles, counts, records, projection, traces_out, first_out, own_out, blocks)


def end_kernel(
    roles, velocity, levels, neighbours, lift, base, partial, got, got_even, got_odd, got_a, got_b, field_out, arrived
):
    field_out[...] = finished(
        0.5 * time_step, roles, velocity, levels, neighbours, lift, base, partial, got, got_even, got_odd, got_a, got_b, arrived
    )


def paired(count, step, lower):
    partner = {}
    for s in range(count):
        if lower(s) and s + step < count:
            partner[s] = s + step
            partner[s + step] = s
    rest = [s for s in range(count) if s not in partner]
    for a, b in zip(rest[::2], rest[1::2]):
        partner[a] = b
        partner[b] = a
    return sorted(partner.items())


def call(kernel, out_shape, scratch, scalars, flops, *operands):
    specs = [pl.BlockSpec(memory_space=pltpu.SMEM)] * scalars
    specs += [pl.BlockSpec(memory_space=pltpu.VMEM)] * (len(operands) - scalars)
    read = sum(x.size * x.dtype.itemsize for x in operands)
    return pl.pallas_call(
        kernel,
        out_shape=out_shape,
        in_specs=specs,
        out_specs=[pl.BlockSpec(memory_space=pltpu.VMEM)] * len(out_shape),
        scratch_shapes=scratch,
        compiler_params=pltpu.CompilerParams(vmem_limit_bytes=40 * 1024 * 1024),
        cost_estimate=pl.CostEstimate(flops=flops, bytes_accessed=read, transcendentals=0),
    )(*operands)


def exchange(first, own, chip, core, rim, capacity):
    count = lax.axis_size(CURVE)
    got = lax.ppermute(first, CURVE, paired(count, 1, lambda s: s % 2 == 0))
    forward = got[rim : 2 * rim]
    at = 2 * rim
    up = got[at : at + capacity, 128:256]
    down = got[at : at + capacity, 256:384]
    far = got[at + capacity : at + 2 * capacity, 0:128]
    blank = jnp.zeros_like(up)
    even = chip % 2 == 0
    upper = ((chip // 2) % 2 == 0) == (core == 0)
    mine = [own[capacity * t : capacity * t + capacity] for t in range(4)]

    def near(block, other):
        return jnp.concatenate([forward, jnp.concatenate([block, other, blank], axis=1)], axis=0)

    to_even = near(mine[0], jnp.where(even, up, down))
    to_odd = near(mine[1], jnp.where(even, down, up))
    to_a = jnp.concatenate([mine[2], jnp.where(upper, far, 0)], axis=0)
    to_b = jnp.concatenate([mine[3], jnp.where(upper, 0, far)], axis=0)
    return (
        got,
        lax.ppermute(to_even, CURVE, paired(count, 2, lambda s: (s // 2) % 2 == 0)),
        lax.ppermute(to_odd, CURVE, paired(count, 2, lambda s: (s // 2) % 2 == 1)),
        lax.ppermute(to_a, CURVE, paired(count, 4, lambda s: (s // 4) % 2 == 0)),
        lax.ppermute(to_b, CURVE, paired(count, 4, lambda s: (s // 4) % 2 == 1)),
    )


def body(
    state, velocity, levels, neighbours, records, counts, stiffness, trace_map, lift, projection
):
    elements, modes = state.shape
    width = trace_map.shape[1]
    slots = records.shape[1]
    capacity = slots // counts.shape[1]
    rim = elements // 8
    chip = lax.axis_index(("curve", "sub"))
    core = lax.axis_index("pair")
    position = 2 * chip + core
    even = chip % 2 == 0
    second = (chip // 2) % 2 == 0
    first_core = core == 0

    def pick(which, a, b):
        return jnp.where(which, a, b)

    roles = jnp.stack(
        [
            pick(first_core, 4, 3),
            pick(first_core, 6, 4),
            pick(first_core, 3, 1),
            pick(first_core, 1, 6),
            pick(even, 5, 2),
            pick(even, 2, 5),
            pick(second, 7, 0),
            pick(second, 0, 7),
            pick(first_core, 7, 0),
            pick(first_core, 0, 7),
            position,
            pick(even == first_core, 0, 1),
            pick(second == first_core, 0, 1),
            pick(first_core, 2 * rim, rim),
            pick(first_core, elements, elements - rim),
            0,
        ]
    ).astype(jnp.int32)
    levels = levels.reshape(1, elements)

    def array(shape, dtype):
        return jax.ShapeDtypeStruct(shape, dtype)

    sent = [
        array((elements, width), bf16),
        array((2 * rim + 2 * capacity, width), bf16),
        array((4 * capacity, 128), bf16),
    ]
    whole = array((elements, modes), f32)
    partial_shape = array((elements, width), f32)
    blocks = pltpu.VMEM((slots, 128), bf16)
    arrived = pltpu.VMEM((slots, 128), bf16)

    traces, first, own = call(
        start_kernel, sent, [blocks], 2, 2 * 10**8, roles, counts, state, records, trace_map, projection
    )
    got = exchange(first, own, chip, core, rim, capacity)
    base, partial = call(
        functools.partial(local_kernel, (1.0, time_step)), [whole, partial_shape], [], 1, 3 * 10**9,
        roles, state, velocity, levels, neighbours, stiffness, traces,
    )
    field, traces, first, own = call(
        middle_kernel, [whole] + sent, [arrived, blocks], 2, 10**9,
        roles, counts, velocity, levels, neighbours, lift, base, partial, *got, records, trace_map, projection,
    )
    got = exchange(first, own, chip, core, rim, capacity)
    base, partial = call(
        functools.partial(local_kernel, (0.5, 0.5, 0.5 * time_step)), [whole, partial_shape], [], 1, 3 * 10**9,
        roles, state, field, velocity, levels, neighbours, stiffness, traces,
    )
    return call(
        end_kernel, [whole], [arrived], 1, 10**9,
        roles, velocity, levels, neighbours, lift, base, partial, *got,
    )[0]


def solution(mesh):
    placed = (
        P(("groups", "curve", "sub", "pair"), None),
        P(None, ("groups", "curve", "sub", "pair")),
        P(("groups", "curve", "sub", "pair")),
        P(None, ("groups", "curve", "sub", "pair")),
        P(None, ("groups", "curve", "sub", "pair")),
        P(("groups", "curve", "sub", "pair"), None),
        P(),
        P(),
        P(),
        P(),
    )
    return jax.shard_map(
        body,
        mesh=mesh,
        in_specs=placed,
        out_specs=P(("groups", "curve", "sub", "pair"), None),
        check_vma=False,
    )
```

time: 166 us -> 33.4 us (0.20)
  starting transfers between devices: 79.5 us -> 12.2 us
  local copies, waits for them, and re-layouts: 40.5 us -> 5.95 us
  matrix products: 31.1 us -> 0 us
  Pallas kernels: 0 us -> 12.2 us
  other arithmetic: 8.26 us -> 0.07 us
    ppermute x28 -> x10, starting transfers between devices: 79.5 us -> 12.2 us  [the longest x2 6.98 us: exchange(): lax.ppermute(to_even, CURVE, paired(count, 2, lambda s: s // 2 % 2 == 0))]
    dot_general x22 -> x0, matrix products: 31.1 us -> none  [the longest x12 15.5 us: tendency(): pieces.append(jnp.dot(picker, column, preferred_element_type=jnp.float32))]
    unnamed x84 -> x30, local copies, waits for them, and re-layouts: 23.3 us -> 5.84 us
    pallas_call x0 -> x5, Pallas kernels: none -> 12.2 us  [call(): pl.pallas_call(kernel, out_shape=out_shape, in_specs=specs, out_specs=[pl...]
    slice x9 -> x4, local copies, waits for them, and re-layouts: 6.22 us -> 0.02 us  [the longest x2 0.01 us: exchange(): forward = got[rim:2 * rim]]
    concatenate x2 -> x0, local copies, waits for them, and re-layouts: 4.76 us -> none  [tendency(): conforming = jnp.concatenate(pieces, axis=1)]
    gather x2 -> x0, other arithmetic: 4.37 us -> none  [tendency(): live = slot_ids % capacity < counts[0][slot_ids // capacity]]
    reshape x1 -> x0, local copies, waits for them, and re-layouts: 2.32 us -> none  [tendency(): speeds = jnp.repeat(inflow_speeds(velocity), face_modes, axis=1)]
  transfers between devices with their start and end apart: 28 -> 10, of which waited for: 3 -> 2; matrix products, arithmetic and copies ran while one was open for 25% -> 0% of each run, Pallas kernels for 0% -> 15%
where the time goes in v1:
time: 33.4 us; the launch traced here: 33.1 us
  Pallas kernels  12.2 us (37%)
  starting transfers between devices  12.2 us (37%)
  local copies, waits for them, and re-layouts  5.95 us (18%)
  waiting for transfers between devices  2.37 us (7%)
    pallas_call x5, Pallas kernels, call(): pl.pallas_call(kernel, out_shape=out_shape, in_specs=specs, out_specs=[pl...  12.2 us
    ppermute x2, starting transfers between devices, exchange(): lax.ppermute(to_even, CURVE, paired(count, 2, lambda s: s // 2 % 2 == 0))  6.98 us
    unnamed x30, local copies, waits for them, and re-layouts  5.84 us
    ppermute x2, starting transfers between devices, exchange(): lax.ppermute(to_a, CURVE, paired(count, 4, lambda s: s // 4 % 2 == 0))  3.45 us
    ppermute x2, waiting for transfers between devices, exchange(): got = lax.ppermute(first, CURVE, paired(count, 1, lambda s: s % 2 == 0))  2.35 us
    ppermute x2, starting transfers between devices, exchange(): lax.ppermute(to_odd, CURVE, paired(count, 2, lambda s: s // 2 % 2 == 1))  1.13 us
    ppermute x2, starting transfers between devices, exchange(): got = lax.ppermute(first, CURVE, paired(count, 1, lambda s: s % 2 == 0))  0.68 us
  transfers between devices with their start and end apart: 10, of which 2 were waited for; matrix products, arithmetic and copies ran while one was open for 0% of the time, Pallas kernels for 15%

profile of v1, /device:TPU:0, one launch (start us, length us, event | category | flops | bytes accessed | tf_op | source)
XLA Modules:
  0.0 33.1 jit_solution(15558447400463560632)
XLA Ops:
  0.0 0.1 stack.63.roles
  0.1 0.0 copy-start
  0.1 1.2 %copy-done = f32[512,512]{1,0:T(8,128)S(1)} copy-done((f32[512,512]{1,0:T(8,128)S(1)}, f32[512,512]{1,0:T(8,128)}, u32[]{:S(2)}) %copy-start) | copy-done | bytes 1048600
  1.3 1.0 %copy-done.2 = bf16[512,384]{1,0:T(8,128)(2,1)S(1)} copy-done((bf16[512,384]{1,0:T(8,128)(2,1)S(1)}, bf16[512,384]{1,0:T(8,128)(2,1)}, u32[]{:S(2)}) %copy-start.2) | copy-done | bytes 393240
  2.3 0.8 %copy-done.4 = bf16[64,512]{1,0:T(8,128)(2,1)S(1)} copy-done((bf16[64,512]{1,0:T(8,128)(2,1)S(1)}, bf16[64,512]{1,0:T(8,128)(2,1)}, u32[]{:S(2)}) %copy-start.4) | copy-done | bytes 65560
  3.2 0.7 %copy-done.6 = s32[4,256]{1,0:T(4,128)S(1)} copy-done((s32[4,256]{1,0:T(4,128)S(1)}, s32[4,256]{1,0:T(4,128)}, u32[]{:S(2)}) %copy-start.6) | copy-done | bytes 4120
  3.9 0.7 %copy-done.8 = s32[1,8]{1,0:T(1,128)S(1)} copy-done((s32[1,8]{1,0:T(1,128)S(1)}, s32[1,8]{1,0:T(1,128)}, u32[]{:S(2)}) %copy-start.8) | copy-done | bytes 56
  4.5 1.5 %shard_map.100 = (bf16[512,384]{1,0:T(8,128)(2,1)S(1)}, bf16[192,384]{1,0:T(8,128)(2,1)S(1)}, bf16[128,128]{1,0:T(8,128)(2,1)S(1)}) custom-call(s32[16]{0:T(128)S(1)} %stack.63.roles, s32[1,8]{1,0:T(1,128)S(1)} %copy-done.8, f32[512,512]{1,0:T(8,128)S(1)} %copy-done, s32[4,256]{1,0:T(4,128)S(1)} %copy-done.6, bf16[512,384]{1,0:T(8,128)(2,1)S(1)} %copy-done.2, ...), custom_call_target="tpu_custom_call" | custom-call | flops 200000000 | bytes 1511520 | tf_op jit(solution)/shard_map/pallas_call | solution.py:223
  6.1 0.6 %collective-permute-start = (bf16[192,384]{1,0:T(8,128)(2,1)S(1)}, bf16[192,384]{1,0:T(8,128)(2,1)S(1)}, u32[]{:S(2)}, u32[]{:S(2)}) collective-permute-start(bf16[192,384]{1,0:T(8,128)(2,1)S(1)} %get-tuple-element.19), channel_id=1, source_target_pairs={{0,1},{1,0},{2,3},{3,2},{4,5},{5,4},{6,7},{7,6},{8,9},{9,8},{10,11... | collective-permute-start | bytes 442376 | tf_op jit(solution)/shard_map/ppermute | solution.py:236
  6.7 1.0 %collective-permute-done.got = bf16[192,384]{1,0:T(8,128)(2,1)S(1)} collective-permute-done((bf16[192,384]{1,0:T(8,128)(2,1)S(1)}, bf16[192,384]{1,0:T(8,128)(2,1)S(1)}, u32[]{:S(2)}, u32[]{:S(2)}) %collective-permute-start) | collective-permute-done | bytes 147488 | tf_op jit(solution)/shard_map/ppermute | solution.py:236
  7.7 3.0 %collective-permute-start.3 = (bf16[64,128]{1,0:T(8,128)(2,1)S(1)}, bf16[64,128]{1,0:T(8,128)(2,1)S(1)}, u32[]{:S(2)}, u32[]{:S(2)}) collective-permute-start(bf16[64,128]{1,0:T(8,128)(2,1)S(1)} %pad_maximum_fusion.8), channel_id=1, source_target_pairs={{0,4},{1,5},{2,6},{3,7},{4,0},{5,1},{6,2},{7,3},{8,12},{9,13},{10,... | collective-permute-start | bytes 49160 | tf_op jit(solution)/shard_map/ppermute | solution.py:258
  10.7 0.6 %collective-permute-start.2 = (bf16[96,384]{1,0:T(8,128)(2,1)S(1)}, bf16[96,384]{1,0:T(8,128)(2,1)S(1)}, u32[]{:S(2)}, u32[]{:S(2)}) collective-permute-start(bf16[96,384]{1,0:T(8,128)(2,1)S(1)} %get-tuple-element.37), channel_id=1, source_target_pairs={{0,1},{1,0},{2,4},{3,5},{4,2},{5,3},{6,8},{7,9},{8,6},{9,7},{10,12... | collective-permute-start | bytes 221192 | tf_op jit(solution)/shard_map/ppermute | solution.py:257
  11.3 4.1 %collective-permute-start.1 = (bf16[96,384]{1,0:T(8,128)(2,1)S(1)}, bf16[96,384]{1,0:T(8,128)(2,1)S(1)}, u32[]{:S(2)}, u32[]{:S(2)}) collective-permute-start(bf16[96,384]{1,0:T(8,128)(2,1)S(1)} %get-tuple-element.38), channel_id=1, source_target_pairs={{0,2},{1,3},{2,0},{3,1},{4,6},{5,7},{6,4},{7,5},{8,10},{9,11},{10,... | collective-permute-start | bytes 221192 | tf_op jit(solution)/shard_map/ppermute | solution.py:256
  15.4 1.4 %copy-done.9 = bf16[512,1536]{1,0:T(8,128)(2,1)S(1)} copy-done((bf16[512,1536]{1,0:T(8,128)(2,1)S(1)}, bf16[512,1536]{1,0:T(8,128)(2,1)}, u32[]{:S(2)}) %copy-start.9) | copy-done | bytes 1572888
  16.8 2.4 %shard_map.101 = (f32[512,512]{1,0:T(8,128)S(1)}, f32[512,384]{1,0:T(8,128)S(1)}) custom-call(s32[16]{0:T(128)S(1)} %stack.63.roles, f32[512,512]{1,0:T(8,128)S(1)} %copy-done.1, f32[3,512]{1,0:T(4,128)S(1)} %copy-done.13, s32[1,512]{1,0:T(1,128)S(1)} %bitcast.16, s32[6,512]{1,0:T(8,128)S(1)} %copy-done.12, bf16[512,1536]{1,0:T(8,128)(2,1)S(1)} %copy-done.9, ...), custom_call_target="tpu_custom_call" | custom-call | flops 3000000000 | bytes 3035200 | tf_op jit(solution)/shard_map/pallas_call | solution.py:223
  19.4 0.0 copy-start.10
  19.4 2.8 %shard_map.102 = (f32[512,512]{1,0:T(8,128)S(1)}, bf16[512,384]{1,0:T(8,128)(2,1)S(1)}, bf16[192,384]{1,0:T(8,128)(2,1)S(1)}, bf16[128,128]{1,0:T(8,128)(2,1)S(1)}) custom-call(s32[16]{0:T(128)S(1)} %stack.63.roles, s32[1,8]{1,0:T(1,128)S(1)} %copy-done.8, f32[3,512]{1,0:T(4,128)S(1)} %copy-done.13, s32[1,512]{1,0:T(1,128)S(1)} %bitcast.17, ...), custom_call_target="tpu_custom_call" | custom-call | flops 1000000000 | bytes 3039328 | tf_op jit(solution)/shard_map/pallas_call | solution.py:223
  22.2 0.1 collective-permute-start.5
  22.2 1.3 %collective-permute-done.5.got = bf16[192,384]{1,0:T(8,128)(2,1)S(1)} collective-permute-done((bf16[192,384]{1,0:T(8,128)(2,1)S(1)}, bf16[192,384]{1,0:T(8,128)(2,1)S(1)}, u32[]{:S(2)}, u32[]{:S(2)}) %collective-permute-start.5) | collective-permute-done | bytes 147488 | tf_op jit(solution)/shard_map/ppermute | solution.py:236
  23.6 0.4 %collective-permute-start.8 = (bf16[64,128]{1,0:T(8,128)(2,1)S(1)}, bf16[64,128]{1,0:T(8,128)(2,1)S(1)}, u32[]{:S(2)}, u32[]{:S(2)}) collective-permute-start(bf16[64,128]{1,0:T(8,128)(2,1)S(1)} %pad_maximum_fusion.10), channel_id=1, source_target_pairs={{0,4},{1,5},{2,6},{3,7},{4,0},{5,1},{6,2},{7,3},{8,12},{9,13},{10,... | collective-permute-start | bytes 49160 | tf_op jit(solution)/shard_map/ppermute | solution.py:258
  24.1 0.6 %collective-permute-start.7 = (bf16[96,384]{1,0:T(8,128)(2,1)S(1)}, bf16[96,384]{1,0:T(8,128)(2,1)S(1)}, u32[]{:S(2)}, u32[]{:S(2)}) collective-permute-start(bf16[96,384]{1,0:T(8,128)(2,1)S(1)} %get-tuple-element.35), channel_id=1, source_target_pairs={{0,1},{1,0},{2,4},{3,5},{4,2},{5,3},{6,8},{7,9},{8,6},{9,7},{10,12... | collective-permute-start | bytes 221192 | tf_op jit(solution)/shard_map/ppermute | solution.py:257
  24.7 2.9 %collective-permute-start.6 = (bf16[96,384]{1,0:T(8,128)(2,1)S(1)}, bf16[96,384]{1,0:T(8,128)(2,1)S(1)}, u32[]{:S(2)}, u32[]{:S(2)}) collective-permute-start(bf16[96,384]{1,0:T(8,128)(2,1)S(1)} %get-tuple-element.36), channel_id=1, source_target_pairs={{0,2},{1,3},{2,0},{3,1},{4,6},{5,7},{6,4},{7,5},{8,10},{9,11},{10,... | collective-permute-start | bytes 221192 | tf_op jit(solution)/shard_map/ppermute | solution.py:256
  27.5 2.5 %shard_map.103 = (f32[512,512]{1,0:T(8,128)S(1)}, f32[512,384]{1,0:T(8,128)S(1)}) custom-call(s32[16]{0:T(128)S(1)} %stack.63.roles, f32[512,512]{1,0:T(8,128)S(1)} %copy-done.1, f32[512,512]{1,0:T(8,128)S(1)} %get-tuple-element.21.refs_1_, f32[3,512]{1,0:T(4,128)S(1)} %copy-done.13, s32[1,512]{1,0:T(1,128)S(1)} %bitcast.18, s32[6,512]{1,0:T(8,128)S(1)} %copy-done.12, ...), custom_call_target="tpu_custom_call" | custom-call | flops 3000000000 | bytes 4083776 | tf_op jit(solution)/shard_map/pallas_call | solution.py:223
  30.1 3.0 %shard_map.104 = f32[512,512]{1,0:T(8,128)} custom-call(s32[16]{0:T(128)S(1)} %stack.63.roles, f32[3,512]{1,0:T(4,128)S(1)} %copy-done.13, s32[1,512]{1,0:T(1,128)S(1)} %bitcast.19, s32[6,512]{1,0:T(8,128)S(1)} %copy-done.12, bf16[384,512]{1,0:T(8,128)(2,1)S(1)} %copy-done.11, f32[512,512]{1,0:T(8,128)S(1)} %get-tuple-element.23.base, ...), custom_call_target="tpu_custom_call" | custom-call | flops 1000000000 | bytes 2576448 | tf_op jit(solution)/shard_map/pallas_call | solution.py:223
  (45 shorter events, 0.2 us)
Async XLA Ops:
  0.0 15.4 %copy-start.12 = (s32[6,512]{1,0:T(8,128)S(1)}, s32[6,512]{1,0:T(8,128)}, u32[]{:S(2)}) copy-start(s32[6,512]{1,0:T(8,128)} %neighbours.3) | copy-start | bytes 36868
  0.0 15.4 %copy-start.13 = (f32[3,512]{1,0:T(4,128)S(1)}, f32[3,512]{1,0:T(4,128)}, u32[]{:S(2)}) copy-start(f32[3,512]{1,0:T(4,128)} %velocity.3) | copy-start | bytes 18436
  0.0 15.4 %copy-start.14 = (s32[512]{0:T(512)S(1)}, s32[512]{0:T(512)}, u32[]{:S(2)}) copy-start(s32[512]{0:T(512)} %param.12) | copy-start | bytes 6148
  0.1 1.2 %copy-start = (f32[512,512]{1,0:T(8,128)S(1)}, f32[512,512]{1,0:T(8,128)}, u32[]{:S(2)}) copy-start(f32[512,512]{1,0:T(8,128)} %refs_0_.3) | copy-start | bytes 3145732
  1.3 1.0 %copy-start.2 = (bf16[512,384]{1,0:T(8,128)(2,1)S(1)}, bf16[512,384]{1,0:T(8,128)(2,1)}, u32[]{:S(2)}) copy-start(bf16[512,384]{1,0:T(8,128)(2,1)} %trace_map.3) | copy-start | bytes 1179652
  2.3 0.8 %copy-start.4 = (bf16[64,512]{1,0:T(8,128)(2,1)S(1)}, bf16[64,512]{1,0:T(8,128)(2,1)}, u32[]{:S(2)}) copy-start(bf16[64,512]{1,0:T(8,128)(2,1)} %projection.3) | copy-start | bytes 196612
  3.2 0.7 %copy-start.6 = (s32[4,256]{1,0:T(4,128)S(1)}, s32[4,256]{1,0:T(4,128)}, u32[]{:S(2)}) copy-start(s32[4,256]{1,0:T(4,128)} %records.3) | copy-start | bytes 12292
  4.5 10.9 %copy-start.1 = (f32[512,512]{1,0:T(8,128)S(1)}, f32[512,512]{1,0:T(8,128)}, u32[]{:S(2)}) copy-start(f32[512,512]{1,0:T(8,128)} %refs_0_.3) | copy-start | bytes 3145732
  6.1 1.6 %collective-permute-start = (bf16[192,384]{1,0:T(8,128)(2,1)S(1)}, bf16[192,384]{1,0:T(8,128)(2,1)S(1)}, u32[]{:S(2)}, u32[]{:S(2)}) collective-permute-start(bf16[192,384]{1,0:T(8,128)(2,1)S(1)} %get-tuple-element.19), channel_id=1, source_target_pairs={{0,1},{1,0},{2,3},{3,2},{4,5},{5,4},{6,7},{7,6},{8,9},{9,8},{10,11... | collective-permute-start | bytes 442376 | tf_op jit(solution)/shard_map/ppermute | solution.py:236
  7.7 11.6 %collective-permute-start.3 = (bf16[64,128]{1,0:T(8,128)(2,1)S(1)}, bf16[64,128]{1,0:T(8,128)(2,1)S(1)}, u32[]{:S(2)}, u32[]{:S(2)}) collective-permute-start(bf16[64,128]{1,0:T(8,128)(2,1)S(1)} %pad_maximum_fusion.8), channel_id=1, source_target_pairs={{0,4},{1,5},{2,6},{3,7},{4,0},{5,1},{6,2},{7,3},{8,12},{9,13},{10,... | collective-permute-start | bytes 49160 | tf_op jit(solution)/shard_map/ppermute | solution.py:258
  10.7 8.6 %collective-permute-start.4 = (bf16[64,128]{1,0:T(8,128)(2,1)S(1)}, bf16[64,128]{1,0:T(8,128)(2,1)S(1)}, u32[]{:S(2)}, u32[]{:S(2)}) collective-permute-start(bf16[64,128]{1,0:T(8,128)(2,1)S(1)} %pad_maximum_fusion.9), channel_id=1, source_target_pairs={{0,1},{1,0},{2,3},{3,2},{4,8},{5,9},{6,10},{7,11},{8,4},{9,5},{10,... | collective-permute-start | bytes 49160 | tf_op jit(solution)/shard_map/ppermute | solution.py:259
  10.7 8.6 %collective-permute-start.2 = (bf16[96,384]{1,0:T(8,128)(2,1)S(1)}, bf16[96,384]{1,0:T(8,128)(2,1)S(1)}, u32[]{:S(2)}, u32[]{:S(2)}) collective-permute-start(bf16[96,384]{1,0:T(8,128)(2,1)S(1)} %get-tuple-element.37), channel_id=1, source_target_pairs={{0,1},{1,0},{2,4},{3,5},{4,2},{5,3},{6,8},{7,9},{8,6},{9,7},{10,12... | collective-permute-start | bytes 221192 | tf_op jit(solution)/shard_map/ppermute | solution.py:257
  11.3 8.0 %collective-permute-start.1 = (bf16[96,384]{1,0:T(8,128)(2,1)S(1)}, bf16[96,384]{1,0:T(8,128)(2,1)S(1)}, u32[]{:S(2)}, u32[]{:S(2)}) collective-permute-start(bf16[96,384]{1,0:T(8,128)(2,1)S(1)} %get-tuple-element.38), channel_id=1, source_target_pairs={{0,2},{1,3},{2,0},{3,1},{4,6},{5,7},{6,4},{7,5},{8,10},{9,11},{10,... | collective-permute-start | bytes 221192 | tf_op jit(solution)/shard_map/ppermute | solution.py:256
  15.4 1.4 %copy-start.9 = (bf16[512,1536]{1,0:T(8,128)(2,1)S(1)}, bf16[512,1536]{1,0:T(8,128)(2,1)}, u32[]{:S(2)}) copy-start(bf16[512,1536]{1,0:T(8,128)(2,1)} %refs_5_.1) | copy-start | bytes 4718596
  16.8 2.5 %copy-start.3 = (bf16[512,384]{1,0:T(8,128)(2,1)S(1)}, bf16[512,384]{1,0:T(8,128)(2,1)}, u32[]{:S(2)}) copy-start(bf16[512,384]{1,0:T(8,128)(2,1)} %trace_map.3) | copy-start | bytes 1179652
  16.8 2.5 %copy-start.5 = (bf16[64,512]{1,0:T(8,128)(2,1)S(1)}, bf16[64,512]{1,0:T(8,128)(2,1)}, u32[]{:S(2)}) copy-start(bf16[64,512]{1,0:T(8,128)(2,1)} %projection.3) | copy-start | bytes 196612
  16.8 2.5 %copy-start.7 = (s32[4,256]{1,0:T(4,128)S(1)}, s32[4,256]{1,0:T(4,128)}, u32[]{:S(2)}) copy-start(s32[4,256]{1,0:T(4,128)} %records.3) | copy-start | bytes 12292
  16.8 2.5 %copy-start.11 = (bf16[384,512]{1,0:T(8,128)(2,1)S(1)}, bf16[384,512]{1,0:T(8,128)(2,1)}, u32[]{:S(2)}) copy-start(bf16[384,512]{1,0:T(8,128)(2,1)} %lift.3) | copy-start | bytes 1179652
  19.4 8.2 %copy-start.10 = (bf16[512,1536]{1,0:T(8,128)(2,1)S(1)}, bf16[512,1536]{1,0:T(8,128)(2,1)}, u32[]{:S(2)}) copy-start(bf16[512,1536]{1,0:T(8,128)(2,1)} %refs_5_.1) | copy-start | bytes 4718596
  22.2 1.4 %collective-permute-start.5 = (bf16[192,384]{1,0:T(8,128)(2,1)S(1)}, bf16[192,384]{1,0:T(8,128)(2,1)S(1)}, u32[]{:S(2)}, u32[]{:S(2)}) collective-permute-start(bf16[192,384]{1,0:T(8,128)(2,1)S(1)} %get-tuple-element.25), channel_id=1, source_target_pairs={{0,1},{1,0},{2,3},{3,2},{4,5},{5,4},{6,7},{7,6},{8,9},{9,8},{10,11... | collective-permute-start | bytes 442376 | tf_op jit(solution)/shard_map/ppermute | solution.py:236
  23.6 6.5 %collective-permute-start.8 = (bf16[64,128]{1,0:T(8,128)(2,1)S(1)}, bf16[64,128]{1,0:T(8,128)(2,1)S(1)}, u32[]{:S(2)}, u32[]{:S(2)}) collective-permute-start(bf16[64,128]{1,0:T(8,128)(2,1)S(1)} %pad_maximum_fusion.10), channel_id=1, source_target_pairs={{0,4},{1,5},{2,6},{3,7},{4,0},{5,1},{6,2},{7,3},{8,12},{9,13},{10,... | collective-permute-start | bytes 49160 | tf_op jit(solution)/shard_map/ppermute | solution.py:258
  24.1 6.0 %collective-permute-start.9 = (bf16[64,128]{1,0:T(8,128)(2,1)S(1)}, bf16[64,128]{1,0:T(8,128)(2,1)S(1)}, u32[]{:S(2)}, u32[]{:S(2)}) collective-permute-start(bf16[64,128]{1,0:T(8,128)(2,1)S(1)} %pad_maximum_fusion.11), channel_id=1, source_target_pairs={{0,1},{1,0},{2,3},{3,2},{4,8},{5,9},{6,10},{7,11},{8,4},{9,5},{10,... | collective-permute-start | bytes 49160 | tf_op jit(solution)/shard_map/ppermute | solution.py:259
  24.1 6.0 %collective-permute-start.7 = (bf16[96,384]{1,0:T(8,128)(2,1)S(1)}, bf16[96,384]{1,0:T(8,128)(2,1)S(1)}, u32[]{:S(2)}, u32[]{:S(2)}) collective-permute-start(bf16[96,384]{1,0:T(8,128)(2,1)S(1)} %get-tuple-element.35), channel_id=1, source_target_pairs={{0,1},{1,0},{2,4},{3,5},{4,2},{5,3},{6,8},{7,9},{8,6},{9,7},{10,12... | collective-permute-start | bytes 221192 | tf_op jit(solution)/shard_map/ppermute | solution.py:257
  24.7 5.4 %collective-permute-start.6 = (bf16[96,384]{1,0:T(8,128)(2,1)S(1)}, bf16[96,384]{1,0:T(8,128)(2,1)S(1)}, u32[]{:S(2)}, u32[]{:S(2)}) collective-permute-start(bf16[96,384]{1,0:T(8,128)(2,1)S(1)} %get-tuple-element.36), channel_id=1, source_target_pairs={{0,2},{1,3},{2,0},{3,1},{4,6},{5,7},{6,4},{7,5},{8,10},{9,11},{10,... | collective-permute-start | bytes 221192 | tf_op jit(solution)/shard_map/ppermute | solution.py:256
  (1 other events, 0.7 us)

commit v2 on v1

v2 whole, which is shorter than its diff:
```python
import jax
import jax.numpy as jnp
from jax import lax
from jax.experimental import pallas as pl
from jax.experimental.pallas import tpu as pltpu
from jax.sharding import PartitionSpec as P

time_step = 0.3
bf16 = jnp.bfloat16
f32 = jnp.float32
CURVE = ("curve", "sub", "pair")


def dot(a, b):
    return jnp.dot(a, b, preferred_element_type=f32)


def transposed(rows):
    pad = jnp.zeros((128 - rows.shape[0], rows.shape[1]), f32)
    return jnp.concatenate([rows, pad], axis=0).T


def lanes(shape):
    return lax.broadcasted_iota(jnp.int32, shape, 1)


def rows_of(shape):
    return lax.broadcasted_iota(jnp.int32, shape, 0)


def swapped(tile):
    turned = pltpu.roll(tile.astype(f32), 64, 1)
    low = lanes(turned.shape) < 64
    top = jnp.where(low, turned, 0.0).astype(bf16)
    bottom = jnp.where(low, 0.0, turned).astype(bf16)
    return jnp.concatenate([top, bottom], axis=0)


def hot(column, width):
    rows = column.shape[0]
    picked = column.astype(jnp.int32) == lanes((rows, width))
    return jnp.where(picked, 1.0, 0.0).astype(bf16)


def place():
    return lax.axis_index("curve") * lax.axis_size("sub") + lax.axis_index("sub"), lax.axis_index("pair")


def record_columns(records, counts):
    slots = records.shape[1]
    capacity = slots // 8
    source, face, kind, target = (records[i : i + 1, :] for i in range(4))
    slot = lanes((1, slots))
    allowed = jnp.zeros((1, slots), jnp.int32)
    for j in range(8):
        inside = (slot >= j * capacity) & (slot < (j + 1) * capacity)
        allowed = jnp.where(inside, counts[:, j : j + 1] + j * capacity, allowed)
    facing = jnp.where(slot < allowed, jnp.bitwise_xor(face, 1) + 1, 0)
    digits = [lax.shift_right_logical(target, 4), jnp.bitwise_and(target, 15), facing]
    gap = jnp.zeros((61, slots), f32)
    rows = [x.astype(f32) for x in (source, face, kind)] + [gap] + [x.astype(f32) for x in digits]
    return transposed(jnp.concatenate(rows, axis=0))


def send(traces, source_hot, column, projection, first_out, own_out, blocks):
    elements, width = traces.shape
    slots = column.shape[0]
    capacity = slots // 8
    rim = elements // 8
    chip, core = place()
    own = lax.rem(chip, 2)
    second = lax.rem(lax.div(chip, 2), 2)
    shape = (slots, 128)
    lane = lanes(shape)
    half = jnp.where(lane < 64, 0.0, 1.0)
    picked = dot(source_hot, traces[...])
    face = column[:, 1:2]
    row = jnp.zeros(shape, f32)
    for t in range(3):
        row = jnp.where(half + 2 * t == face, picked[:, 128 * t : 128 * t + 128], row)
    every = dot(row.astype(bf16), jnp.concatenate([projection[...]] * 2, axis=0))
    kind = column[:, 2:3]
    folded = jnp.zeros(shape, f32)
    for t in range(4):
        folded = jnp.where(half + 2 * t == kind, every[:, 128 * t : 128 * t + 128], folded)
    piece = folded + pltpu.roll(folded, 64, 1)
    blocks[...] = jnp.where(lane < 64, piece, column[...]).astype(bf16)

    def block(index):
        return blocks[pl.ds(pl.multiple_of(index * capacity, capacity), capacity), :]

    def pick(which, a, b):
        return a + which * (b - a)

    final_at = pl.multiple_of(pick(core, elements - rim, 0), rim)
    other_at = pl.multiple_of(pick(core, 0, elements - rim), rim)
    first_out[0:rim, :] = traces[pl.ds(final_at, rim), :]
    first_out[rim : 2 * rim, :] = traces[pl.ds(other_at, rim), :]
    at = 2 * rim
    for t, (a, b) in enumerate(((4, 3), (6, 4), (3, 1))):
        first_out[at : at + capacity, 128 * t : 128 * t + 128] = block(pick(core, a, b))
    at += capacity
    first_out[at : at + capacity, 0:128] = block(pick(core, 1, 6))
    first_out[at : at + capacity, 128:] = jnp.zeros((capacity, width - 128), bf16)
    for t, (which, a, b) in enumerate(((own, 5, 2), (own, 2, 5), (second, 7, 0), (second, 0, 7))):
        own_out[capacity * t : capacity * t + capacity, :] = block(pick(which, a, b))


def start_kernel(
    state_in, trace_map_in, records_in, counts_in, velocity_in, levels_in, neighbours_in, projection_in,
    trace_map, projection, traces, first_out, own_out, source_hot, column, elements_column,
    state, records, counts, velocity, levels, neighbours, blocks, sems
):
    elements = state.shape[0]
    part = elements // 2
    pairs = [(trace_map_in, trace_map)]
    for i in range(2):
        cut = pl.ds(i * part, part)
        pairs.append((state_in.at[cut], state.at[cut]))
    pairs += [(records_in, records), (counts_in, counts), (velocity_in, velocity), (levels_in, levels)]
    pairs += [(neighbours_in, neighbours), (projection_in, projection)]
    copies = [pltpu.make_async_copy(a, b, sems.at[i]) for i, (a, b) in enumerate(pairs)]
    for copy in copies:
        copy.start()
    for copy in copies[3:]:
        copy.wait()
    columns = record_columns(records, counts)
    column[...] = columns
    source_hot[...] = hot(columns[:, 0:1], elements)
    elements_column[...] = element_columns(velocity, levels, neighbours)
    copies[0].wait()
    for i in range(2):
        copies[1 + i].wait()
        cut = slice(i * part, i * part + part)
        traces[cut, :] = dot(state[cut, :].astype(bf16), trace_map[...]).astype(bf16)
    send(traces, source_hot[...], column, projection, first_out, own_out, blocks)


def element_columns(velocity, levels, neighbours):
    elements = velocity.shape[1]
    rim = elements // 8
    chip, core = place()
    raw = neighbours[...].astype(f32)
    local = raw - ((2 * chip + core) * elements).astype(f32)
    before = ((2 - core) * rim).astype(f32)
    after = (elements - core * rim).astype(f32)
    index = jnp.where(local < 0, local + before, jnp.where(local >= elements, local - after, -1.0))
    index = jnp.where(raw < 0, -1.0, index)
    scale = jnp.exp2(levels[...].astype(f32)) * 0.25
    gap = jnp.zeros((4, elements), f32)
    return transposed(jnp.concatenate([velocity[...], scale, gap, local, gap[0:2], index], axis=0))


def volume_term(column, lowered, stiffness, n, step):
    modes = stiffness.shape[0]
    volume = jnp.zeros((lowered.shape[0], step), f32)
    for d in range(3):
        volume += column[:, d : d + 1] * dot(lowered, stiffness[:, d * modes + n : d * modes + n + step])
    return column[:, 3:4] * volume


def own_part(column, traces, partial_out):
    elements = traces.shape[0]
    for t in range(3):
        tile = traces[:, 128 * t : 128 * t + 128]
        at = 8 + 2 * t
        picks = [hot(column[:, at + i : at + i + 1], elements) for i in range(2)]
        near = dot(jnp.concatenate(picks, axis=1), swapped(tile))
        partial_out[:, 128 * t : 128 * t + 128] = near - tile.astype(f32)


def local_kernel(stiffness_in, lift_in, column, state, traces, stiffness, lift, base, partial, inflow, picks, sems):
    elements, modes = state.shape
    rim = elements // 8
    copies = [
        pltpu.make_async_copy(stiffness_in, stiffness, sems.at[0]),
        pltpu.make_async_copy(lift_in, lift, sems.at[1]),
    ]
    for copy in copies:
        copy.start()
    columns = column[...]
    own_part(columns, traces, partial)
    low = lanes((elements, 128)) < 64
    for t in range(3):
        speed = columns[:, t : t + 1]
        inflow[:, 128 * t : 128 * t + 128] = columns[:, 3:4] * jnp.maximum(jnp.where(low, speed, -speed), 0.0)
    for i in range(6):
        picks[:, 2 * rim * i : 2 * rim * i + 2 * rim] = hot(columns[:, 16 + i : 17 + i], 2 * rim)
    lowered = state[...].astype(bf16)
    step = 256
    copies[0].wait()
    for n in range(0, modes, step):
        base[:, n : n + step] = state[:, n : n + step] + time_step * volume_term(columns, lowered, stiffness, n, step)
    copies[1].wait()


def second_local_kernel(column, state, field, stiffness, traces, base, partial):
    modes = state.shape[1]
    columns = column[...]
    lowered = field[...].astype(bf16)
    step = 256
    for n in range(0, modes, step):
        volume = volume_term(columns, lowered, stiffness, n, step)
        base[:, n : n + step] = 0.5 * (state[:, n : n + step] + field[:, n : n + step]) + 0.5 * time_step * volume
    own_part(columns, traces, partial)


def gather_arrivals(got, got_even, got_odd, got_a, got_b, arrived):
    capacity = arrived.shape[0] // 8
    rim = 2 * capacity
    at = 2 * rim
    chip, core = place()
    own = lax.rem(chip, 2)
    second = lax.rem(lax.div(chip, 2), 2)
    arrived[0:capacity, :] = got[at : at + capacity, 0:128]
    for i, ref in enumerate((got_even, got_odd)):
        for k in range(2):
            to = capacity * (1 + 2 * i + k)
            arrived[to : to + capacity, :] = ref[rim : rim + capacity, 128 * k : 128 * k + 128]
    arrived[5 * capacity : 6 * capacity, :] = got_a[0:capacity, :]
    arrived[6 * capacity : 7 * capacity, :] = got_b[0:capacity, :]
    arrived[7 * capacity :, :] = jnp.where(
        second != core, got_a[capacity : 2 * capacity, :], got_b[capacity : 2 * capacity, :]
    )
    forward = jnp.where(own != core, got_even[0:rim, :], got_odd[0:rim, :])
    return jnp.concatenate([got[0:rim, :], forward], axis=0)


def targets(pieces, elements):
    face_of = jnp.where(rows_of((128, 128)) == 66, 1.0, 0.0).astype(bf16)
    face = dot(pieces, face_of) - 1.0
    lane = lanes((8, 128))
    element_of = jnp.where(lane == 64, 16.0, jnp.where(lane == 65, 1.0, 0.0)).astype(bf16)
    target = lax.dot_general(element_of, pieces, (((1,), (1,)), ((), ())), preferred_element_type=f32)[0:1, :]
    match = rows_of((elements, pieces.shape[0])) == target.astype(jnp.int32)
    return face, jnp.where(match, 1.0, 0.0).astype(bf16)


def fluxes(pieces, face, element_hot, window, partial, inflow, picks):
    half = jnp.where(lanes(pieces.shape) < 64, 0.0, 1.0)
    plain = jnp.where(half == 0.0, pieces.astype(f32), 0.0)
    both = plain + pltpu.roll(plain, 64, 1)
    parts = []
    for t in range(3):
        cut = slice(128 * t, 128 * t + 128)
        placed = jnp.where(half + 2 * t == face, both, 0.0).astype(bf16)
        near = dot(picks[:, 256 * t : 256 * t + 256], swapped(window[:, cut]))
        mortar = dot(element_hot, placed)
        parts.append((inflow[:, cut] * (partial[:, cut] + near + mortar)).astype(bf16))
    return jnp.concatenate(parts, axis=1)


def middle_kernel(
    lift, base, partial, inflow, picks, got, got_even, got_odd, got_a, got_b, trace_map, projection, source_hot, column,
    field, traces, first_out, own_out, face_out, element_hot_out, arrived, blocks
):
    elements = base.shape[0]
    window = gather_arrivals(got, got_even, got_odd, got_a, got_b, arrived)
    pieces = arrived[...]
    face, element_hot = targets(pieces, elements)
    face_out[...] = face
    element_hot_out[...] = element_hot
    flux = fluxes(pieces, face, element_hot, window, partial, inflow, picks)
    new = base[...] + time_step * dot(flux, lift[...])
    field[...] = new
    traces[...] = dot(new.astype(bf16), trace_map[...]).astype(bf16)
    send(traces, source_hot[...], column, projection, first_out, own_out, blocks)


def end_kernel(
    lift, base, partial, inflow, picks, got, got_even, got_odd, got_a, got_b, face, element_hot, field, arrived, result, sems
):
    elements = base.shape[0]
    window = gather_arrivals(got, got_even, got_odd, got_a, got_b, arrived)
    flux = fluxes(arrived[...], face[...], element_hot[...], window, partial, inflow, picks)
    part = elements // 2
    copies = []
    for i in range(2):
        cut = slice(i * part, i * part + part)
        result[cut, :] = base[cut, :] + 0.5 * time_step * dot(flux[cut, :], lift[...])
        rows = pl.ds(i * part, part)
        copies.append(pltpu.make_async_copy(result.at[rows], field.at[rows], sems.at[i]))
        copies[i].start()
    for copy in copies:
        copy.wait()


def paired(count, step, lower):
    partner = {}
    for s in range(count):
        if lower(s) and s + step < count:
            partner[s] = s + step
            partner[s + step] = s
    rest = [s for s in range(count) if s not in partner]
    for a, b in zip(rest[::2], rest[1::2]):
        partner[a] = b
        partner[b] = a
    return sorted(partner.items())


def call(kernel, out_shape, scratch, flops, far, near, out_space=pltpu.VMEM):
    operands = [pltpu.with_memory_space_constraint(x, pltpu.HBM) for x in far] + list(near)
    read = sum(x.size * x.dtype.itemsize for x in operands)
    specs = [pl.BlockSpec(memory_space=pl.ANY)] * len(far) + [pl.BlockSpec(memory_space=pltpu.VMEM)] * len(near)
    return pl.pallas_call(
        kernel,
        out_shape=out_shape,
        in_specs=specs,
        out_specs=[pl.BlockSpec(memory_space=out_space)] * len(out_shape),
        scratch_shapes=scratch,
        compiler_params=pltpu.CompilerParams(vmem_limit_bytes=16 * 1024 * 1024),
        cost_estimate=pl.CostEstimate(flops=flops, bytes_accessed=read, transcendentals=0),
    )(*operands)


def exchange(first, own, chip, core, rim, capacity):
    count = lax.axis_size(CURVE)
    got = lax.ppermute(first, CURVE, paired(count, 1, lambda s: s % 2 == 0))
    forward = got[rim : 2 * rim]
    at = 2 * rim
    up = got[at : at + capacity, 128:256]
    down = got[at : at + capacity, 256:384]
    far = got[at + capacity : at + 2 * capacity, 0:128]
    blank = jnp.zeros_like(up)
    even = chip % 2 == 0
    upper = ((chip // 2) % 2 == 0) == (core == 0)
    mine = [own[capacity * t : capacity * t + capacity] for t in range(4)]

    def near(block, other):
        return jnp.concatenate([forward, jnp.concatenate([block, other, blank], axis=1)], axis=0)

    to_even = near(mine[0], jnp.where(even, up, down))
    to_odd = near(mine[1], jnp.where(even, down, up))
    to_a = jnp.concatenate([mine[2], jnp.where(upper, far, 0)], axis=0)
    to_b = jnp.concatenate([mine[3], jnp.where(upper, 0, far)], axis=0)
    return (
        got,
        lax.ppermute(to_even, CURVE, paired(count, 2, lambda s: (s // 2) % 2 == 0)),
        lax.ppermute(to_odd, CURVE, paired(count, 2, lambda s: (s // 2) % 2 == 1)),
        lax.ppermute(to_a, CURVE, paired(count, 4, lambda s: (s // 4) % 2 == 0)),
        lax.ppermute(to_b, CURVE, paired(count, 4, lambda s: (s // 4) % 2 == 1)),
    )


def body(
    state, velocity, levels, neighbours, records, counts, stiffness, trace_map, lift, projection
):
    elements, modes = state.shape
    width = trace_map.shape[1]
    slots = records.shape[1]
    capacity = slots // counts.shape[1]
    rim = elements // 8
    chip, core = place()

    def array(shape, dtype):
        return jax.ShapeDtypeStruct(shape, dtype)

    def like(x):
        return array(x.shape, x.dtype)

    sent = [
        array((elements, width), bf16),
        array((2 * rim + 2 * capacity, width), bf16),
        array((4 * capacity, 128), bf16),
    ]
    whole = array((elements, modes), f32)
    faces = array((elements, width), f32)
    blocks = pltpu.VMEM((slots, 128), bf16)
    column_shape = array((slots, 128), f32)

    levels = levels.reshape(1, elements)
    vmem = pltpu.VMEM
    wide = (elements, 128)
    trace_map, projection, traces, first, own, source_hot, column, element_column = call(
        start_kernel,
        [like(trace_map), like(projection)]
        + sent
        + [array((slots, elements), bf16), column_shape, array(wide, f32)],
        [vmem(x.shape, x.dtype) for x in (state, records, counts, velocity, levels, neighbours)]
        + [blocks, pltpu.SemaphoreType.DMA((9,))],
        2 * 10**8,
        (state, trace_map, records, counts, velocity, levels, neighbours, projection),
        (),
    )
    got = exchange(first, own, chip, core, rim, capacity)
    stiffness, lift, base, partial, inflow, picks = call(
        local_kernel,
        [like(stiffness), like(lift), whole, faces, faces, array((elements, 12 * rim), bf16)],
        [pltpu.SemaphoreType.DMA((2,))],
        3 * 10**9,
        (stiffness, lift),
        (element_column, state, traces),
    )
    field, traces, first, own, face, element_hot = call(
        middle_kernel,
        [whole] + sent + [column_shape, array((elements, slots), bf16)],
        [blocks, blocks],
        10**9,
        (),
        (lift, base, partial, inflow, picks, *got, trace_map, projection, source_hot, column),
    )
    got = exchange(first, own, chip, core, rim, capacity)
    base, partial = call(
        second_local_kernel, [whole, faces], [], 3 * 10**9, (), (element_column, state, field, stiffness, traces)
    )
    return call(
        end_kernel,
        [whole],
        [blocks, vmem((elements, modes), f32), pltpu.SemaphoreType.DMA((2,))],
        10**9,
        (),
        (lift, base, partial, inflow, picks, *got, face, element_hot),
        out_space=pl.ANY,
    )[0]


def solution(mesh):
    placed = (
        P(("groups", "curve", "sub", "pair"), None),
        P(None, ("groups", "curve", "sub", "pair")),
        P(("groups", "curve", "sub", "pair")),
        P(None, ("groups", "curve", "sub", "pair")),
        P(None, ("groups", "curve", "sub", "pair")),
        P(("groups", "curve", "sub", "pair"), None),
        P(),
        P(),
        P(),
        P(),
    )
    return jax.shard_map(
        body,
        mesh=mesh,
        in_specs=placed,
        out_specs=P(("groups", "curve", "sub", "pair"), None),
        check_vma=False,
    )
```

time: 33.4 us -> 27.8 us (0.83)
  local copies, waits for them, and re-layouts: 5.95 us -> 0.03 us
  starting transfers between devices: 12.2 us -> 13.2 us
  Pallas kernels: 12.2 us -> 11.4 us
  waiting for transfers between devices: 2.37 us -> 2.83 us
    unnamed x30 -> x2, local copies, waits for them, and re-layouts: 5.84 us -> 0.01 us
    ppermute x2, starting transfers between devices: 3.45 us -> 4.52 us  [exchange(): lax.ppermute(to_a, CURVE, paired(count, 4, lambda s: s // 4 % 2 == 0))]
    pallas_call x5, Pallas kernels: 12.2 us -> 11.4 us  [call(): pl.pallas_call(kernel, out_shape=out_shape, in_specs=specs, out_specs=[pl...]
    ppermute x2, waiting for transfers between devices: 0.01 us -> 0.46 us  [exchange(): lax.ppermute(to_even, CURVE, paired(count, 2, lambda s: s // 2 % 2 == 0))]
  transfers between devices with their start and end apart: 10 -> 10, of which waited for: 2 -> 3; matrix products, arithmetic and copies ran while one was open for 0% -> 0% of each run, Pallas kernels for 15% -> 17%
where the time goes in v2:
time: 27.8 us; the launch traced here: 27.7 us
  starting transfers between devices  13.2 us (47%)
  Pallas kernels  11.4 us (41%)
  waiting for transfers between devices  2.83 us (10%)
    pallas_call x5, Pallas kernels, call(): pl.pallas_call(kernel, out_shape=out_shape, in_specs=specs, out_specs=[pl...  11.4 us
    ppermute x2, starting transfers between devices, exchange(): lax.ppermute(to_even, CURVE, paired(count, 2, lambda s: s // 2 % 2 == 0))  7 us
    ppermute x2, starting transfers between devices, exchange(): lax.ppermute(to_a, CURVE, paired(count, 4, lambda s: s // 4 % 2 == 0))  4.52 us
    ppermute x2, waiting for transfers between devices, exchange(): got = lax.ppermute(first, CURVE, paired(count, 1, lambda s: s % 2 == 0))  2.35 us
    ppermute x2, starting transfers between devices, exchange(): lax.ppermute(to_odd, CURVE, paired(count, 2, lambda s: s // 2 % 2 == 1))  1.13 us
    ppermute x2, starting transfers between devices, exchange(): got = lax.ppermute(first, CURVE, paired(count, 1, lambda s: s % 2 == 0))  0.59 us
  transfers between devices with their start and end apart: 10, of which 3 were waited for; matrix products, arithmetic and copies ran while one was open for 0% of the time, Pallas kernels for 17%

profile of v2, /device:TPU:0, one launch (start us, length us, event | category | flops | bytes accessed | tf_op | source)
XLA Modules:
  0.0 27.7 jit_solution(10553258176754116773)
XLA Ops:
  0.0 2.9 %shard_map.100 = (bf16[512,384]{1,0:T(8,128)(2,1)S(1)}, bf16[64,512]{1,0:T(8,128)(2,1)S(1)}, bf16[512,384]{1,0:T(8,128)(2,1)S(1)}, bf16[192,384]{1,0:T(8,128)(2,...) custom-call(f32[512,512]{1,0:T(8,128)} %state.3, ...), custom_call_target="tpu_custom_call" | custom-call | flops 200000000 | bytes 1531936 | tf_op jit(solution)/shard_map/pallas_call | solution.py:305
  2.9 0.5 %collective-permute-start = (bf16[192,384]{1,0:T(8,128)(2,1)S(1)}, bf16[192,384]{1,0:T(8,128)(2,1)S(1)}, u32[]{:S(2)}, u32[]{:S(2)}) collective-permute-start(bf16[192,384]{1,0:T(8,128)(2,1)S(1)} %get-tuple-element.34), channel_id=1, source_target_pairs={{0,1},{1,0},{2,3},{3,2},{4,5},{5,4},{6,7},{7,6},{8,9},{9,8},{10,11... | collective-permute-start | bytes 442376 | tf_op jit(solution)/shard_map/ppermute | solution.py:318
  3.4 1.0 %collective-permute-done.got = bf16[192,384]{1,0:T(8,128)(2,1)S(1)} collective-permute-done((bf16[192,384]{1,0:T(8,128)(2,1)S(1)}, bf16[192,384]{1,0:T(8,128)(2,1)S(1)}, u32[]{:S(2)}, u32[]{:S(2)}) %collective-permute-start) | collective-permute-done | bytes 147488 | tf_op jit(solution)/shard_map/ppermute | solution.py:318
  4.4 3.0 %collective-permute-start.3 = (bf16[64,128]{1,0:T(8,128)(2,1)S(1)}, bf16[64,128]{1,0:T(8,128)(2,1)S(1)}, u32[]{:S(2)}, u32[]{:S(2)}) collective-permute-start(bf16[64,128]{1,0:T(8,128)(2,1)S(1)} %pad_maximum_fusion.8), channel_id=1, source_target_pairs={{0,4},{1,5},{2,6},{3,7},{4,0},{5,1},{6,2},{7,3},{8,12},{9,13},{10,... | collective-permute-start | bytes 49160 | tf_op jit(solution)/shard_map/ppermute | solution.py:340
  7.4 0.0 collective-permute-start.4
  7.5 0.6 %collective-permute-start.2 = (bf16[96,384]{1,0:T(8,128)(2,1)S(1)}, bf16[96,384]{1,0:T(8,128)(2,1)S(1)}, u32[]{:S(2)}, u32[]{:S(2)}) collective-permute-start(bf16[96,384]{1,0:T(8,128)(2,1)S(1)} %get-tuple-element.59), channel_id=1, source_target_pairs={{0,1},{1,0},{2,4},{3,5},{4,2},{5,3},{6,8},{7,9},{8,6},{9,7},{10,12... | collective-permute-start | bytes 221192 | tf_op jit(solution)/shard_map/ppermute | solution.py:339
  8.0 4.1 %collective-permute-start.1 = (bf16[96,384]{1,0:T(8,128)(2,1)S(1)}, bf16[96,384]{1,0:T(8,128)(2,1)S(1)}, u32[]{:S(2)}, u32[]{:S(2)}) collective-permute-start(bf16[96,384]{1,0:T(8,128)(2,1)S(1)} %get-tuple-element.60), channel_id=1, source_target_pairs={{0,2},{1,3},{2,0},{3,1},{4,6},{5,7},{6,4},{7,5},{8,10},{9,11},{10,... | collective-permute-start | bytes 221192 | tf_op jit(solution)/shard_map/ppermute | solution.py:338
  12.1 2.8 %shard_map.101 = (bf16[512,1536]{1,0:T(8,128)(2,1)S(1)}, bf16[384,512]{1,0:T(8,128)(2,1)S(1)}, f32[512,512]{1,0:T(8,128)S(1)}, f32[512,384]{1,0:T(8,128)S(1)}, f...) custom-call(bf16[512,1536]{1,0:T(8,128)(2,1)} %stiffness_in.1, bf16[384,512]{1,0:T(8,128)(2,1)} %lift_in.1, ...), custom_call_target="tpu_custom_call" | custom-call | flops 3000000000 | bytes 3670016 | tf_op jit(solution)/shard_map/pallas_call | solution.py:305
  15.0 0.0 collective-permute-done.3.got_a
  15.0 0.0 collective-permute-done.4.got_b
  15.0 0.0 collective-permute-done.2.got_odd
  15.0 0.0 collective-permute-done.1.got_even
  15.0 1.8 %shard_map.102 = (f32[512,512]{1,0:T(8,128)S(1)}, bf16[512,384]{1,0:T(8,128)(2,1)S(1)}, bf16[192,384]{1,0:T(8,128)(2,1)S(1)}, bf16[128,128]{1,0:T(8,128)(2,1)S(1...) custom-call(bf16[384,512]{1,0:T(8,128)(2,1)S(1)} %get-tuple-element.29.lift, ...), custom_call_target="tpu_custom_call" | custom-call | flops 1000000000 | bytes 4980736 | tf_op jit(solution)/shard_map/pallas_call | solution.py:305
  16.8 0.1 collective-permute-start.5
  16.9 1.3 %collective-permute-done.5.got = bf16[192,384]{1,0:T(8,128)(2,1)S(1)} collective-permute-done((bf16[192,384]{1,0:T(8,128)(2,1)S(1)}, bf16[192,384]{1,0:T(8,128)(2,1)S(1)}, u32[]{:S(2)}, u32[]{:S(2)}) %collective-permute-start.5) | collective-permute-done | bytes 147488 | tf_op jit(solution)/shard_map/ppermute | solution.py:318
  18.3 1.5 %collective-permute-start.8 = (bf16[64,128]{1,0:T(8,128)(2,1)S(1)}, bf16[64,128]{1,0:T(8,128)(2,1)S(1)}, u32[]{:S(2)}, u32[]{:S(2)}) collective-permute-start(bf16[64,128]{1,0:T(8,128)(2,1)S(1)} %pad_maximum_fusion.10), channel_id=1, source_target_pairs={{0,4},{1,5},{2,6},{3,7},{4,0},{5,1},{6,2},{7,3},{8,12},{9,13},{10,... | collective-permute-start | bytes 49160 | tf_op jit(solution)/shard_map/ppermute | solution.py:340
  19.8 0.0 collective-permute-start.9
  19.8 0.6 %collective-permute-start.7 = (bf16[96,384]{1,0:T(8,128)(2,1)S(1)}, bf16[96,384]{1,0:T(8,128)(2,1)S(1)}, u32[]{:S(2)}, u32[]{:S(2)}) collective-permute-start(bf16[96,384]{1,0:T(8,128)(2,1)S(1)} %get-tuple-element.57), channel_id=1, source_target_pairs={{0,1},{1,0},{2,4},{3,5},{4,2},{5,3},{6,8},{7,9},{8,6},{9,7},{10,12... | collective-permute-start | bytes 221192 | tf_op jit(solution)/shard_map/ppermute | solution.py:339
  20.4 2.9 %collective-permute-start.6 = (bf16[96,384]{1,0:T(8,128)(2,1)S(1)}, bf16[96,384]{1,0:T(8,128)(2,1)S(1)}, u32[]{:S(2)}, u32[]{:S(2)}) collective-permute-start(bf16[96,384]{1,0:T(8,128)(2,1)S(1)} %get-tuple-element.58), channel_id=1, source_target_pairs={{0,2},{1,3},{2,0},{3,1},{4,6},{5,7},{6,4},{7,5},{8,10},{9,11},{10,... | collective-permute-start | bytes 221192 | tf_op jit(solution)/shard_map/ppermute | solution.py:338
  23.3 1.9 %shard_map.103 = (f32[512,512]{1,0:T(8,128)S(1)}, f32[512,384]{1,0:T(8,128)S(1)}) custom-call(f32[512,128]{1,0:T(8,128)S(1)} %get-tuple-element.27.column, f32[512,512]{1,0:T(8,128)S(1)} %copy-done, f32[512,512]{1,0:T(8,128)S(1)} %get-tuple-element.40.field, bf16[512,1536]{1,0:T(8,128)(2,1)S(1)} %get-tuple-element.41.stiffness, ...), custom_call_target="tpu_custom_call" | custom-call | flops 3000000000 | bytes 4325376 | tf_op jit(solution)/shard_map/pallas_call | solution.py:305
  25.2 0.0 collective-permute-done.8.got_a
  25.2 0.0 collective-permute-done.9.got_b
  25.3 0.5 %collective-permute-done.6.got_even = bf16[96,384]{1,0:T(8,128)(2,1)S(1)} collective-permute-done((bf16[96,384]{1,0:T(8,128)(2,1)S(1)}, bf16[96,384]{1,0:T(8,128)(2,1)S(1)}, u32[]{:S(2)}, u32[]{:S(2)}) %collective-permute-start.6) | collective-permute-done | bytes 73760 | tf_op jit(solution)/shard_map/ppermute | solution.py:338
  25.7 2.0 %shard_map.104 = f32[512,512]{1,0:T(8,128)} custom-call(bf16[384,512]{1,0:T(8,128)(2,1)S(1)} %get-tuple-element.29.lift, f32[512,512]{1,0:T(8,128)S(1)} %get-tuple-element.43.base, f32[512,384]{1,0:T(8,128)S(1)} %get-tuple-element.44.partial, f32[512,384]{1,0:T(8,128)S(1)} %get-tuple-element.32.inflow, bf16[512,768]{1,0:T(8,128)(2,1)S(1)} %get-tuple-element.33.picks, ...), custom_call_target="tpu_custom_call" | custom-call | flops 1000000000 | bytes 4521984 | tf_op jit(solution)/shard_map/pallas_call | solution.py:305
  (16 shorter events, 0.1 us)
Async XLA Ops:
  0.0 12.1 %copy-start = (f32[512,512]{1,0:T(8,128)S(1)}, f32[512,512]{1,0:T(8,128)}, u32[]{:S(2)}) copy-start(f32[512,512]{1,0:T(8,128)} %state.3) | copy-start | bytes 3145732
  2.9 1.5 %collective-permute-start = (bf16[192,384]{1,0:T(8,128)(2,1)S(1)}, bf16[192,384]{1,0:T(8,128)(2,1)S(1)}, u32[]{:S(2)}, u32[]{:S(2)}) collective-permute-start(bf16[192,384]{1,0:T(8,128)(2,1)S(1)} %get-tuple-element.34), channel_id=1, source_target_pairs={{0,1},{1,0},{2,3},{3,2},{4,5},{5,4},{6,7},{7,6},{8,9},{9,8},{10,11... | collective-permute-start | bytes 442376 | tf_op jit(solution)/shard_map/ppermute | solution.py:318
  4.4 10.5 %collective-permute-start.3 = (bf16[64,128]{1,0:T(8,128)(2,1)S(1)}, bf16[64,128]{1,0:T(8,128)(2,1)S(1)}, u32[]{:S(2)}, u32[]{:S(2)}) collective-permute-start(bf16[64,128]{1,0:T(8,128)(2,1)S(1)} %pad_maximum_fusion.8), channel_id=1, source_target_pairs={{0,4},{1,5},{2,6},{3,7},{4,0},{5,1},{6,2},{7,3},{8,12},{9,13},{10,... | collective-permute-start | bytes 49160 | tf_op jit(solution)/shard_map/ppermute | solution.py:340
  7.4 7.6 %collective-permute-start.4 = (bf16[64,128]{1,0:T(8,128)(2,1)S(1)}, bf16[64,128]{1,0:T(8,128)(2,1)S(1)}, u32[]{:S(2)}, u32[]{:S(2)}) collective-permute-start(bf16[64,128]{1,0:T(8,128)(2,1)S(1)} %pad_maximum_fusion.9), channel_id=1, source_target_pairs={{0,1},{1,0},{2,3},{3,2},{4,8},{5,9},{6,10},{7,11},{8,4},{9,5},{10,... | collective-permute-start | bytes 49160 | tf_op jit(solution)/shard_map/ppermute | solution.py:341
  7.5 7.5 %collective-permute-start.2 = (bf16[96,384]{1,0:T(8,128)(2,1)S(1)}, bf16[96,384]{1,0:T(8,128)(2,1)S(1)}, u32[]{:S(2)}, u32[]{:S(2)}) collective-permute-start(bf16[96,384]{1,0:T(8,128)(2,1)S(1)} %get-tuple-element.59), channel_id=1, source_target_pairs={{0,1},{1,0},{2,4},{3,5},{4,2},{5,3},{6,8},{7,9},{8,6},{9,7},{10,12... | collective-permute-start | bytes 221192 | tf_op jit(solution)/shard_map/ppermute | solution.py:339
  8.0 7.0 %collective-permute-start.1 = (bf16[96,384]{1,0:T(8,128)(2,1)S(1)}, bf16[96,384]{1,0:T(8,128)(2,1)S(1)}, u32[]{:S(2)}, u32[]{:S(2)}) collective-permute-start(bf16[96,384]{1,0:T(8,128)(2,1)S(1)} %get-tuple-element.60), channel_id=1, source_target_pairs={{0,2},{1,3},{2,0},{3,1},{4,6},{5,7},{6,4},{7,5},{8,10},{9,11},{10,... | collective-permute-start | bytes 221192 | tf_op jit(solution)/shard_map/ppermute | solution.py:338
  16.8 1.4 %collective-permute-start.5 = (bf16[192,384]{1,0:T(8,128)(2,1)S(1)}, bf16[192,384]{1,0:T(8,128)(2,1)S(1)}, u32[]{:S(2)}, u32[]{:S(2)}) collective-permute-start(bf16[192,384]{1,0:T(8,128)(2,1)S(1)} %get-tuple-element.45), channel_id=1, source_target_pairs={{0,1},{1,0},{2,3},{3,2},{4,5},{5,4},{6,7},{7,6},{8,9},{9,8},{10,11... | collective-permute-start | bytes 442376 | tf_op jit(solution)/shard_map/ppermute | solution.py:318
  18.3 7.0 %collective-permute-start.8 = (bf16[64,128]{1,0:T(8,128)(2,1)S(1)}, bf16[64,128]{1,0:T(8,128)(2,1)S(1)}, u32[]{:S(2)}, u32[]{:S(2)}) collective-permute-start(bf16[64,128]{1,0:T(8,128)(2,1)S(1)} %pad_maximum_fusion.10), channel_id=1, source_target_pairs={{0,4},{1,5},{2,6},{3,7},{4,0},{5,1},{6,2},{7,3},{8,12},{9,13},{10,... | collective-permute-start | bytes 49160 | tf_op jit(solution)/shard_map/ppermute | solution.py:340
  19.8 5.4 %collective-permute-start.9 = (bf16[64,128]{1,0:T(8,128)(2,1)S(1)}, bf16[64,128]{1,0:T(8,128)(2,1)S(1)}, u32[]{:S(2)}, u32[]{:S(2)}) collective-permute-start(bf16[64,128]{1,0:T(8,128)(2,1)S(1)} %pad_maximum_fusion.11), channel_id=1, source_target_pairs={{0,1},{1,0},{2,3},{3,2},{4,8},{5,9},{6,10},{7,11},{8,4},{9,5},{10,... | collective-permute-start | bytes 49160 | tf_op jit(solution)/shard_map/ppermute | solution.py:341
  19.8 5.4 %collective-permute-start.7 = (bf16[96,384]{1,0:T(8,128)(2,1)S(1)}, bf16[96,384]{1,0:T(8,128)(2,1)S(1)}, u32[]{:S(2)}, u32[]{:S(2)}) collective-permute-start(bf16[96,384]{1,0:T(8,128)(2,1)S(1)} %get-tuple-element.57), channel_id=1, source_target_pairs={{0,1},{1,0},{2,4},{3,5},{4,2},{5,3},{6,8},{7,9},{8,6},{9,7},{10,12... | collective-permute-start | bytes 221192 | tf_op jit(solution)/shard_map/ppermute | solution.py:339
  20.4 5.3 %collective-permute-start.6 = (bf16[96,384]{1,0:T(8,128)(2,1)S(1)}, bf16[96,384]{1,0:T(8,128)(2,1)S(1)}, u32[]{:S(2)}, u32[]{:S(2)}) collective-permute-start(bf16[96,384]{1,0:T(8,128)(2,1)S(1)} %get-tuple-element.58), channel_id=1, source_target_pairs={{0,2},{1,3},{2,0},{3,1},{4,6},{5,7},{6,4},{7,5},{8,10},{9,11},{10,... | collective-permute-start | bytes 221192 | tf_op jit(solution)/shard_map/ppermute | solution.py:338

commit v3 on v2

--- a/solution.py
+++ b/solution.py
@@ -62,7 +62,7 @@
     return transposed(jnp.concatenate(rows, axis=0))
 
 
-def send(traces, source_hot, column, projection, first_out, own_out, blocks):
+def send(traces, source_hot, column, projection, first_out, rim_out, own_out, blocks):
     elements, width = traces.shape
     slots = column.shape[0]
     capacity = slots // 8
@@ -95,8 +95,8 @@
     final_at = pl.multiple_of(pick(core, elements - rim, 0), rim)
     other_at = pl.multiple_of(pick(core, 0, elements - rim), rim)
     first_out[0:rim, :] = traces[pl.ds(final_at, rim), :]
-    first_out[rim : 2 * rim, :] = traces[pl.ds(other_at, rim), :]
-    at = 2 * rim
+    rim_out[...] = traces[pl.ds(other_at, rim), :]
+    at = rim
     for t, (a, b) in enumerate(((4, 3), (6, 4), (3, 1))):
         first_out[at : at + capacity, 128 * t : 128 * t + 128] = block(pick(core, a, b))
     at += capacity
@@ -108,7 +108,7 @@
 
 def start_kernel(
     state_in, trace_map_in, records_in, counts_in, velocity_in, levels_in, neighbours_in, projection_in,
-    trace_map, projection, traces, first_out, own_out, source_hot, column, elements_column,
+    trace_map, projection, traces, first_out, rim_out, own_out, source_hot, column, elements_column,
     state, records, counts, velocity, levels, neighbours, blocks, sems
 ):
     elements = state.shape[0]
@@ -133,7 +133,7 @@
         copies[1 + i].wait()
         cut = slice(i * part, i * part + part)
         traces[cut, :] = dot(state[cut, :].astype(bf16), trace_map[...]).astype(bf16)
-    send(traces, source_hot[...], column, projection, first_out, own_out, blocks)
+    send(traces, source_hot[...], column, projection, first_out, rim_out, own_out, blocks)
 
 
 def element_columns(velocity, levels, neighbours):
@@ -205,25 +205,21 @@
     own_part(columns, traces, partial)
 
 
-def gather_arrivals(got, got_even, got_odd, got_a, got_b, arrived):
+def gather_arrivals(got, got_rim, got_even, got_odd, got_a, got_b, arrived):
     capacity = arrived.shape[0] // 8
     rim = 2 * capacity
-    at = 2 * rim
     chip, core = place()
-    own = lax.rem(chip, 2)
     second = lax.rem(lax.div(chip, 2), 2)
-    arrived[0:capacity, :] = got[at : at + capacity, 0:128]
+    arrived[0:capacity, :] = got[rim : rim + capacity, 0:128]
     for i, ref in enumerate((got_even, got_odd)):
-        for k in range(2):
-            to = capacity * (1 + 2 * i + k)
-            arrived[to : to + capacity, :] = ref[rim : rim + capacity, 128 * k : 128 * k + 128]
+        to = capacity * (1 + 2 * i)
+        arrived[to : to + 2 * capacity, :] = ref[...]
     arrived[5 * capacity : 6 * capacity, :] = got_a[0:capacity, :]
     arrived[6 * capacity : 7 * capacity, :] = got_b[0:capacity, :]
     arrived[7 * capacity :, :] = jnp.where(
         second != core, got_a[capacity : 2 * capacity, :], got_b[capacity : 2 * capacity, :]
     )
-    forward = jnp.where(own != core, got_even[0:rim, :], got_odd[0:rim, :])
-    return jnp.concatenate([got[0:rim, :], forward], axis=0)
+    return jnp.concatenate([got[0:rim, :], got_rim[...]], axis=0)
 
 
 def targets(pieces, elements):
@@ -251,11 +247,11 @@
 
 
 def middle_kernel(
-    lift, base, partial, inflow, picks, got, got_even, got_odd, got_a, got_b, trace_map, projection, source_hot, column,
-    field, traces, first_out, own_out, face_out, element_hot_out, arrived, blocks
+    lift, base, partial, inflow, picks, got, got_rim, got_even, got_odd, got_a, got_b, trace_map, projection, source_hot, column,
+    field, traces, first_out, rim_out, own_out, face_out, element_hot_out, arrived, blocks
 ):
     elements = base.shape[0]
-    window = gather_arrivals(got, got_even, got_odd, got_a, got_b, arrived)
+    window = gather_arrivals(got, got_rim, got_even, got_odd, got_a, got_b, arrived)
     pieces = arrived[...]
     face, element_hot = targets(pieces, elements)
     face_out[...] = face
@@ -264,14 +260,14 @@
     new = base[...] + time_step * dot(flux, lift[...])
     field[...] = new
     traces[...] = dot(new.astype(bf16), trace_map[...]).astype(bf16)
-    send(traces, source_hot[...], column, projection, first_out, own_out, blocks)
+    send(traces, source_hot[...], column, projection, first_out, rim_out, own_out, blocks)
 
 
 def end_kernel(
-    lift, base, partial, inflow, picks, got, got_even, got_odd, got_a, got_b, face, element_hot, field, arrived, result, sems
+    lift, base, partial, inflow, picks, got, got_rim, got_even, got_odd, got_a, got_b, face, element_hot, field, arrived, result, sems
 ):
     elements = base.shape[0]
-    window = gather_arrivals(got, got_even, got_odd, got_a, got_b, arrived)
+    window = gather_arrivals(got, got_rim, got_even, got_odd, got_a, got_b, arrived)
     flux = fluxes(arrived[...], face[...], element_hot[...], window, partial, inflow, picks)
     part = elements // 2
     copies = []
@@ -313,33 +309,34 @@
     )(*operands)
 
 
-def exchange(first, own, chip, core, rim, capacity):
+def exchange(first, rim, own, chip, core):
     count = lax.axis_size(CURVE)
+    groups = lax.axis_size("groups")
+    capacity = own.shape[0] // 4
+    border = [(s, s ^ 1) for s in range(groups) if s ^ 1 < groups]
+    to_next = [(g * count + s, g * count + s + 1) for g in range(groups) for s in range(1, count - 1, 2)]
+    to_next += [(b, a) for a, b in to_next]
+    to_next += [(a * count + s, b * count + s) for a, b in border for s in (0, count - 1)]
     got = lax.ppermute(first, CURVE, paired(count, 1, lambda s: s % 2 == 0))
-    forward = got[rim : 2 * rim]
-    at = 2 * rim
+    got_rim = lax.ppermute(rim, ("groups",) + CURVE, sorted(to_next))
+    at = rim.shape[0]
     up = got[at : at + capacity, 128:256]
     down = got[at : at + capacity, 256:384]
     far = got[at + capacity : at + 2 * capacity, 0:128]
-    blank = jnp.zeros_like(up)
     even = chip % 2 == 0
     upper = ((chip // 2) % 2 == 0) == (core == 0)
-    mine = [own[capacity * t : capacity * t + capacity] for t in range(4)]
-
-    def near(block, other):
-        return jnp.concatenate([forward, jnp.concatenate([block, other, blank], axis=1)], axis=0)
-
-    to_even = near(mine[0], jnp.where(even, up, down))
-    to_odd = near(mine[1], jnp.where(even, down, up))
-    to_a = jnp.concatenate([mine[2], jnp.where(upper, far, 0)], axis=0)
-    to_b = jnp.concatenate([mine[3], jnp.where(upper, 0, far)], axis=0)
-    return (
-        got,
-        lax.ppermute(to_even, CURVE, paired(count, 2, lambda s: (s // 2) % 2 == 0)),
-        lax.ppermute(to_odd, CURVE, paired(count, 2, lambda s: (s // 2) % 2 == 1)),
-        lax.ppermute(to_a, CURVE, paired(count, 4, lambda s: (s // 4) % 2 == 0)),
-        lax.ppermute(to_b, CURVE, paired(count, 4, lambda s: (s // 4) % 2 == 1)),
-    )
+    others = (jnp.where(even, up, down), jnp.where(even, down, up), jnp.where(upper, far, 0), jnp.where(upper, 0, far))
+    swaps = [
+        paired(count, 2, lambda s: (s // 2) % 2 == 0),
+        paired(count, 2, lambda s: (s // 2) % 2 == 1),
+        paired(count, 4, lambda s: (s // 4) % 2 == 0),
+        paired(count, 4, lambda s: (s // 4) % 2 == 1),
+    ]
+    swapped_blocks = []
+    for t, (other, pairs) in enumerate(zip(others, swaps)):
+        block = jnp.concatenate([own[capacity * t : capacity * t + capacity], other], axis=0)
+        swapped_blocks.append(lax.ppermute(block, CURVE, pairs))
+    return got, got_rim, *swapped_blocks
 
 
 def body(
@@ -360,7 +357,8 @@
 
     sent = [
         array((elements, width), bf16),
-        array((2 * rim + 2 * capacity, width), bf16),
+        array((rim + 2 * capacity, width), bf16),
+        array((rim, width), bf16),
         array((4 * capacity, 128), bf16),
     ]
     whole = array((elements, modes), f32)
@@ -371,7 +369,7 @@
     levels = levels.reshape(1, elements)
     vmem = pltpu.VMEM
     wide = (elements, 128)
-    trace_map, projection, traces, first, own, source_hot, column, element_column = call(
+    trace_map, projection, traces, first, rims, own, source_hot, column, element_column = call(
         start_kernel,
         [like(trace_map), like(projection)]
         + sent
@@ -382,7 +380,7 @@
         (state, trace_map, records, counts, velocity, levels, neighbours, projection),
         (),
     )
-    got = exchange(first, own, chip, core, rim, capacity)
+    got = exchange(first, rims, own, chip, core)
     stiffness, lift, base, partial, inflow, picks = call(
         local_kernel,
         [like(stiffness), like(lift), whole, faces, faces, array((elements, 12 * rim), bf16)],
@@ -391,7 +389,7 @@
         (stiffness, lift),
         (element_column, state, traces),
     )
-    field, traces, first, own, face, element_hot = call(
+    field, traces, first, rims, own, face, element_hot = call(
         middle_kernel,
         [whole] + sent + [column_shape, array((elements, slots), bf16)],
         [blocks, blocks],
@@ -399,7 +397,7 @@
         (),
         (lift, base, partial, inflow, picks, *got, trace_map, projection, source_hot, column),
     )
-    got = exchange(first, own, chip, core, rim, capacity)
+    got = exchange(first, rims, own, chip, core)
     base, partial = call(
         second_local_kernel, [whole, faces], [], 3 * 10**9, (), (element_column, state, field, stiffness, traces)
     )

time: 27.8 us -> 26.4 us (0.950)
  waiting for transfers between devices: 2.83 us -> 1.52 us
  starting transfers between devices: 13.2 us -> 12.9 us
    ppermute x2, waiting for transfers between devices: 2.35 us -> 1.22 us  [exchange(): got = lax.ppermute(first, CURVE, paired(count, 1, lambda s: s % 2 == 0))]
    ppermute x8 -> x10, starting transfers between devices: 12.7 us -> 12.3 us  [the longest x8 8 us: exchange(): swapped_blocks.append(lax.ppermute(block, CURVE, pairs))]
  transfers between devices with their start and end apart: 10 -> 12, of which waited for: 3 -> 2; matrix products, arithmetic and copies ran while one was open for 0% -> 0% of each run, Pallas kernels for 17% -> 18%
where the time goes in v3:
time: 26.4 us; the launch traced here: 26 us
  starting transfers between devices  12.9 us (49%)
  Pallas kernels  11.4 us (43%)
  waiting for transfers between devices  1.52 us (6%)
    pallas_call x5, Pallas kernels, call(): pl.pallas_call(kernel, out_shape=out_shape, in_specs=specs, out_specs=[pl...  11.4 us
    ppermute x8, starting transfers between devices, exchange(): swapped_blocks.append(lax.ppermute(block, CURVE, pairs))  8 us
    ppermute x2, starting transfers between devices, exchange(): got_rim = lax.ppermute(rim, ('groups',) + CURVE, sorted(to_next))  4.29 us
    ppermute x2, waiting for transfers between devices, exchange(): got = lax.ppermute(first, CURVE, paired(count, 1, lambda s: s % 2 == 0))  1.22 us
    ppermute x2, starting transfers between devices, exchange(): got = lax.ppermute(first, CURVE, paired(count, 1, lambda s: s % 2 == 0))  0.65 us
  transfers between devices with their start and end apart: 12, of which 2 were waited for; matrix products, arithmetic and copies ran while one was open for 0% of the time, Pallas kernels for 18%

profile of v3, /device:TPU:0, one launch (start us, length us, event | category | flops | bytes accessed | tf_op | source)
XLA Modules:
  0.0 26.0 jit_solution(17838749988648738812)
XLA Ops:
  0.0 2.9 %shard_map.100 = (bf16[512,384]{1,0:T(8,128)(2,1)S(1)}, bf16[64,512]{1,0:T(8,128)(2,1)S(1)}, bf16[512,384]{1,0:T(8,128)(2,1)S(1)}, bf16[128,384]{1,0:T(8,128)(2,...) custom-call(f32[512,512]{1,0:T(8,128)} %state.3, ...), custom_call_target="tpu_custom_call" | custom-call | flops 200000000 | bytes 1531936 | tf_op jit(solution)/shard_map/pallas_call | solution.py:301
  2.9 3.0 %collective-permute-start.1 = (bf16[64,384]{1,0:T(8,128)(2,1)S(1)}, bf16[64,384]{1,0:T(8,128)(2,1)S(1)}, u32[]{:S(2)}, u32[]{:S(2)}) collective-permute-start(bf16[64,384]{1,0:T(8,128)(2,1)S(1)} %get-tuple-element.37), channel_id=1, source_target_pairs={{0,16},{1,2},{2,1},{3,4},{4,3},{5,6},{6,5},{7,8},{8,7},{9,10},{10,... | collective-permute-start | bytes 147464 | tf_op jit(solution)/shard_map/ppermute | solution.py:321
  5.9 0.1 collective-permute-start
  6.0 1.2 %collective-permute-done.got = bf16[128,384]{1,0:T(8,128)(2,1)S(1)} collective-permute-done((bf16[128,384]{1,0:T(8,128)(2,1)S(1)}, bf16[128,384]{1,0:T(8,128)(2,1)S(1)}, u32[]{:S(2)}, u32[]{:S(2)}) %collective-permute-start) | collective-permute-done | bytes 98336 | tf_op jit(solution)/shard_map/ppermute | solution.py:320
  7.2 1.4 %collective-permute-start.4 = (bf16[64,128]{1,0:T(8,128)(2,1)S(1)}, bf16[64,128]{1,0:T(8,128)(2,1)S(1)}, u32[]{:S(2)}, u32[]{:S(2)}) collective-permute-start(bf16[64,128]{1,0:T(8,128)(2,1)S(1)} %pad_maximum_fusion.2), channel_id=1, source_target_pairs={{0,4},{1,5},{2,6},{3,7},{4,0},{5,1},{6,2},{7,3},{8,12},{9,13},{10,... | collective-permute-start | bytes 49160 | tf_op jit(solution)/shard_map/ppermute | solution.py:338
  8.6 0.1 collective-permute-start.3
  8.7 2.1 %collective-permute-start.2 = (bf16[64,128]{1,0:T(8,128)(2,1)S(1)}, bf16[64,128]{1,0:T(8,128)(2,1)S(1)}, u32[]{:S(2)}, u32[]{:S(2)}) collective-permute-start(bf16[64,128]{1,0:T(8,128)(2,1)S(1)} %pad_maximum_fusion), channel_id=1, source_target_pairs={{0,2},{1,3},{2,0},{3,1},{4,6},{5,7},{6,4},{7,5},{8,10},{9,11},{10,... | collective-permute-start | bytes 49160 | tf_op jit(solution)/shard_map/ppermute | solution.py:338
  10.8 0.0 collective-permute-start.5
  10.8 2.8 %shard_map.101 = (bf16[512,1536]{1,0:T(8,128)(2,1)S(1)}, bf16[384,512]{1,0:T(8,128)(2,1)S(1)}, f32[512,512]{1,0:T(8,128)S(1)}, f32[512,384]{1,0:T(8,128)S(1)}, f...) custom-call(bf16[512,1536]{1,0:T(8,128)(2,1)} %stiffness_in.1, bf16[384,512]{1,0:T(8,128)(2,1)} %lift_in.1, ...), custom_call_target="tpu_custom_call" | custom-call | flops 3000000000 | bytes 3670016 | tf_op jit(solution)/shard_map/pallas_call | solution.py:301
  13.6 0.0 collective-permute-done.1.got_rim
  13.6 0.0 collective-permute-done.3.got_odd
  13.6 0.0 collective-permute-done.2.got_even
  13.7 1.8 %shard_map.102 = (f32[512,512]{1,0:T(8,128)S(1)}, bf16[512,384]{1,0:T(8,128)(2,1)S(1)}, bf16[128,384]{1,0:T(8,128)(2,1)S(1)}, bf16[64,384]{1,0:T(8,128)(2,1)S(1)...) custom-call(bf16[384,512]{1,0:T(8,128)(2,1)S(1)} %get-tuple-element.31.lift, ...), custom_call_target="tpu_custom_call" | custom-call | flops 1000000000 | bytes 4866048 | tf_op jit(solution)/shard_map/pallas_call | solution.py:301
  15.5 0.6 %collective-permute-start.6 = (bf16[128,384]{1,0:T(8,128)(2,1)S(1)}, bf16[128,384]{1,0:T(8,128)(2,1)S(1)}, u32[]{:S(2)}, u32[]{:S(2)}) collective-permute-start(bf16[128,384]{1,0:T(8,128)(2,1)S(1)} %get-tuple-element.48), channel_id=1, source_target_pairs={{0,1},{1,0},{2,3},{3,2},{4,5},{5,4},{6,7},{7,6},{8,9},{9,8},{10,11... | collective-permute-start | bytes 294920 | tf_op jit(solution)/shard_map/ppermute | solution.py:320
  16.1 1.3 %collective-permute-start.7 = (bf16[64,384]{1,0:T(8,128)(2,1)S(1)}, bf16[64,384]{1,0:T(8,128)(2,1)S(1)}, u32[]{:S(2)}, u32[]{:S(2)}) collective-permute-start(bf16[64,384]{1,0:T(8,128)(2,1)S(1)} %get-tuple-element.49), channel_id=1, source_target_pairs={{0,16},{1,2},{2,1},{3,4},{4,3},{5,6},{6,5},{7,8},{8,7},{9,10},{10,... | collective-permute-start | bytes 147464 | tf_op jit(solution)/shard_map/ppermute | solution.py:321
  17.3 2.9 %collective-permute-start.10 = (bf16[64,128]{1,0:T(8,128)(2,1)S(1)}, bf16[64,128]{1,0:T(8,128)(2,1)S(1)}, u32[]{:S(2)}, u32[]{:S(2)}) collective-permute-start(bf16[64,128]{1,0:T(8,128)(2,1)S(1)} %pad_maximum_fusion.6), channel_id=1, source_target_pairs={{0,4},{1,5},{2,6},{3,7},{4,0},{5,1},{6,2},{7,3},{8,12},{9,13},{10,... | collective-permute-start | bytes 49160 | tf_op jit(solution)/shard_map/ppermute | solution.py:338
  20.2 0.0 collective-permute-start.9
  20.2 1.5 %collective-permute-start.8 = (bf16[64,128]{1,0:T(8,128)(2,1)S(1)}, bf16[64,128]{1,0:T(8,128)(2,1)S(1)}, u32[]{:S(2)}, u32[]{:S(2)}) collective-permute-start(bf16[64,128]{1,0:T(8,128)(2,1)S(1)} %pad_maximum_fusion.4), channel_id=1, source_target_pairs={{0,2},{1,3},{2,0},{3,1},{4,6},{5,7},{6,4},{7,5},{8,10},{9,11},{10,... | collective-permute-start | bytes 49160 | tf_op jit(solution)/shard_map/ppermute | solution.py:338
  21.8 0.0 collective-permute-start.11
  21.8 1.9 %shard_map.103 = (f32[512,512]{1,0:T(8,128)S(1)}, f32[512,384]{1,0:T(8,128)S(1)}) custom-call(f32[512,128]{1,0:T(8,128)S(1)} %get-tuple-element.29.column, f32[512,512]{1,0:T(8,128)S(1)} %copy-done, f32[512,512]{1,0:T(8,128)S(1)} %get-tuple-element.43.field, bf16[512,1536]{1,0:T(8,128)(2,1)S(1)} %get-tuple-element.44.stiffness, ...), custom_call_target="tpu_custom_call" | custom-call | flops 3000000000 | bytes 4325376 | tf_op jit(solution)/shard_map/pallas_call | solution.py:301
  23.7 0.0 collective-permute-done.7.got_rim
  23.8 0.0 collective-permute-done.9.got_odd
  23.8 0.3 %collective-permute-done.8.got_even = bf16[64,128]{1,0:T(8,128)(2,1)S(1)} collective-permute-done((bf16[64,128]{1,0:T(8,128)(2,1)S(1)}, bf16[64,128]{1,0:T(8,128)(2,1)S(1)}, u32[]{:S(2)}, u32[]{:S(2)}) %collective-permute-start.8) | collective-permute-done | bytes 16416 | tf_op jit(solution)/shard_map/ppermute | solution.py:338
  24.1 2.0 %shard_map.104 = f32[512,512]{1,0:T(8,128)} custom-call(bf16[384,512]{1,0:T(8,128)(2,1)S(1)} %get-tuple-element.31.lift, f32[512,512]{1,0:T(8,128)S(1)} %get-tuple-element.46.base, f32[512,384]{1,0:T(8,128)S(1)} %get-tuple-element.47.partial, f32[512,384]{1,0:T(8,128)S(1)} %get-tuple-element.34.inflow, bf16[512,768]{1,0:T(8,128)(2,1)S(1)} %get-tuple-element.35.picks, ...), custom_call_target="tpu_custom_call" | custom-call | flops 1000000000 | bytes 4407296 | tf_op jit(solution)/shard_map/pallas_call | solution.py:301
  (19 shorter events, 0.1 us)
Async XLA Ops:
  0.0 10.8 %copy-start = (f32[512,512]{1,0:T(8,128)S(1)}, f32[512,512]{1,0:T(8,128)}, u32[]{:S(2)}) copy-start(f32[512,512]{1,0:T(8,128)} %state.3) | copy-start | bytes 3145732
  2.9 10.7 %collective-permute-start.1 = (bf16[64,384]{1,0:T(8,128)(2,1)S(1)}, bf16[64,384]{1,0:T(8,128)(2,1)S(1)}, u32[]{:S(2)}, u32[]{:S(2)}) collective-permute-start(bf16[64,384]{1,0:T(8,128)(2,1)S(1)} %get-tuple-element.37), channel_id=1, source_target_pairs={{0,16},{1,2},{2,1},{3,4},{4,3},{5,6},{6,5},{7,8},{8,7},{9,10},{10,... | collective-permute-start | bytes 147464 | tf_op jit(solution)/shard_map/ppermute | solution.py:321
  5.9 1.3 %collective-permute-start = (bf16[128,384]{1,0:T(8,128)(2,1)S(1)}, bf16[128,384]{1,0:T(8,128)(2,1)S(1)}, u32[]{:S(2)}, u32[]{:S(2)}) collective-permute-start(bf16[128,384]{1,0:T(8,128)(2,1)S(1)} %get-tuple-element.36), channel_id=1, source_target_pairs={{0,1},{1,0},{2,3},{3,2},{4,5},{5,4},{6,7},{7,6},{8,9},{9,8},{10,11... | collective-permute-start | bytes 294920 | tf_op jit(solution)/shard_map/ppermute | solution.py:320
  7.2 6.4 %collective-permute-start.4 = (bf16[64,128]{1,0:T(8,128)(2,1)S(1)}, bf16[64,128]{1,0:T(8,128)(2,1)S(1)}, u32[]{:S(2)}, u32[]{:S(2)}) collective-permute-start(bf16[64,128]{1,0:T(8,128)(2,1)S(1)} %pad_maximum_fusion.2), channel_id=1, source_target_pairs={{0,4},{1,5},{2,6},{3,7},{4,0},{5,1},{6,2},{7,3},{8,12},{9,13},{10,... | collective-permute-start | bytes 49160 | tf_op jit(solution)/shard_map/ppermute | solution.py:338
  8.6 5.0 %collective-permute-start.3 = (bf16[64,128]{1,0:T(8,128)(2,1)S(1)}, bf16[64,128]{1,0:T(8,128)(2,1)S(1)}, u32[]{:S(2)}, u32[]{:S(2)}) collective-permute-start(bf16[64,128]{1,0:T(8,128)(2,1)S(1)} %pad_maximum_fusion.1), channel_id=1, source_target_pairs={{0,1},{1,0},{2,4},{3,5},{4,2},{5,3},{6,8},{7,9},{8,6},{9,7},{10,12... | collective-permute-start | bytes 49160 | tf_op jit(solution)/shard_map/ppermute | solution.py:338
  8.7 5.0 %collective-permute-start.2 = (bf16[64,128]{1,0:T(8,128)(2,1)S(1)}, bf16[64,128]{1,0:T(8,128)(2,1)S(1)}, u32[]{:S(2)}, u32[]{:S(2)}) collective-permute-start(bf16[64,128]{1,0:T(8,128)(2,1)S(1)} %pad_maximum_fusion), channel_id=1, source_target_pairs={{0,2},{1,3},{2,0},{3,1},{4,6},{5,7},{6,4},{7,5},{8,10},{9,11},{10,... | collective-permute-start | bytes 49160 | tf_op jit(solution)/shard_map/ppermute | solution.py:338
  10.8 2.9 %collective-permute-start.5 = (bf16[64,128]{1,0:T(8,128)(2,1)S(1)}, bf16[64,128]{1,0:T(8,128)(2,1)S(1)}, u32[]{:S(2)}, u32[]{:S(2)}) collective-permute-start(bf16[64,128]{1,0:T(8,128)(2,1)S(1)} %pad_maximum_fusion.3), channel_id=1, source_target_pairs={{0,1},{1,0},{2,3},{3,2},{4,8},{5,9},{6,10},{7,11},{8,4},{9,5},{10,... | collective-permute-start | bytes 49160 | tf_op jit(solution)/shard_map/ppermute | solution.py:338
  15.5 1.8 %collective-permute-start.6 = (bf16[128,384]{1,0:T(8,128)(2,1)S(1)}, bf16[128,384]{1,0:T(8,128)(2,1)S(1)}, u32[]{:S(2)}, u32[]{:S(2)}) collective-permute-start(bf16[128,384]{1,0:T(8,128)(2,1)S(1)} %get-tuple-element.48), channel_id=1, source_target_pairs={{0,1},{1,0},{2,3},{3,2},{4,5},{5,4},{6,7},{7,6},{8,9},{9,8},{10,11... | collective-permute-start | bytes 294920 | tf_op jit(solution)/shard_map/ppermute | solution.py:320
  16.1 7.7 %collective-permute-start.7 = (bf16[64,384]{1,0:T(8,128)(2,1)S(1)}, bf16[64,384]{1,0:T(8,128)(2,1)S(1)}, u32[]{:S(2)}, u32[]{:S(2)}) collective-permute-start(bf16[64,384]{1,0:T(8,128)(2,1)S(1)} %get-tuple-element.49), channel_id=1, source_target_pairs={{0,16},{1,2},{2,1},{3,4},{4,3},{5,6},{6,5},{7,8},{8,7},{9,10},{10,... | collective-permute-start | bytes 147464 | tf_op jit(solution)/shard_map/ppermute | solution.py:321
  17.3 6.4 %collective-permute-start.10 = (bf16[64,128]{1,0:T(8,128)(2,1)S(1)}, bf16[64,128]{1,0:T(8,128)(2,1)S(1)}, u32[]{:S(2)}, u32[]{:S(2)}) collective-permute-start(bf16[64,128]{1,0:T(8,128)(2,1)S(1)} %pad_maximum_fusion.6), channel_id=1, source_target_pairs={{0,4},{1,5},{2,6},{3,7},{4,0},{5,1},{6,2},{7,3},{8,12},{9,13},{10,... | collective-permute-start | bytes 49160 | tf_op jit(solution)/shard_map/ppermute | solution.py:338
  20.2 3.5 %collective-permute-start.9 = (bf16[64,128]{1,0:T(8,128)(2,1)S(1)}, bf16[64,128]{1,0:T(8,128)(2,1)S(1)}, u32[]{:S(2)}, u32[]{:S(2)}) collective-permute-start(bf16[64,128]{1,0:T(8,128)(2,1)S(1)} %pad_maximum_fusion.5), channel_id=1, source_target_pairs={{0,1},{1,0},{2,4},{3,5},{4,2},{5,3},{6,8},{7,9},{8,6},{9,7},{10,12... | collective-permute-start | bytes 49160 | tf_op jit(solution)/shard_map/ppermute | solution.py:338
  20.2 3.8 %collective-permute-start.8 = (bf16[64,128]{1,0:T(8,128)(2,1)S(1)}, bf16[64,128]{1,0:T(8,128)(2,1)S(1)}, u32[]{:S(2)}, u32[]{:S(2)}) collective-permute-start(bf16[64,128]{1,0:T(8,128)(2,1)S(1)} %pad_maximum_fusion.4), channel_id=1, source_target_pairs={{0,2},{1,3},{2,0},{3,1},{4,6},{5,7},{6,4},{7,5},{8,10},{9,11},{10,... | collective-permute-start | bytes 49160 | tf_op jit(solution)/shard_map/ppermute | solution.py:338
  21.8 2.3 %collective-permute-start.11 = (bf16[64,128]{1,0:T(8,128)(2,1)S(1)}, bf16[64,128]{1,0:T(8,128)(2,1)S(1)}, u32[]{:S(2)}, u32[]{:S(2)}) collective-permute-start(bf16[64,128]{1,0:T(8,128)(2,1)S(1)} %pad_maximum_fusion.7), channel_id=1, source_target_pairs={{0,1},{1,0},{2,3},{3,2},{4,8},{5,9},{6,10},{7,11},{8,4},{9,5},{10,... | collective-permute-start | bytes 49160 | tf_op jit(solution)/shard_map/ppermute | solution.py:338

commit v4 on v2

--- a/solution.py
+++ b/solution.py
@@ -68,8 +68,8 @@
     capacity = slots // 8
     rim = elements // 8
     chip, core = place()
-    own = lax.rem(chip, 2)
-    second = lax.rem(lax.div(chip, 2), 2)
+    near_up = 1 - jnp.bitwise_xor(core, lax.rem(chip, 2))
+    far_up = 1 - jnp.bitwise_xor(core, lax.rem(lax.div(chip, 2), 2))
     shape = (slots, 128)
     lane = lanes(shape)
     half = jnp.where(lane < 64, 0.0, 1.0)
@@ -84,26 +84,28 @@
     for t in range(4):
         folded = jnp.where(half + 2 * t == kind, every[:, 128 * t : 128 * t + 128], folded)
     piece = folded + pltpu.roll(folded, 64, 1)
-    blocks[...] = jnp.where(lane < 64, piece, column[...]).astype(bf16)
+    nothing = jnp.zeros((capacity, 128), bf16)
+    blocks[0:capacity, :] = nothing
+    blocks[capacity : capacity + slots, :] = jnp.where(lane < 64, piece, column[...]).astype(bf16)
+    blocks[capacity + slots :, :] = nothing
 
     def block(index):
-        return blocks[pl.ds(pl.multiple_of(index * capacity, capacity), capacity), :]
-
-    def pick(which, a, b):
-        return a + which * (b - a)
-
-    final_at = pl.multiple_of(pick(core, elements - rim, 0), rim)
-    other_at = pl.multiple_of(pick(core, 0, elements - rim), rim)
-    first_out[0:rim, :] = traces[pl.ds(final_at, rim), :]
-    first_out[rim : 2 * rim, :] = traces[pl.ds(other_at, rim), :]
-    at = 2 * rim
-    for t, (a, b) in enumerate(((4, 3), (6, 4), (3, 1))):
-        first_out[at : at + capacity, 128 * t : 128 * t + 128] = block(pick(core, a, b))
-    at += capacity
-    first_out[at : at + capacity, 0:128] = block(pick(core, 1, 6))
-    first_out[at : at + capacity, 128:] = jnp.zeros((capacity, width - 128), bf16)
-    for t, (which, a, b) in enumerate(((own, 5, 2), (own, 2, 5), (second, 7, 0), (second, 0, 7))):
-        own_out[capacity * t : capacity * t + capacity, :] = block(pick(which, a, b))
+        return blocks[pl.ds(pl.multiple_of((index + 1) * capacity, capacity), capacity), :]
+
+    final_at = pl.multiple_of((1 - core) * (elements - rim), rim)
+    other_at = pl.multiple_of(core * (elements - rim), rim)
+    for t in range(3):
+        cut = slice(128 * t, 128 * t + 128)
+        first_out[rim * t : rim * t + rim, :] = traces[pl.ds(final_at, rim), cut]
+        first_out[rim * (3 + t) : rim * (4 + t), :] = traces[pl.ds(other_at, rim), cut]
+    at = 6 * rim
+    inside = 4 - core
+    here = [2 + 3 * near_up - core, 3 + 3 * near_up - core, 7 * far_up - core, 1 + 7 * far_up - core]
+    there = [5 - 3 * near_up - core, 6 - 3 * near_up - core, 7 - 7 * far_up - core, 8 - 7 * far_up - core]
+    for i, index in enumerate([inside] + there):
+        first_out[at + capacity * i : at + capacity * i + capacity, :] = block(index)
+    for i, index in enumerate(here):
+        own_out[capacity * i : capacity * i + capacity, :] = block(index)
 
 
 def start_kernel(
@@ -113,26 +115,27 @@
 ):
     elements = state.shape[0]
     part = elements // 2
-    pairs = [(trace_map_in, trace_map)]
+    pairs = [(records_in, records), (counts_in, counts), (velocity_in, velocity), (levels_in, levels)]
+    pairs += [(neighbours_in, neighbours), (trace_map_in, trace_map)]
     for i in range(2):
         cut = pl.ds(i * part, part)
         pairs.append((state_in.at[cut], state.at[cut]))
-    pairs += [(records_in, records), (counts_in, counts), (velocity_in, velocity), (levels_in, levels)]
-    pairs += [(neighbours_in, neighbours), (projection_in, projection)]
+    pairs.append((projection_in, projection))
     copies = [pltpu.make_async_copy(a, b, sems.at[i]) for i, (a, b) in enumerate(pairs)]
     for copy in copies:
         copy.start()
-    for copy in copies[3:]:
+    for copy in copies[:5]:
         copy.wait()
     columns = record_columns(records, counts)
     column[...] = columns
     source_hot[...] = hot(columns[:, 0:1], elements)
     elements_column[...] = element_columns(velocity, levels, neighbours)
-    copies[0].wait()
+    copies[5].wait()
     for i in range(2):
-        copies[1 + i].wait()
+        copies[6 + i].wait()
         cut = slice(i * part, i * part + part)
         traces[cut, :] = dot(state[cut, :].astype(bf16), trace_map[...]).astype(bf16)
+    copies[8].wait()
     send(traces, source_hot[...], column, projection, first_out, own_out, blocks)
 
 
@@ -169,7 +172,8 @@
         partial_out[:, 128 * t : 128 * t + 128] = near - tile.astype(f32)
 
 
-def local_kernel(stiffness_in, lift_in, column, state, traces, stiffness, lift, base, partial, inflow, picks, sems):
+def local_kernel(stiffness_in, lift_in, column, state, traces, got, stiffness, lift, base, partial, inflow, picks, token, sems):
+    token[...] = got[0:16, :]
     elements, modes = state.shape
     rim = elements // 8
     copies = [
@@ -194,7 +198,8 @@
     copies[1].wait()
 
 
-def second_local_kernel(column, state, field, stiffness, traces, base, partial):
+def second_local_kernel(column, state, field, stiffness, traces, got, base, partial, token):
+    token[...] = got[0:16, :]
     modes = state.shape[1]
     columns = column[...]
     lowered = field[...].astype(bf16)
@@ -205,25 +210,34 @@
     own_part(columns, traces, partial)
 
 
-def gather_arrivals(got, got_even, got_odd, got_a, got_b, arrived):
+def gather_arrivals(got, near, far, last, arrived):
     capacity = arrived.shape[0] // 8
     rim = 2 * capacity
-    at = 2 * rim
     chip, core = place()
-    own = lax.rem(chip, 2)
-    second = lax.rem(lax.div(chip, 2), 2)
-    arrived[0:capacity, :] = got[at : at + capacity, 0:128]
-    for i, ref in enumerate((got_even, got_odd)):
-        for k in range(2):
-            to = capacity * (1 + 2 * i + k)
-            arrived[to : to + capacity, :] = ref[rim : rim + capacity, 128 * k : 128 * k + 128]
-    arrived[5 * capacity : 6 * capacity, :] = got_a[0:capacity, :]
-    arrived[6 * capacity : 7 * capacity, :] = got_b[0:capacity, :]
-    arrived[7 * capacity :, :] = jnp.where(
-        second != core, got_a[capacity : 2 * capacity, :], got_b[capacity : 2 * capacity, :]
-    )
-    forward = jnp.where(own != core, got_even[0:rim, :], got_odd[0:rim, :])
-    return jnp.concatenate([got[0:rim, :], forward], axis=0)
+    near_up = 1 - jnp.bitwise_xor(core, lax.rem(chip, 2))
+    far_up = 1 - jnp.bitwise_xor(core, lax.rem(lax.div(chip, 2), 2))
+    at = 3 * rim
+
+    def mine(ref, start):
+        return ref[pl.ds(pl.multiple_of(start + core * capacity, capacity), capacity), :]
+
+    parts = [
+        got[2 * at : 2 * at + capacity, :],
+        mine(near, at),
+        mine(near, at + 2 * capacity),
+        last[at : at + capacity, :],
+        last[at + capacity : at + 2 * capacity, :],
+        mine(far, 0),
+        last[at + 3 * capacity : at + 4 * capacity, :],
+        jnp.where(far_up != core, last[at + 2 * capacity : at + 3 * capacity, :], mine(far, 2 * capacity)),
+    ]
+    for i, part in enumerate(parts):
+        arrived[capacity * i : capacity * i + capacity, :] = part
+    window = []
+    for t in range(3):
+        cut = slice(rim * t, rim * t + rim)
+        window.append(jnp.concatenate([got[cut, :], jnp.where(near_up == core, near[cut, :], last[cut, :])], axis=0))
+    return window
 
 
 def targets(pieces, elements):
@@ -244,18 +258,18 @@
     for t in range(3):
         cut = slice(128 * t, 128 * t + 128)
         placed = jnp.where(half + 2 * t == face, both, 0.0).astype(bf16)
-        near = dot(picks[:, 256 * t : 256 * t + 256], swapped(window[:, cut]))
+        near = dot(picks[:, 256 * t : 256 * t + 256], swapped(window[t]))
         mortar = dot(element_hot, placed)
         parts.append((inflow[:, cut] * (partial[:, cut] + near + mortar)).astype(bf16))
     return jnp.concatenate(parts, axis=1)
 
 
 def middle_kernel(
-    lift, base, partial, inflow, picks, got, got_even, got_odd, got_a, got_b, trace_map, projection, source_hot, column,
+    lift, base, partial, inflow, picks, got, near, far, last, trace_map, projection, source_hot, column,
     field, traces, first_out, own_out, face_out, element_hot_out, arrived, blocks
 ):
     elements = base.shape[0]
-    window = gather_arrivals(got, got_even, got_odd, got_a, got_b, arrived)
+    window = gather_arrivals(got, near, far, last, arrived)
     pieces = arrived[...]
     face, element_hot = targets(pieces, elements)
     face_out[...] = face
@@ -268,10 +282,10 @@
 
 
 def end_kernel(
-    lift, base, partial, inflow, picks, got, got_even, got_odd, got_a, got_b, face, element_hot, field, arrived, result, sems
+    lift, base, partial, inflow, picks, got, near, far, last, face, element_hot, field, arrived, result, sems
 ):
     elements = base.shape[0]
-    window = gather_arrivals(got, got_even, got_odd, got_a, got_b, arrived)
+    window = gather_arrivals(got, near, far, last, arrived)
     flux = fluxes(arrived[...], face[...], element_hot[...], window, partial, inflow, picks)
     part = elements // 2
     copies = []
@@ -285,17 +299,20 @@
         copy.wait()
 
 
-def paired(count, step, lower):
+def paired(groups, count, step, lower):
     partner = {}
     for s in range(count):
         if lower(s) and s + step < count:
             partner[s] = s + step
             partner[s + step] = s
-    rest = [s for s in range(count) if s not in partner]
-    for a, b in zip(rest[::2], rest[1::2]):
-        partner[a] = b
-        partner[b] = a
-    return sorted(partner.items())
+    pairs = []
+    for g in range(groups):
+        for s in range(count):
+            if s in partner:
+                pairs.append((g * count + s, g * count + partner[s]))
+            elif g ^ 1 < groups:
+                pairs.append((g * count + s, (g ^ 1) * count + s))
+    return pairs
 
 
 def call(kernel, out_shape, scratch, flops, far, near, out_space=pltpu.VMEM):
@@ -313,33 +330,33 @@
     )(*operands)
 
 
-def exchange(first, own, chip, core, rim, capacity):
-    count = lax.axis_size(CURVE)
-    got = lax.ppermute(first, CURVE, paired(count, 1, lambda s: s % 2 == 0))
-    forward = got[rim : 2 * rim]
-    at = 2 * rim
-    up = got[at : at + capacity, 128:256]
-    down = got[at : at + capacity, 256:384]
-    far = got[at + capacity : at + 2 * capacity, 0:128]
-    blank = jnp.zeros_like(up)
-    even = chip % 2 == 0
-    upper = ((chip // 2) % 2 == 0) == (core == 0)
-    mine = [own[capacity * t : capacity * t + capacity] for t in range(4)]
-
-    def near(block, other):
-        return jnp.concatenate([forward, jnp.concatenate([block, other, blank], axis=1)], axis=0)
-
-    to_even = near(mine[0], jnp.where(even, up, down))
-    to_odd = near(mine[1], jnp.where(even, down, up))
-    to_a = jnp.concatenate([mine[2], jnp.where(upper, far, 0)], axis=0)
-    to_b = jnp.concatenate([mine[3], jnp.where(upper, 0, far)], axis=0)
-    return (
-        got,
-        lax.ppermute(to_even, CURVE, paired(count, 2, lambda s: (s // 2) % 2 == 0)),
-        lax.ppermute(to_odd, CURVE, paired(count, 2, lambda s: (s // 2) % 2 == 1)),
-        lax.ppermute(to_a, CURVE, paired(count, 4, lambda s: (s // 4) % 2 == 0)),
-        lax.ppermute(to_b, CURVE, paired(count, 4, lambda s: (s // 4) % 2 == 1)),
-    )
+def exchange(first, own, chip, core, local):
+    axes = ("groups",) + CURVE
+    groups, count = lax.axis_size("groups"), lax.axis_size(CURVE)
+    cores = paired(groups, count, 1, lambda s: s % 2 == 0)
+    chips = paired(groups, count, 2, lambda s: (s // 2) % 2 == s % 2)
+    far_chips = paired(groups, count, 4, lambda s: (s // 4) % 2 == s % 2)
+    capacity = own.shape[0] // 4
+    rim = 6 * capacity
+    at = 2 * rim + capacity
+    got = lax.ppermute(first, axes, cores)
+    own_rim = ((chip % 2) == core) == (core == 1)
+    rims = jnp.where(own_rim, first[rim : 2 * rim], got[rim : 2 * rim])
+    near = jnp.concatenate([rims, own[: 2 * capacity], got[at : at + 2 * capacity]], axis=0)
+    far = jnp.concatenate([own[2 * capacity :], got[at + 2 * capacity : at + 4 * capacity]], axis=0)
+    near = lax.ppermute(near, axes, chips)
+    far = lax.ppermute(far, axes, far_chips)
+
+    *results, token = local(got)
+
+    def theirs(x):
+        return jnp.where(core == 0, x[capacity : 2 * capacity], x[:capacity])
+
+    parts = [near[:rim]]
+    parts += [theirs(near[rim : rim + 2 * capacity]), theirs(near[rim + 2 * capacity :])]
+    parts += [theirs(far[: 2 * capacity]), theirs(far[2 * capacity :]), token]
+    last = lax.ppermute(jnp.concatenate(parts, axis=0), axes, cores)
+    return (got, near, far, last), results
 
 
 def body(
@@ -360,13 +377,15 @@
 
     sent = [
         array((elements, width), bf16),
-        array((2 * rim + 2 * capacity, width), bf16),
+        array((6 * rim + 5 * capacity, 128), bf16),
         array((4 * capacity, 128), bf16),
     ]
     whole = array((elements, modes), f32)
     faces = array((elements, width), f32)
-    blocks = pltpu.VMEM((slots, 128), bf16)
+    blocks = pltpu.VMEM((slots + 2 * capacity, 128), bf16)
+    arrived = pltpu.VMEM((slots, 128), bf16)
     column_shape = array((slots, 128), f32)
+    mark = array((16, 128), bf16)
 
     levels = levels.reshape(1, elements)
     vmem = pltpu.VMEM
@@ -382,34 +401,45 @@
         (state, trace_map, records, counts, velocity, levels, neighbours, projection),
         (),
     )
-    got = exchange(first, own, chip, core, rim, capacity)
-    stiffness, lift, base, partial, inflow, picks = call(
-        local_kernel,
-        [like(stiffness), like(lift), whole, faces, faces, array((elements, 12 * rim), bf16)],
-        [pltpu.SemaphoreType.DMA((2,))],
-        3 * 10**9,
-        (stiffness, lift),
-        (element_column, state, traces),
-    )
+
+    def local(got):
+        return call(
+            local_kernel,
+            [like(stiffness), like(lift), whole, faces, faces, array((elements, 12 * rim), bf16), mark],
+            [pltpu.SemaphoreType.DMA((2,))],
+            3 * 10**9,
+            (stiffness, lift),
+            (element_column, state, traces, got),
+        )
+
+    got, (near_stiffness, near_lift, base, partial, inflow, picks) = exchange(first, own, chip, core, local)
     field, traces, first, own, face, element_hot = call(
         middle_kernel,
         [whole] + sent + [column_shape, array((elements, slots), bf16)],
-        [blocks, blocks],
+        [arrived, blocks],
         10**9,
         (),
-        (lift, base, partial, inflow, picks, *got, trace_map, projection, source_hot, column),
+        (near_lift, base, partial, inflow, picks, *got, trace_map, projection, source_hot, column),
     )
-    got = exchange(first, own, chip, core, rim, capacity)
-    base, partial = call(
-        second_local_kernel, [whole, faces], [], 3 * 10**9, (), (element_column, state, field, stiffness, traces)
-    )
+
+    def second_local(got):
+        return call(
+            second_local_kernel,
+            [whole, faces, mark],
+            [],
+            3 * 10**9,
+            (),
+            (element_column, state, field, near_stiffness, traces, got),
+        )
+
+    got, (base, partial) = exchange(first, own, chip, core, second_local)
     return call(
         end_kernel,
         [whole],
-        [blocks, vmem((elements, modes), f32), pltpu.SemaphoreType.DMA((2,))],
+        [arrived, vmem((elements, modes), f32), pltpu.SemaphoreType.DMA((2,))],
         10**9,
         (),
-        (lift, base, partial, inflow, picks, *got, face, element_hot),
+        (near_lift, base, partial, inflow, picks, *got, face, element_hot),
         out_space=pl.ANY,
     )[0]
 

time: 27.8 us -> 25.3 us (0.910)
  starting transfers between devices: 13.2 us -> 7.84 us
  waiting for transfers between devices: 2.83 us -> 5.72 us
    ppermute x10 -> x8, starting transfers between devices: 13.2 us -> 7.84 us  [the longest x2 3.83 us: exchange(): far = lax.ppermute(far, axes, far_chips)]
    ppermute x10 -> x8, waiting for transfers between devices: 2.83 us -> 5.72 us  [the longest x2 2.54 us: exchange(): last = lax.ppermute(jnp.concatenate(parts, axis=0), axes, cores)]
  transfers between devices with their start and end apart: 10 -> 8, of which waited for: 3 -> 6; matrix products, arithmetic and copies ran while one was open for 0% -> 0% of each run, Pallas kernels for 17% -> 19%
where the time goes in v4:
time: 25.3 us; the launch traced here: 25.1 us
  Pallas kernels  11.2 us (44%)
  starting transfers between devices  7.84 us (31%)
  waiting for transfers between devices  5.72 us (23%)
    pallas_call x5, Pallas kernels, call(): pl.pallas_call(kernel, out_shape=out_shape, in_specs=specs, out_specs=[pl...  11.2 us
    ppermute x2, starting transfers between devices, exchange(): far = lax.ppermute(far, axes, far_chips)  3.83 us
    ppermute x2, starting transfers between devices, exchange(): near = lax.ppermute(near, axes, chips)  3.14 us
    ppermute x2, waiting for transfers between devices, exchange(): last = lax.ppermute(jnp.concatenate(parts, axis=0), axes, cores)  2.54 us
    ppermute x2, waiting for transfers between devices, exchange(): got = lax.ppermute(first, axes, cores)  2.2 us
    ppermute x2, waiting for transfers between devices, exchange(): near = lax.ppermute(near, axes, chips)  0.98 us
    ppermute x2, starting transfers between devices, exchange(): got = lax.ppermute(first, axes, cores)  0.73 us
  transfers between devices with their start and end apart: 8, of which 6 were waited for; matrix products, arithmetic and copies ran while one was open for 0% of the time, Pallas kernels for 19%

profile of v4, /device:TPU:0, one launch (start us, length us, event | category | flops | bytes accessed | tf_op | source)
XLA Modules:
  0.0 25.1 jit_solution(8616802940905245227)
XLA Ops:
  0.0 0.0 copy-start
  0.0 2.5 %shard_map.100 = (bf16[512,384]{1,0:T(8,128)(2,1)S(1)}, bf16[64,512]{1,0:T(8,128)(2,1)S(1)}, bf16[512,384]{1,0:T(8,128)(2,1)S(1)}, bf16[544,128]{1,0:T(8,128)(2,...) custom-call(f32[512,512]{1,0:T(8,128)} %state.3, ...), custom_call_target="tpu_custom_call" | custom-call | flops 200000000 | bytes 1531936 | tf_op jit(solution)/shard_map/pallas_call | solution.py:322
  2.6 0.5 %collective-permute-start = (bf16[544,128]{1,0:T(8,128)(2,1)S(1)}, bf16[544,128]{1,0:T(8,128)(2,1)S(1)}, u32[]{:S(2)}, u32[]{:S(2)}) collective-permute-start(bf16[544,128]{1,0:T(8,128)(2,1)S(1)} %get-tuple-element.31), channel_id=1, source_target_pairs={{0,1},{1,0},{2,3},{3,2},{4,5},{5,4},{6,7},{7,6},{8,9},{9,8},{10,11... | collective-permute-start | bytes 417800 | tf_op jit(solution)/shard_map/ppermute | solution.py:342
  3.1 1.0 %collective-permute-done.got = bf16[544,128]{1,0:T(8,128)(2,1)S(1)} collective-permute-done((bf16[544,128]{1,0:T(8,128)(2,1)S(1)}, bf16[544,128]{1,0:T(8,128)(2,1)S(1)}, u32[]{:S(2)}, u32[]{:S(2)}) %collective-permute-start) | collective-permute-done | bytes 139296 | tf_op jit(solution)/shard_map/ppermute | solution.py:342
  4.1 3.0 %collective-permute-start.2 = (bf16[128,128]{1,0:T(8,128)(2,1)S(1)}, bf16[128,128]{1,0:T(8,128)(2,1)S(1)}, u32[]{:S(2)}, u32[]{:S(2)}) collective-permute-start(bf16[128,128]{1,0:T(8,128)(2,1)S(1)} %pad_maximum_fusion.2), channel_id=1, source_target_pairs={{0,4},{1,17},{2,6},{3,19},{4,0},{5,9},{6,2},{7,11},{8,12},{9,5},{1... | collective-permute-start | bytes 98312 | tf_op jit(solution)/shard_map/ppermute | solution.py:348
  7.1 1.6 %collective-permute-start.1 = (bf16[320,128]{1,0:T(8,128)(2,1)S(1)}, bf16[320,128]{1,0:T(8,128)(2,1)S(1)}, u32[]{:S(2)}, u32[]{:S(2)}) collective-permute-start(bf16[320,128]{1,0:T(8,128)(2,1)S(1)} %pad_maximum_fusion), channel_id=1, source_target_pairs={{0,2},{1,17},{2,0},{3,5},{4,6},{5,3},{6,4},{7,9},{8,10},{9,7},{10,... | collective-permute-start | bytes 245768 | tf_op jit(solution)/shard_map/ppermute | solution.py:347
  8.7 0.0 copy-done
  8.7 2.8 %shard_map.101 = (bf16[512,1536]{1,0:T(8,128)(2,1)S(1)}, bf16[384,512]{1,0:T(8,128)(2,1)S(1)}, f32[512,512]{1,0:T(8,128)S(1)}, f32[512,384]{1,0:T(8,128)S(1)}, f...) custom-call(bf16[512,1536]{1,0:T(8,128)(2,1)} %stiffness_in.1, ...), custom_call_target="tpu_custom_call" | custom-call | flops 3000000000 | bytes 3809280 | tf_op jit(solution)/shard_map/pallas_call | solution.py:322
  11.5 0.1 collective-permute-done.1.near
  11.6 0.0 collective-permute-done.2.far
  11.7 0.1 collective-permute-start.3
  11.8 1.3 %collective-permute-done.3.last = bf16[336,128]{1,0:T(8,128)(2,1)S(1)} collective-permute-done((bf16[336,128]{1,0:T(8,128)(2,1)S(1)}, bf16[336,128]{1,0:T(8,128)(2,1)S(1)}, u32[]{:S(2)}, u32[]{:S(2)}) %collective-permute-start.3) | collective-permute-done | bytes 86048 | tf_op jit(solution)/shard_map/ppermute | solution.py:358
  13.0 1.8 %shard_map.102 = (f32[512,512]{1,0:T(8,128)S(1)}, bf16[512,384]{1,0:T(8,128)(2,1)S(1)}, bf16[544,128]{1,0:T(8,128)(2,1)S(1)}, bf16[128,128]{1,0:T(8,128)(2,1)S(1...) custom-call(bf16[384,512]{1,0:T(8,128)(2,1)S(1)} %get-tuple-element.32.lift, ...), custom_call_target="tpu_custom_call" | custom-call | flops 1000000000 | bytes 4993024 | tf_op jit(solution)/shard_map/pallas_call | solution.py:322
  14.9 0.2 collective-permute-start.4
  15.1 1.2 %collective-permute-done.4.got = bf16[544,128]{1,0:T(8,128)(2,1)S(1)} collective-permute-done((bf16[544,128]{1,0:T(8,128)(2,1)S(1)}, bf16[544,128]{1,0:T(8,128)(2,1)S(1)}, u32[]{:S(2)}, u32[]{:S(2)}) %collective-permute-start.4) | collective-permute-done | bytes 139296 | tf_op jit(solution)/shard_map/ppermute | solution.py:342
  16.3 0.8 %collective-permute-start.6 = (bf16[128,128]{1,0:T(8,128)(2,1)S(1)}, bf16[128,128]{1,0:T(8,128)(2,1)S(1)}, u32[]{:S(2)}, u32[]{:S(2)}) collective-permute-start(bf16[128,128]{1,0:T(8,128)(2,1)S(1)} %pad_maximum_fusion.3), channel_id=1, source_target_pairs={{0,4},{1,17},{2,6},{3,19},{4,0},{5,9},{6,2},{7,11},{8,12},{9,5},{1... | collective-permute-start | bytes 98312 | tf_op jit(solution)/shard_map/ppermute | solution.py:348
  17.2 1.6 %collective-permute-start.5 = (bf16[320,128]{1,0:T(8,128)(2,1)S(1)}, bf16[320,128]{1,0:T(8,128)(2,1)S(1)}, u32[]{:S(2)}, u32[]{:S(2)}) collective-permute-start(bf16[320,128]{1,0:T(8,128)(2,1)S(1)} %pad_maximum_fusion.1), channel_id=1, source_target_pairs={{0,2},{1,17},{2,0},{3,5},{4,6},{5,3},{6,4},{7,9},{8,10},{9,7},{10,... | collective-permute-start | bytes 245768 | tf_op jit(solution)/shard_map/ppermute | solution.py:347
  18.8 2.1 %shard_map.103 = (f32[512,512]{1,0:T(8,128)S(1)}, f32[512,384]{1,0:T(8,128)S(1)}, bf16[16,128]{1,0:T(8,128)(2,1)S(1)}) custom-call(f32[512,128]{1,0:T(8,128)S(1)} %get-tuple-element.29.column, f32[512,512]{1,0:T(8,128)S(1)} %copy-done, f32[512,512]{1,0:T(8,128)S(1)} %get-tuple-element.43.field, bf16[512,1536]{1,0:T(8,128)(2,1)S(1)} %get-tuple-element.44.stiffness, ...), custom_call_target="tpu_custom_call" | custom-call | flops 3000000000 | bytes 4464640 | tf_op jit(solution)/shard_map/pallas_call | solution.py:322
  20.8 0.9 %collective-permute-done.5.near = bf16[320,128]{1,0:T(8,128)(2,1)S(1)} collective-permute-done((bf16[320,128]{1,0:T(8,128)(2,1)S(1)}, bf16[320,128]{1,0:T(8,128)(2,1)S(1)}, u32[]{:S(2)}, u32[]{:S(2)}) %collective-permute-start.5) | collective-permute-done | bytes 81952 | tf_op jit(solution)/shard_map/ppermute | solution.py:347
  21.7 0.0 collective-permute-done.6.far
  21.8 0.1 collective-permute-start.7
  21.9 1.3 %collective-permute-done.7.last = bf16[336,128]{1,0:T(8,128)(2,1)S(1)} collective-permute-done((bf16[336,128]{1,0:T(8,128)(2,1)S(1)}, bf16[336,128]{1,0:T(8,128)(2,1)S(1)}, u32[]{:S(2)}, u32[]{:S(2)}) %collective-permute-start.7) | collective-permute-done | bytes 86048 | tf_op jit(solution)/shard_map/ppermute | solution.py:358
  23.1 2.0 %shard_map.104 = f32[512,512]{1,0:T(8,128)} custom-call(bf16[384,512]{1,0:T(8,128)(2,1)S(1)} %get-tuple-element.32.lift, f32[512,512]{1,0:T(8,128)S(1)} %get-tuple-element.47.base, f32[512,384]{1,0:T(8,128)S(1)} %get-tuple-element.48.partial, f32[512,384]{1,0:T(8,128)S(1)} %get-tuple-element.35.inflow, bf16[512,768]{1,0:T(8,128)(2,1)S(1)} %get-tuple-element.36.picks, ...), custom_call_target="tpu_custom_call" | custom-call | flops 1000000000 | bytes 4534272 | tf_op jit(solution)/shard_map/pallas_call | solution.py:322
  (22 shorter events, 0.2 us)
Async XLA Ops:
  0.0 8.7 %copy-start = (f32[512,512]{1,0:T(8,128)S(1)}, f32[512,512]{1,0:T(8,128)}, u32[]{:S(2)}) copy-start(f32[512,512]{1,0:T(8,128)} %state.3) | copy-start | bytes 3145732
  2.6 1.5 %collective-permute-start = (bf16[544,128]{1,0:T(8,128)(2,1)S(1)}, bf16[544,128]{1,0:T(8,128)(2,1)S(1)}, u32[]{:S(2)}, u32[]{:S(2)}) collective-permute-start(bf16[544,128]{1,0:T(8,128)(2,1)S(1)} %get-tuple-element.31), channel_id=1, source_target_pairs={{0,1},{1,0},{2,3},{3,2},{4,5},{5,4},{6,7},{7,6},{8,9},{9,8},{10,11... | collective-permute-start | bytes 417800 | tf_op jit(solution)/shard_map/ppermute | solution.py:342
  4.1 7.6 %collective-permute-start.2 = (bf16[128,128]{1,0:T(8,128)(2,1)S(1)}, bf16[128,128]{1,0:T(8,128)(2,1)S(1)}, u32[]{:S(2)}, u32[]{:S(2)}) collective-permute-start(bf16[128,128]{1,0:T(8,128)(2,1)S(1)} %pad_maximum_fusion.2), channel_id=1, source_target_pairs={{0,4},{1,17},{2,6},{3,19},{4,0},{5,9},{6,2},{7,11},{8,12},{9,5},{1... | collective-permute-start | bytes 98312 | tf_op jit(solution)/shard_map/ppermute | solution.py:348
  7.1 4.5 %collective-permute-start.1 = (bf16[320,128]{1,0:T(8,128)(2,1)S(1)}, bf16[320,128]{1,0:T(8,128)(2,1)S(1)}, u32[]{:S(2)}, u32[]{:S(2)}) collective-permute-start(bf16[320,128]{1,0:T(8,128)(2,1)S(1)} %pad_maximum_fusion), channel_id=1, source_target_pairs={{0,2},{1,17},{2,0},{3,5},{4,6},{5,3},{6,4},{7,9},{8,10},{9,7},{10,... | collective-permute-start | bytes 245768 | tf_op jit(solution)/shard_map/ppermute | solution.py:347
  11.7 1.3 %collective-permute-start.3 = (bf16[336,128]{1,0:T(8,128)(2,1)S(1)}, bf16[336,128]{1,0:T(8,128)(2,1)S(1)}, u32[]{:S(2)}, u32[]{:S(2)}) collective-permute-start(bf16[336,128]{1,0:T(8,128)(2,1)S(1)} %constant_dynamic-update-slice_fusion), channel_id=1, source_target_pairs={{0,1},{1,0},{2,3},{3,2},{4,5},{5,4},{6,7},{7,6},{8,9},{9,8},{10,11... | collective-permute-start | bytes 258056 | tf_op jit(solution)/shard_map/ppermute | solution.py:358
  14.9 1.4 %collective-permute-start.4 = (bf16[544,128]{1,0:T(8,128)(2,1)S(1)}, bf16[544,128]{1,0:T(8,128)(2,1)S(1)}, u32[]{:S(2)}, u32[]{:S(2)}) collective-permute-start(bf16[544,128]{1,0:T(8,128)(2,1)S(1)} %get-tuple-element.46), channel_id=1, source_target_pairs={{0,1},{1,0},{2,3},{3,2},{4,5},{5,4},{6,7},{7,6},{8,9},{9,8},{10,11... | collective-permute-start | bytes 417800 | tf_op jit(solution)/shard_map/ppermute | solution.py:342
  16.3 5.4 %collective-permute-start.6 = (bf16[128,128]{1,0:T(8,128)(2,1)S(1)}, bf16[128,128]{1,0:T(8,128)(2,1)S(1)}, u32[]{:S(2)}, u32[]{:S(2)}) collective-permute-start(bf16[128,128]{1,0:T(8,128)(2,1)S(1)} %pad_maximum_fusion.3), channel_id=1, source_target_pairs={{0,4},{1,17},{2,6},{3,19},{4,0},{5,9},{6,2},{7,11},{8,12},{9,5},{1... | collective-permute-start | bytes 98312 | tf_op jit(solution)/shard_map/ppermute | solution.py:348
  17.2 4.5 %collective-permute-start.5 = (bf16[320,128]{1,0:T(8,128)(2,1)S(1)}, bf16[320,128]{1,0:T(8,128)(2,1)S(1)}, u32[]{:S(2)}, u32[]{:S(2)}) collective-permute-start(bf16[320,128]{1,0:T(8,128)(2,1)S(1)} %pad_maximum_fusion.1), channel_id=1, source_target_pairs={{0,2},{1,17},{2,0},{3,5},{4,6},{5,3},{6,4},{7,9},{8,10},{9,7},{10,... | collective-permute-start | bytes 245768 | tf_op jit(solution)/shard_map/ppermute | solution.py:347
  21.8 1.3 %collective-permute-start.7 = (bf16[336,128]{1,0:T(8,128)(2,1)S(1)}, bf16[336,128]{1,0:T(8,128)(2,1)S(1)}, u32[]{:S(2)}, u32[]{:S(2)}) collective-permute-start(bf16[336,128]{1,0:T(8,128)(2,1)S(1)} %constant_dynamic-update-slice_fusion.5), channel_id=1, source_target_pairs={{0,1},{1,0},{2,3},{3,2},{4,5},{5,4},{6,7},{7,6},{8,9},{9,8},{10,11... | collective-permute-start | bytes 258056 | tf_op jit(solution)/shard_map/ppermute | solution.py:358

commit v5 on v4

--- a/solution.py
+++ b/solution.py
@@ -67,9 +67,7 @@
     slots = column.shape[0]
     capacity = slots // 8
     rim = elements // 8
-    chip, core = place()
-    near_up = 1 - jnp.bitwise_xor(core, lax.rem(chip, 2))
-    far_up = 1 - jnp.bitwise_xor(core, lax.rem(lax.div(chip, 2), 2))
+    core = lax.axis_index("pair")
     shape = (slots, 128)
     lane = lanes(shape)
     half = jnp.where(lane < 64, 0.0, 1.0)
@@ -84,28 +82,26 @@
     for t in range(4):
         folded = jnp.where(half + 2 * t == kind, every[:, 128 * t : 128 * t + 128], folded)
     piece = folded + pltpu.roll(folded, 64, 1)
-    nothing = jnp.zeros((capacity, 128), bf16)
-    blocks[0:capacity, :] = nothing
-    blocks[capacity : capacity + slots, :] = jnp.where(lane < 64, piece, column[...]).astype(bf16)
-    blocks[capacity + slots :, :] = nothing
-
-    def block(index):
-        return blocks[pl.ds(pl.multiple_of((index + 1) * capacity, capacity), capacity), :]
+    blocks[...] = jnp.where(lane < 64, piece, column[...]).astype(bf16)
+
+    def block(at_first, at_second):
+        index = at_first + core * (at_second - at_first)
+        return blocks[pl.ds(pl.multiple_of(index * capacity, capacity), capacity), :]
 
     final_at = pl.multiple_of((1 - core) * (elements - rim), rim)
     other_at = pl.multiple_of(core * (elements - rim), rim)
     for t in range(3):
         cut = slice(128 * t, 128 * t + 128)
-        first_out[rim * t : rim * t + rim, :] = traces[pl.ds(final_at, rim), cut]
-        first_out[rim * (3 + t) : rim * (4 + t), :] = traces[pl.ds(other_at, rim), cut]
-    at = 6 * rim
-    inside = 4 - core
-    here = [2 + 3 * near_up - core, 3 + 3 * near_up - core, 7 * far_up - core, 1 + 7 * far_up - core]
-    there = [5 - 3 * near_up - core, 6 - 3 * near_up - core, 7 - 7 * far_up - core, 8 - 7 * far_up - core]
-    for i, index in enumerate([inside] + there):
-        first_out[at + capacity * i : at + capacity * i + capacity, :] = block(index)
-    for i, index in enumerate(here):
-        own_out[capacity * i : capacity * i + capacity, :] = block(index)
+        rows = slice(rim * t, rim * t + rim)
+        first_out[rows, :] = traces[pl.ds(final_at, rim), cut]
+        own_out[rows, :] = traces[pl.ds(other_at, rim), cut]
+    at = 3 * rim
+    there = [(4, 3), (5, 1), (6, 2), (7, 0)]
+    here = [(2, 4), (3, 5), (0, 6), (1, 7)]
+    for i in range(4):
+        rows = slice(at + capacity * i, at + capacity * i + capacity)
+        first_out[rows, :] = block(*there[i])
+        own_out[rows, :] = block(*here[i])
 
 
 def start_kernel(
@@ -213,31 +209,20 @@
 def gather_arrivals(got, near, far, last, arrived):
     capacity = arrived.shape[0] // 8
     rim = 2 * capacity
-    chip, core = place()
-    near_up = 1 - jnp.bitwise_xor(core, lax.rem(chip, 2))
-    far_up = 1 - jnp.bitwise_xor(core, lax.rem(lax.div(chip, 2), 2))
+    core = lax.axis_index("pair")
     at = 3 * rim
 
     def mine(ref, start):
         return ref[pl.ds(pl.multiple_of(start + core * capacity, capacity), capacity), :]
 
-    parts = [
-        got[2 * at : 2 * at + capacity, :],
-        mine(near, at),
-        mine(near, at + 2 * capacity),
-        last[at : at + capacity, :],
-        last[at + capacity : at + 2 * capacity, :],
-        mine(far, 0),
-        last[at + 3 * capacity : at + 4 * capacity, :],
-        jnp.where(far_up != core, last[at + 2 * capacity : at + 3 * capacity, :], mine(far, 2 * capacity)),
-    ]
-    for i, part in enumerate(parts):
-        arrived[capacity * i : capacity * i + capacity, :] = part
-    window = []
-    for t in range(3):
-        cut = slice(rim * t, rim * t + rim)
-        window.append(jnp.concatenate([got[cut, :], jnp.where(near_up == core, near[cut, :], last[cut, :])], axis=0))
-    return window
+    arrived[0:capacity, :] = got[at : at + capacity, :]
+    arrived[capacity : 2 * capacity, :] = mine(near, at)
+    arrived[2 * capacity : 3 * capacity, :] = mine(near, at + 2 * capacity)
+    arrived[3 * capacity : 4 * capacity, :] = mine(far, 0)
+    arrived[4 * capacity : 5 * capacity, :] = far[2 * capacity : 3 * capacity, :]
+    arrived[5 * capacity :, :] = last[0 : 3 * capacity, :]
+    cuts = [slice(rim * t, rim * t + rim) for t in range(3)]
+    return [jnp.concatenate([got[cut, :], near[cut, :]], axis=0) for cut in cuts]
 
 
 def targets(pieces, elements):
@@ -286,14 +271,15 @@
 ):
     elements = base.shape[0]
     window = gather_arrivals(got, near, far, last, arrived)
-    flux = fluxes(arrived[...], face[...], element_hot[...], window, partial, inflow, picks)
     part = elements // 2
     copies = []
     for i in range(2):
-        cut = slice(i * part, i * part + part)
-        result[cut, :] = base[cut, :] + 0.5 * time_step * dot(flux[cut, :], lift[...])
-        rows = pl.ds(i * part, part)
-        copies.append(pltpu.make_async_copy(result.at[rows], field.at[rows], sems.at[i]))
+        cut = pl.ds(i * part, part)
+        flux = fluxes(
+            arrived[...], face[...], element_hot[cut, :], window, partial.at[cut], inflow.at[cut], picks.at[cut]
+        )
+        result[cut, :] = base[cut, :] + 0.5 * time_step * dot(flux, lift[...])
+        copies.append(pltpu.make_async_copy(result.at[cut], field.at[cut], sems.at[i]))
         copies[i].start()
     for copy in copies:
         copy.wait()
@@ -330,32 +316,25 @@
     )(*operands)
 
 
-def exchange(first, own, chip, core, local):
+def exchange(first, own, core, capacity, local):
     axes = ("groups",) + CURVE
     groups, count = lax.axis_size("groups"), lax.axis_size(CURVE)
     cores = paired(groups, count, 1, lambda s: s % 2 == 0)
-    chips = paired(groups, count, 2, lambda s: (s // 2) % 2 == s % 2)
-    far_chips = paired(groups, count, 4, lambda s: (s // 4) % 2 == s % 2)
-    capacity = own.shape[0] // 4
-    rim = 6 * capacity
-    at = 2 * rim + capacity
+    chips = paired(groups, count, 1, lambda s: s % 2 == 1)
+    far_chips = paired(groups, count, 3, lambda s: s % 2 == 1)
+    at = own.shape[0] - 4 * capacity
     got = lax.ppermute(first, axes, cores)
-    own_rim = ((chip % 2) == core) == (core == 1)
-    rims = jnp.where(own_rim, first[rim : 2 * rim], got[rim : 2 * rim])
-    near = jnp.concatenate([rims, own[: 2 * capacity], got[at : at + 2 * capacity]], axis=0)
-    far = jnp.concatenate([own[2 * capacity :], got[at + 2 * capacity : at + 4 * capacity]], axis=0)
+    near = jnp.concatenate([own[: at + 2 * capacity], got[at + capacity : at + 3 * capacity]], axis=0)
+    far = jnp.concatenate([own[at + 2 * capacity :], got[at + 3 * capacity :]], axis=0)
     near = lax.ppermute(near, axes, chips)
     far = lax.ppermute(far, axes, far_chips)
-
     *results, token = local(got)
 
     def theirs(x):
         return jnp.where(core == 0, x[capacity : 2 * capacity], x[:capacity])
 
-    parts = [near[:rim]]
-    parts += [theirs(near[rim : rim + 2 * capacity]), theirs(near[rim + 2 * capacity :])]
-    parts += [theirs(far[: 2 * capacity]), theirs(far[2 * capacity :]), token]
-    last = lax.ppermute(jnp.concatenate(parts, axis=0), axes, cores)
+    parts = [theirs(near[at : at + 2 * capacity]), theirs(near[at + 2 * capacity :]), theirs(far[: 2 * capacity])]
+    last = lax.ppermute(jnp.concatenate(parts + [token], axis=0), axes, cores)
     return (got, near, far, last), results
 
 
@@ -367,7 +346,7 @@
     slots = records.shape[1]
     capacity = slots // counts.shape[1]
     rim = elements // 8
-    chip, core = place()
+    core = lax.axis_index("pair")
 
     def array(shape, dtype):
         return jax.ShapeDtypeStruct(shape, dtype)
@@ -377,13 +356,12 @@
 
     sent = [
         array((elements, width), bf16),
-        array((6 * rim + 5 * capacity, 128), bf16),
-        array((4 * capacity, 128), bf16),
+        array((3 * rim + 4 * capacity, 128), bf16),
+        array((3 * rim + 4 * capacity, 128), bf16),
     ]
     whole = array((elements, modes), f32)
     faces = array((elements, width), f32)
-    blocks = pltpu.VMEM((slots + 2 * capacity, 128), bf16)
-    arrived = pltpu.VMEM((slots, 128), bf16)
+    blocks = pltpu.VMEM((slots, 128), bf16)
     column_shape = array((slots, 128), f32)
     mark = array((16, 128), bf16)
 
@@ -412,11 +390,11 @@
             (element_column, state, traces, got),
         )
 
-    got, (near_stiffness, near_lift, base, partial, inflow, picks) = exchange(first, own, chip, core, local)
+    got, (near_stiffness, near_lift, base, partial, inflow, picks) = exchange(first, own, core, capacity, local)
     field, traces, first, own, face, element_hot = call(
         middle_kernel,
         [whole] + sent + [column_shape, array((elements, slots), bf16)],
-        [arrived, blocks],
+        [blocks, blocks],
         10**9,
         (),
         (near_lift, base, partial, inflow, picks, *got, trace_map, projection, source_hot, column),
@@ -432,11 +410,11 @@
             (element_column, state, field, near_stiffness, traces, got),
         )
 
-    got, (base, partial) = exchange(first, own, chip, core, second_local)
+    got, (base, partial) = exchange(first, own, core, capacity, second_local)
     return call(
         end_kernel,
         [whole],
-        [arrived, vmem((elements, modes), f32), pltpu.SemaphoreType.DMA((2,))],
+        [blocks, vmem((elements, modes), f32), pltpu.SemaphoreType.DMA((2,))],
         10**9,
         (),
         (near_lift, base, partial, inflow, picks, *got, face, element_hot),

time: 25.3 us -> 24.5 us (0.968)
  starting transfers between devices: 7.84 us -> 6.13 us
  waiting for transfers between devices: 5.72 us -> 6.91 us
    ppermute x2, waiting for transfers between devices: 0.98 us -> 2.7 us  [exchange(): near = lax.ppermute(near, axes, chips)]
    ppermute x2, starting transfers between devices: 3.14 us -> 1.41 us  [exchange(): near = lax.ppermute(near, axes, chips)]
    ppermute x2, waiting for transfers between devices: 2.54 us -> 2.18 us  [exchange(): last = lax.ppermute(jnp.concatenate(parts + [token], axis=0), axes, cores)]
  transfers between devices with their start and end apart: 8 -> 8, of which waited for: 6 -> 6; matrix products, arithmetic and copies ran while one was open for 0% -> 0% of each run, Pallas kernels for 19% -> 20%
where the time goes in v5:
time: 24.5 us; the launch traced here: 24.2 us
  Pallas kernels  11 us (45%)
  waiting for transfers between devices  6.91 us (28%)
  starting transfers between devices  6.13 us (25%)
    pallas_call x5, Pallas kernels, call(): pl.pallas_call(kernel, out_shape=out_shape, in_specs=specs, out_specs=[pl...  11 us
    ppermute x2, starting transfers between devices, exchange(): far = lax.ppermute(far, axes, far_chips)  3.63 us
    ppermute x2, waiting for transfers between devices, exchange(): near = lax.ppermute(near, axes, chips)  2.7 us
    ppermute x2, waiting for transfers between devices, exchange(): last = lax.ppermute(jnp.concatenate(parts + [token], axis=0), axes, cores)  2.18 us
    ppermute x2, waiting for transfers between devices, exchange(): got = lax.ppermute(first, axes, cores)  2.02 us
    ppermute x2, starting transfers between devices, exchange(): near = lax.ppermute(near, axes, chips)  1.41 us
    ppermute x2, starting transfers between devices, exchange(): got = lax.ppermute(first, axes, cores)  0.73 us
  transfers between devices with their start and end apart: 8, of which 6 were waited for; matrix products, arithmetic and copies ran while one was open for 0% of the time, Pallas kernels for 20%

profile of v5, /device:TPU:0, one launch (start us, length us, event | category | flops | bytes accessed | tf_op | source)
XLA Modules:
  0.0 24.2 jit_solution(15035103288734295874)
XLA Ops:
  0.0 0.0 copy-start
  0.0 2.6 %shard_map.100 = (bf16[512,384]{1,0:T(8,128)(2,1)S(1)}, bf16[64,512]{1,0:T(8,128)(2,1)S(1)}, bf16[512,384]{1,0:T(8,128)(2,1)S(1)}, bf16[320,128]{1,0:T(8,128)(2,...) custom-call(f32[512,512]{1,0:T(8,128)} %state.3, ...), custom_call_target="tpu_custom_call" | custom-call | flops 200000000 | bytes 1531936 | tf_op jit(solution)/shard_map/pallas_call | solution.py:308
  2.6 0.5 %collective-permute-start = (bf16[320,128]{1,0:T(8,128)(2,1)S(1)}, bf16[320,128]{1,0:T(8,128)(2,1)S(1)}, u32[]{:S(2)}, u32[]{:S(2)}) collective-permute-start(bf16[320,128]{1,0:T(8,128)(2,1)S(1)} %get-tuple-element.31), channel_id=1, source_target_pairs={{0,1},{1,0},{2,3},{3,2},{4,5},{5,4},{6,7},{7,6},{8,9},{9,8},{10,11... | collective-permute-start | bytes 245768 | tf_op jit(solution)/shard_map/ppermute | solution.py:326
  3.1 0.9 %collective-permute-done.got = bf16[320,128]{1,0:T(8,128)(2,1)S(1)} collective-permute-done((bf16[320,128]{1,0:T(8,128)(2,1)S(1)}, bf16[320,128]{1,0:T(8,128)(2,1)S(1)}, u32[]{:S(2)}, u32[]{:S(2)}) %collective-permute-start) | collective-permute-done | bytes 81952 | tf_op jit(solution)/shard_map/ppermute | solution.py:326
  4.0 2.9 %collective-permute-start.2 = (bf16[96,128]{1,0:T(8,128)(2,1)S(1)}, bf16[96,128]{1,0:T(8,128)(2,1)S(1)}, u32[]{:S(2)}, u32[]{:S(2)}) collective-permute-start(bf16[96,128]{1,0:T(8,128)(2,1)S(1)} %pad_maximum_fusion.4), channel_id=1, source_target_pairs={{0,16},{1,4},{2,18},{3,6},{4,1},{5,8},{6,3},{7,10},{8,5},{9,12},{1... | collective-permute-start | bytes 73736 | tf_op jit(solution)/shard_map/ppermute | solution.py:330
  6.9 0.1 collective-permute-start.1
  7.0 0.0 copy-done
  7.0 2.8 %shard_map.101 = (bf16[512,1536]{1,0:T(8,128)(2,1)S(1)}, bf16[384,512]{1,0:T(8,128)(2,1)S(1)}, f32[512,512]{1,0:T(8,128)S(1)}, f32[512,384]{1,0:T(8,128)S(1)}, f...) custom-call(bf16[512,1536]{1,0:T(8,128)(2,1)} %stiffness_in.1, ...), custom_call_target="tpu_custom_call" | custom-call | flops 3000000000 | bytes 3751936 | tf_op jit(solution)/shard_map/pallas_call | solution.py:308
  9.8 0.0 collective-permute-done.2.far
  9.8 1.6 %collective-permute-done.1.near = bf16[320,128]{1,0:T(8,128)(2,1)S(1)} collective-permute-done((bf16[320,128]{1,0:T(8,128)(2,1)S(1)}, bf16[320,128]{1,0:T(8,128)(2,1)S(1)}, u32[]{:S(2)}, u32[]{:S(2)}) %collective-permute-start.1) | collective-permute-done | bytes 81952 | tf_op jit(solution)/shard_map/ppermute | solution.py:329
  11.4 0.1 collective-permute-start.3
  11.5 1.2 %collective-permute-done.3.last = bf16[112,128]{1,0:T(8,128)(2,1)S(1)} collective-permute-done((bf16[112,128]{1,0:T(8,128)(2,1)S(1)}, bf16[112,128]{1,0:T(8,128)(2,1)S(1)}, u32[]{:S(2)}, u32[]{:S(2)}) %collective-permute-start.3) | collective-permute-done | bytes 28704 | tf_op jit(solution)/shard_map/ppermute | solution.py:337
  12.7 1.8 %shard_map.102 = (f32[512,512]{1,0:T(8,128)S(1)}, bf16[512,384]{1,0:T(8,128)(2,1)S(1)}, bf16[320,128]{1,0:T(8,128)(2,1)S(1)}, bf16[320,128]{1,0:T(8,128)(2,1)S(1...) custom-call(bf16[384,512]{1,0:T(8,128)(2,1)S(1)} %get-tuple-element.32.lift, ...), custom_call_target="tpu_custom_call" | custom-call | flops 1000000000 | bytes 4870144 | tf_op jit(solution)/shard_map/pallas_call | solution.py:308
  14.5 0.2 collective-permute-start.4
  14.8 1.1 %collective-permute-done.4.got = bf16[320,128]{1,0:T(8,128)(2,1)S(1)} collective-permute-done((bf16[320,128]{1,0:T(8,128)(2,1)S(1)}, bf16[320,128]{1,0:T(8,128)(2,1)S(1)}, u32[]{:S(2)}, u32[]{:S(2)}) %collective-permute-start.4) | collective-permute-done | bytes 81952 | tf_op jit(solution)/shard_map/ppermute | solution.py:326
  15.9 0.8 %collective-permute-start.6 = (bf16[96,128]{1,0:T(8,128)(2,1)S(1)}, bf16[96,128]{1,0:T(8,128)(2,1)S(1)}, u32[]{:S(2)}, u32[]{:S(2)}) collective-permute-start(bf16[96,128]{1,0:T(8,128)(2,1)S(1)} %pad_maximum_fusion.5), channel_id=1, source_target_pairs={{0,16},{1,4},{2,18},{3,6},{4,1},{5,8},{6,3},{7,10},{8,5},{9,12},{1... | collective-permute-start | bytes 73736 | tf_op jit(solution)/shard_map/ppermute | solution.py:330
  16.6 1.3 %collective-permute-start.5 = (bf16[320,128]{1,0:T(8,128)(2,1)S(1)}, bf16[320,128]{1,0:T(8,128)(2,1)S(1)}, u32[]{:S(2)}, u32[]{:S(2)}) collective-permute-start(bf16[320,128]{1,0:T(8,128)(2,1)S(1)} %pad_maximum_fusion.1), channel_id=1, source_target_pairs={{0,16},{1,2},{2,1},{3,4},{4,3},{5,6},{6,5},{7,8},{8,7},{9,10},{10,... | collective-permute-start | bytes 245768 | tf_op jit(solution)/shard_map/ppermute | solution.py:329
  18.0 2.0 %shard_map.103 = (f32[512,512]{1,0:T(8,128)S(1)}, f32[512,384]{1,0:T(8,128)S(1)}, bf16[16,128]{1,0:T(8,128)(2,1)S(1)}) custom-call(f32[512,128]{1,0:T(8,128)S(1)} %get-tuple-element.29.column, f32[512,512]{1,0:T(8,128)S(1)} %copy-done, f32[512,512]{1,0:T(8,128)S(1)} %get-tuple-element.43.field, bf16[512,1536]{1,0:T(8,128)(2,1)S(1)} %get-tuple-element.44.stiffness, ...), custom_call_target="tpu_custom_call" | custom-call | flops 3000000000 | bytes 4407296 | tf_op jit(solution)/shard_map/pallas_call | solution.py:308
  20.0 0.0 collective-permute-done.6.far
  20.0 1.1 %collective-permute-done.5.near = bf16[320,128]{1,0:T(8,128)(2,1)S(1)} collective-permute-done((bf16[320,128]{1,0:T(8,128)(2,1)S(1)}, bf16[320,128]{1,0:T(8,128)(2,1)S(1)}, u32[]{:S(2)}, u32[]{:S(2)}) %collective-permute-start.5) | collective-permute-done | bytes 81952 | tf_op jit(solution)/shard_map/ppermute | solution.py:329
  21.2 0.3 %collective-permute-start.7 = (bf16[112,128]{1,0:T(8,128)(2,1)S(1)}, bf16[112,128]{1,0:T(8,128)(2,1)S(1)}, u32[]{:S(2)}, u32[]{:S(2)}) collective-permute-start(bf16[112,128]{1,0:T(8,128)(2,1)S(1)} %pad_maximum_fusion.3), channel_id=1, source_target_pairs={{0,1},{1,0},{2,3},{3,2},{4,5},{5,4},{6,7},{7,6},{8,9},{9,8},{10,11... | collective-permute-start | bytes 86024 | tf_op jit(solution)/shard_map/ppermute | solution.py:337
  21.4 1.0 %collective-permute-done.7.last = bf16[112,128]{1,0:T(8,128)(2,1)S(1)} collective-permute-done((bf16[112,128]{1,0:T(8,128)(2,1)S(1)}, bf16[112,128]{1,0:T(8,128)(2,1)S(1)}, u32[]{:S(2)}, u32[]{:S(2)}) %collective-permute-start.7) | collective-permute-done | bytes 28704 | tf_op jit(solution)/shard_map/ppermute | solution.py:337
  22.4 1.8 %shard_map.104 = f32[512,512]{1,0:T(8,128)} custom-call(bf16[384,512]{1,0:T(8,128)(2,1)S(1)} %get-tuple-element.32.lift, f32[512,512]{1,0:T(8,128)S(1)} %get-tuple-element.47.base, f32[512,384]{1,0:T(8,128)S(1)} %get-tuple-element.48.partial, f32[512,384]{1,0:T(8,128)S(1)} %get-tuple-element.35.inflow, bf16[512,768]{1,0:T(8,128)(2,1)S(1)} %get-tuple-element.36.picks, ...), custom_call_target="tpu_custom_call" | custom-call | flops 1000000000 | bytes 4411392 | tf_op jit(solution)/shard_map/pallas_call | solution.py:308
  (18 shorter events, 0.1 us)
Async XLA Ops:
  0.0 7.0 %copy-start = (f32[512,512]{1,0:T(8,128)S(1)}, f32[512,512]{1,0:T(8,128)}, u32[]{:S(2)}) copy-start(f32[512,512]{1,0:T(8,128)} %state.3) | copy-start | bytes 3145732
  2.6 1.4 %collective-permute-start = (bf16[320,128]{1,0:T(8,128)(2,1)S(1)}, bf16[320,128]{1,0:T(8,128)(2,1)S(1)}, u32[]{:S(2)}, u32[]{:S(2)}) collective-permute-start(bf16[320,128]{1,0:T(8,128)(2,1)S(1)} %get-tuple-element.31), channel_id=1, source_target_pairs={{0,1},{1,0},{2,3},{3,2},{4,5},{5,4},{6,7},{7,6},{8,9},{9,8},{10,11... | collective-permute-start | bytes 245768 | tf_op jit(solution)/shard_map/ppermute | solution.py:326
  4.0 5.8 %collective-permute-start.2 = (bf16[96,128]{1,0:T(8,128)(2,1)S(1)}, bf16[96,128]{1,0:T(8,128)(2,1)S(1)}, u32[]{:S(2)}, u32[]{:S(2)}) collective-permute-start(bf16[96,128]{1,0:T(8,128)(2,1)S(1)} %pad_maximum_fusion.4), channel_id=1, source_target_pairs={{0,16},{1,4},{2,18},{3,6},{4,1},{5,8},{6,3},{7,10},{8,5},{9,12},{1... | collective-permute-start | bytes 73736 | tf_op jit(solution)/shard_map/ppermute | solution.py:330
  6.9 4.5 %collective-permute-start.1 = (bf16[320,128]{1,0:T(8,128)(2,1)S(1)}, bf16[320,128]{1,0:T(8,128)(2,1)S(1)}, u32[]{:S(2)}, u32[]{:S(2)}) collective-permute-start(bf16[320,128]{1,0:T(8,128)(2,1)S(1)} %pad_maximum_fusion), channel_id=1, source_target_pairs={{0,16},{1,2},{2,1},{3,4},{4,3},{5,6},{6,5},{7,8},{8,7},{9,10},{10,... | collective-permute-start | bytes 245768 | tf_op jit(solution)/shard_map/ppermute | solution.py:329
  11.4 1.3 %collective-permute-start.3 = (bf16[112,128]{1,0:T(8,128)(2,1)S(1)}, bf16[112,128]{1,0:T(8,128)(2,1)S(1)}, u32[]{:S(2)}, u32[]{:S(2)}) collective-permute-start(bf16[112,128]{1,0:T(8,128)(2,1)S(1)} %pad_maximum_fusion.2), channel_id=1, source_target_pairs={{0,1},{1,0},{2,3},{3,2},{4,5},{5,4},{6,7},{7,6},{8,9},{9,8},{10,11... | collective-permute-start | bytes 86024 | tf_op jit(solution)/shard_map/ppermute | solution.py:337
  14.5 1.3 %collective-permute-start.4 = (bf16[320,128]{1,0:T(8,128)(2,1)S(1)}, bf16[320,128]{1,0:T(8,128)(2,1)S(1)}, u32[]{:S(2)}, u32[]{:S(2)}) collective-permute-start(bf16[320,128]{1,0:T(8,128)(2,1)S(1)} %get-tuple-element.46), channel_id=1, source_target_pairs={{0,1},{1,0},{2,3},{3,2},{4,5},{5,4},{6,7},{7,6},{8,9},{9,8},{10,11... | collective-permute-start | bytes 245768 | tf_op jit(solution)/shard_map/ppermute | solution.py:326
  15.9 4.1 %collective-permute-start.6 = (bf16[96,128]{1,0:T(8,128)(2,1)S(1)}, bf16[96,128]{1,0:T(8,128)(2,1)S(1)}, u32[]{:S(2)}, u32[]{:S(2)}) collective-permute-start(bf16[96,128]{1,0:T(8,128)(2,1)S(1)} %pad_maximum_fusion.5), channel_id=1, source_target_pairs={{0,16},{1,4},{2,18},{3,6},{4,1},{5,8},{6,3},{7,10},{8,5},{9,12},{1... | collective-permute-start | bytes 73736 | tf_op jit(solution)/shard_map/ppermute | solution.py:330
  16.6 4.5 %collective-permute-start.5 = (bf16[320,128]{1,0:T(8,128)(2,1)S(1)}, bf16[320,128]{1,0:T(8,128)(2,1)S(1)}, u32[]{:S(2)}, u32[]{:S(2)}) collective-permute-start(bf16[320,128]{1,0:T(8,128)(2,1)S(1)} %pad_maximum_fusion.1), channel_id=1, source_target_pairs={{0,16},{1,2},{2,1},{3,4},{4,3},{5,6},{6,5},{7,8},{8,7},{9,10},{10,... | collective-permute-start | bytes 245768 | tf_op jit(solution)/shard_map/ppermute | solution.py:329
  21.2 1.3 %collective-permute-start.7 = (bf16[112,128]{1,0:T(8,128)(2,1)S(1)}, bf16[112,128]{1,0:T(8,128)(2,1)S(1)}, u32[]{:S(2)}, u32[]{:S(2)}) collective-permute-start(bf16[112,128]{1,0:T(8,128)(2,1)S(1)} %pad_maximum_fusion.3), channel_id=1, source_target_pairs={{0,1},{1,0},{2,3},{3,2},{4,5},{5,4},{6,7},{7,6},{8,9},{9,8},{10,11... | collective-permute-start | bytes 86024 | tf_op jit(solution)/shard_map/ppermute | solution.py:337

commit v6 on v5

--- a/solution.py
+++ b/solution.py
@@ -106,8 +106,8 @@
 
 def start_kernel(
     state_in, trace_map_in, records_in, counts_in, velocity_in, levels_in, neighbours_in, projection_in,
-    trace_map, projection, traces, first_out, own_out, source_hot, column, elements_column,
-    state, records, counts, velocity, levels, neighbours, blocks, sems
+    state, trace_map, projection, traces, first_out, own_out, source_hot, column, elements_column,
+    records, counts, velocity, levels, neighbours, blocks, sems
 ):
     elements = state.shape[0]
     part = elements // 2
@@ -206,23 +206,24 @@
     own_part(columns, traces, partial)
 
 
-def gather_arrivals(got, near, far, last, arrived):
-    capacity = arrived.shape[0] // 8
-    rim = 2 * capacity
+def direct_pieces(got, near, far, arrived):
+    capacity = arrived.shape[0] // 5
+    at = 6 * capacity
     core = lax.axis_index("pair")
-    at = 3 * rim
 
     def mine(ref, start):
         return ref[pl.ds(pl.multiple_of(start + core * capacity, capacity), capacity), :]
 
-    arrived[0:capacity, :] = got[at : at + capacity, :]
-    arrived[capacity : 2 * capacity, :] = mine(near, at)
-    arrived[2 * capacity : 3 * capacity, :] = mine(near, at + 2 * capacity)
-    arrived[3 * capacity : 4 * capacity, :] = mine(far, 0)
-    arrived[4 * capacity : 5 * capacity, :] = far[2 * capacity : 3 * capacity, :]
-    arrived[5 * capacity :, :] = last[0 : 3 * capacity, :]
-    cuts = [slice(rim * t, rim * t + rim) for t in range(3)]
-    return [jnp.concatenate([got[cut, :], near[cut, :]], axis=0) for cut in cuts]
+    blocks = [
+        got[at : at + capacity, :],
+        mine(near, at),
+        mine(near, at + 2 * capacity),
+        mine(far, 0),
+        far[2 * capacity : 3 * capacity, :],
+    ]
+    for i, block in enumerate(blocks):
+        arrived[capacity * i : capacity * i + capacity, :] = block
+    return arrived[...]
 
 
 def targets(pieces, elements):
@@ -235,49 +236,69 @@
     return face, jnp.where(match, 1.0, 0.0).astype(bf16)
 
 
-def fluxes(pieces, face, element_hot, window, partial, inflow, picks):
+def mortar_term(pieces, face, element_hot, t):
     half = jnp.where(lanes(pieces.shape) < 64, 0.0, 1.0)
     plain = jnp.where(half == 0.0, pieces.astype(f32), 0.0)
     both = plain + pltpu.roll(plain, 64, 1)
+    return dot(element_hot, jnp.where(half + 2 * t == face, both, 0.0).astype(bf16))
+
+
+def add_direct(picks, partial, got, near, pieces, face, element_hot, total):
+    rim = picks.shape[1] // 12
+    for t in range(3):
+        cut = slice(128 * t, 128 * t + 128)
+        rows = slice(rim * t, rim * t + rim)
+        window = jnp.concatenate([got[rows, :], near[rows, :]], axis=0)
+        conforming = dot(picks[:, 4 * rim * t : 4 * rim * t + 4 * rim], swapped(window))
+        total[:, cut] = partial[:, cut] + conforming + mortar_term(pieces, face, element_hot, t)
+
+
+def direct_kernel(picks, partial, got, near, far, last, total, face_out, element_hot_out, arrived):
+    pieces = direct_pieces(got, near, far, arrived)
+    face, element_hot = targets(pieces, partial.shape[0])
+    face_out[...] = face
+    element_hot_out[...] = element_hot
+    add_direct(picks, partial, got, near, pieces, face, element_hot, total)
+
+
+def second_direct_kernel(picks, partial, face, element_hot, got, near, far, last, total, arrived):
+    pieces = direct_pieces(got, near, far, arrived)
+    add_direct(picks, partial, got, near, pieces, face[...], element_hot[...], total)
+
+
+def fluxes(pieces, face, element_hot, partial, inflow):
     parts = []
     for t in range(3):
         cut = slice(128 * t, 128 * t + 128)
-        placed = jnp.where(half + 2 * t == face, both, 0.0).astype(bf16)
-        near = dot(picks[:, 256 * t : 256 * t + 256], swapped(window[t]))
-        mortar = dot(element_hot, placed)
-        parts.append((inflow[:, cut] * (partial[:, cut] + near + mortar)).astype(bf16))
+        total = partial[:, cut] + mortar_term(pieces, face, element_hot, t)
+        parts.append((inflow[:, cut] * total).astype(bf16))
     return jnp.concatenate(parts, axis=1)
 
 
 def middle_kernel(
-    lift, base, partial, inflow, picks, got, near, far, last, trace_map, projection, source_hot, column,
-    field, traces, first_out, own_out, face_out, element_hot_out, arrived, blocks
+    lift, base, partial, inflow, last, trace_map, projection, source_hot, column,
+    field, traces, first_out, own_out, face_out, element_hot_out, blocks
 ):
     elements = base.shape[0]
-    window = gather_arrivals(got, near, far, last, arrived)
-    pieces = arrived[...]
+    pieces = last[0 : face_out.shape[0], :]
     face, element_hot = targets(pieces, elements)
     face_out[...] = face
     element_hot_out[...] = element_hot
-    flux = fluxes(pieces, face, element_hot, window, partial, inflow, picks)
+    flux = fluxes(pieces, face, element_hot, partial, inflow)
     new = base[...] + time_step * dot(flux, lift[...])
     field[...] = new
     traces[...] = dot(new.astype(bf16), trace_map[...]).astype(bf16)
     send(traces, source_hot[...], column, projection, first_out, own_out, blocks)
 
 
-def end_kernel(
-    lift, base, partial, inflow, picks, got, near, far, last, face, element_hot, field, arrived, result, sems
-):
+def end_kernel(lift, base, partial, inflow, last, face, element_hot, field, result, sems):
     elements = base.shape[0]
-    window = gather_arrivals(got, near, far, last, arrived)
+    pieces = last[0 : face.shape[0], :]
     part = elements // 2
     copies = []
     for i in range(2):
         cut = pl.ds(i * part, part)
-        flux = fluxes(
-            arrived[...], face[...], element_hot[cut, :], window, partial.at[cut], inflow.at[cut], picks.at[cut]
-        )
+        flux = fluxes(pieces, face[...], element_hot[cut, :], partial.at[cut], inflow.at[cut])
         result[cut, :] = base[cut, :] + 0.5 * time_step * dot(flux, lift[...])
         copies.append(pltpu.make_async_copy(result.at[cut], field.at[cut], sems.at[i]))
         copies[i].start()
@@ -316,7 +337,7 @@
     )(*operands)
 
 
-def exchange(first, own, core, capacity, local):
+def exchange(first, own, core, capacity, local, direct):
     axes = ("groups",) + CURVE
     groups, count = lax.axis_size("groups"), lax.axis_size(CURVE)
     cores = paired(groups, count, 1, lambda s: s % 2 == 0)
@@ -334,8 +355,9 @@
         return jnp.where(core == 0, x[capacity : 2 * capacity], x[:capacity])
 
     parts = [theirs(near[at : at + 2 * capacity]), theirs(near[at + 2 * capacity :]), theirs(far[: 2 * capacity])]
-    last = lax.ppermute(jnp.concatenate(parts + [token], axis=0), axes, cores)
-    return (got, near, far, last), results
+    last = jnp.concatenate(parts + [token], axis=0)
+    totals = direct(results, got, near, far, last)
+    return lax.ppermute(last, axes, cores), totals, results
 
 
 def body(
@@ -368,12 +390,12 @@
     levels = levels.reshape(1, elements)
     vmem = pltpu.VMEM
     wide = (elements, 128)
-    trace_map, projection, traces, first, own, source_hot, column, element_column = call(
+    near_state, trace_map, projection, traces, first, own, source_hot, column, element_column = call(
         start_kernel,
-        [like(trace_map), like(projection)]
+        [like(state), like(trace_map), like(projection)]
         + sent
         + [array((slots, elements), bf16), column_shape, array(wide, f32)],
-        [vmem(x.shape, x.dtype) for x in (state, records, counts, velocity, levels, neighbours)]
+        [vmem(x.shape, x.dtype) for x in (records, counts, velocity, levels, neighbours)]
         + [blocks, pltpu.SemaphoreType.DMA((9,))],
         2 * 10**8,
         (state, trace_map, records, counts, velocity, levels, neighbours, projection),
@@ -387,17 +409,29 @@
             [pltpu.SemaphoreType.DMA((2,))],
             3 * 10**9,
             (stiffness, lift),
-            (element_column, state, traces, got),
+            (element_column, near_state, traces, got),
         )
 
-    got, (near_stiffness, near_lift, base, partial, inflow, picks) = exchange(first, own, core, capacity, local)
+    def direct(results, *arrived):
+        return call(
+            direct_kernel,
+            [faces, array((5 * capacity, 128), f32), array((elements, 5 * capacity), bf16)],
+            [vmem((5 * capacity, 128), bf16)],
+            10**9,
+            (),
+            (results[5], results[3], *arrived),
+        )
+
+    last, (partial, *direct_targets), (near_stiffness, near_lift, base, _, inflow, picks) = exchange(
+        first, own, core, capacity, local, direct
+    )
     field, traces, first, own, face, element_hot = call(
         middle_kernel,
-        [whole] + sent + [column_shape, array((elements, slots), bf16)],
-        [blocks, blocks],
+        [whole] + sent + [array((3 * capacity, 128), f32), array((elements, 3 * capacity), bf16)],
+        [blocks],
         10**9,
         (),
-        (near_lift, base, partial, inflow, picks, *got, trace_map, projection, source_hot, column),
+        (near_lift, base, partial, inflow, last, trace_map, projection, source_hot, column),
     )
 
     def second_local(got):
@@ -410,14 +444,24 @@
             (element_column, state, field, near_stiffness, traces, got),
         )
 
-    got, (base, partial) = exchange(first, own, core, capacity, second_local)
+    def second_direct(results, *arrived):
+        return call(
+            second_direct_kernel,
+            [faces],
+            [vmem((5 * capacity, 128), bf16)],
+            10**9,
+            (),
+            (picks, results[1], *direct_targets, *arrived),
+        )
+
+    last, (partial,), (base, _) = exchange(first, own, core, capacity, second_local, second_direct)
     return call(
         end_kernel,
         [whole],
-        [blocks, vmem((elements, modes), f32), pltpu.SemaphoreType.DMA((2,))],
+        [vmem((elements, modes), f32), pltpu.SemaphoreType.DMA((2,))],
         10**9,
         (),
-        (near_lift, base, partial, inflow, picks, *got, face, element_hot),
+        (near_lift, base, partial, inflow, last, face, element_hot),
         out_space=pl.ANY,
     )[0]
 

time: 24.5 us -> 23.9 us (0.976)
  waiting for transfers between devices: 6.91 us -> 5.48 us
  Pallas kernels: 11 us -> 11.8 us
    ppermute x2, waiting for transfers between devices: 2.18 us -> 0.81 us  [exchange(): return (lax.ppermute(last, axes, cores), totals, results)]
    pallas_call x5 -> x7, Pallas kernels: 11 us -> 11.8 us  [call(): pl.pallas_call(kernel, out_shape=out_shape, in_specs=specs, out_specs=[pl...]
  transfers between devices with their start and end apart: 8 -> 8, of which waited for: 6 -> 6; matrix products, arithmetic and copies ran while one was open for 0% -> 0% of each run, Pallas kernels for 20% -> 26%
where the time goes in v6:
time: 23.9 us; the launch traced here: 23.6 us
  Pallas kernels  11.8 us (49%)
  starting transfers between devices  6.15 us (26%)
  waiting for transfers between devices  5.48 us (23%)
    pallas_call x7, Pallas kernels, call(): pl.pallas_call(kernel, out_shape=out_shape, in_specs=specs, out_specs=[pl...  11.8 us
    ppermute x2, starting transfers between devices, exchange(): far = lax.ppermute(far, axes, far_chips)  3.64 us
    ppermute x2, waiting for transfers between devices, exchange(): near = lax.ppermute(near, axes, chips)  2.66 us
    ppermute x2, waiting for transfers between devices, exchange(): got = lax.ppermute(first, axes, cores)  2.01 us
    ppermute x2, starting transfers between devices, exchange(): near = lax.ppermute(near, axes, chips)  1.4 us
    ppermute x2, waiting for transfers between devices, exchange(): return (lax.ppermute(last, axes, cores), totals, results)  0.81 us
    ppermute x2, starting transfers between devices, exchange(): got = lax.ppermute(first, axes, cores)  0.75 us
  transfers between devices with their start and end apart: 8, of which 6 were waited for; matrix products, arithmetic and copies ran while one was open for 0% of the time, Pallas kernels for 26%

profile of v6, /device:TPU:0, one launch (start us, length us, event | category | flops | bytes accessed | tf_op | source)
XLA Modules:
  0.0 23.6 jit_solution(15019110531808481150)
XLA Ops:
  0.0 2.5 %shard_map.100 = (f32[512,512]{1,0:T(8,128)S(1)}, bf16[512,384]{1,0:T(8,128)(2,1)S(1)}, bf16[64,512]{1,0:T(8,128)(2,1)S(1)}, bf16[512,384]{1,0:T(8,128)(2,1)S(1)...) custom-call(f32[512,512]{1,0:T(8,128)} %state.1, ...), custom_call_target="tpu_custom_call" | custom-call | flops 200000000 | bytes 1531936 | tf_op jit(solution)/shard_map/pallas_call | solution.py:329
  2.5 0.5 %collective-permute-start = (bf16[320,128]{1,0:T(8,128)(2,1)S(1)}, bf16[320,128]{1,0:T(8,128)(2,1)S(1)}, u32[]{:S(2)}, u32[]{:S(2)}) collective-permute-start(bf16[320,128]{1,0:T(8,128)(2,1)S(1)} %get-tuple-element.36), channel_id=1, source_target_pairs={{0,1},{1,0},{2,3},{3,2},{4,5},{5,4},{6,7},{7,6},{8,9},{9,8},{10,11... | collective-permute-start | bytes 245768 | tf_op jit(solution)/shard_map/ppermute | solution.py:347
  3.0 0.9 %collective-permute-done.got = bf16[320,128]{1,0:T(8,128)(2,1)S(1)} collective-permute-done((bf16[320,128]{1,0:T(8,128)(2,1)S(1)}, bf16[320,128]{1,0:T(8,128)(2,1)S(1)}, u32[]{:S(2)}, u32[]{:S(2)}) %collective-permute-start) | collective-permute-done | bytes 81952 | tf_op jit(solution)/shard_map/ppermute | solution.py:347
  3.9 2.9 %collective-permute-start.2 = (bf16[96,128]{1,0:T(8,128)(2,1)S(1)}, bf16[96,128]{1,0:T(8,128)(2,1)S(1)}, u32[]{:S(2)}, u32[]{:S(2)}) collective-permute-start(bf16[96,128]{1,0:T(8,128)(2,1)S(1)} %pad_maximum_fusion.4), channel_id=1, source_target_pairs={{0,16},{1,4},{2,18},{3,6},{4,1},{5,8},{6,3},{7,10},{8,5},{9,12},{1... | collective-permute-start | bytes 73736 | tf_op jit(solution)/shard_map/ppermute | solution.py:351
  6.8 0.1 collective-permute-start.1
  6.9 2.8 %shard_map.101 = (bf16[512,1536]{1,0:T(8,128)(2,1)S(1)}, bf16[384,512]{1,0:T(8,128)(2,1)S(1)}, f32[512,512]{1,0:T(8,128)S(1)}, f32[512,384]{1,0:T(8,128)S(1)}, f...) custom-call(bf16[512,1536]{1,0:T(8,128)(2,1)} %stiffness_in.1, ...), custom_call_target="tpu_custom_call" | custom-call | flops 3000000000 | bytes 3751936 | tf_op jit(solution)/shard_map/pallas_call | solution.py:329
  9.7 0.0 collective-permute-done.2.far
  9.7 1.6 %collective-permute-done.1.near = bf16[320,128]{1,0:T(8,128)(2,1)S(1)} collective-permute-done((bf16[320,128]{1,0:T(8,128)(2,1)S(1)}, bf16[320,128]{1,0:T(8,128)(2,1)S(1)}, u32[]{:S(2)}, u32[]{:S(2)}) %collective-permute-start.1) | collective-permute-done | bytes 81952 | tf_op jit(solution)/shard_map/ppermute | solution.py:350
  11.3 0.1 collective-permute-start.3
  11.4 0.7 %shard_map.102 = (f32[512,384]{1,0:T(8,128)S(1)}, f32[160,128]{1,0:T(8,128)S(1)}, bf16[512,160]{1,0:T(8,128)(2,1)S(1)}) custom-call(bf16[512,768]{1,0:T(8,128)(2,1)S(1)} %get-tuple-element.39.picks, f32[512,384]{1,0:T(8,128)S(1)} %get-tuple-element.40.partial, bf16[320,128]{1,0:T(8,128)(2,1)S(1)} %collective-permute-done.got, ...), custom_call_target="tpu_custom_call" | custom-call | flops 1000000000 | bytes 1789952 | tf_op jit(solution)/shard_map/pallas_call | solution.py:329
  12.1 0.5 %collective-permute-done.3.last = bf16[112,128]{1,0:T(8,128)(2,1)S(1)} collective-permute-done((bf16[112,128]{1,0:T(8,128)(2,1)S(1)}, bf16[112,128]{1,0:T(8,128)(2,1)S(1)}, u32[]{:S(2)}, u32[]{:S(2)}) %collective-permute-start.3) | collective-permute-done | bytes 28704 | tf_op jit(solution)/shard_map/ppermute | solution.py:360
  12.6 1.5 %shard_map.103 = (f32[512,512]{1,0:T(8,128)S(1)}, bf16[512,384]{1,0:T(8,128)(2,1)S(1)}, bf16[320,128]{1,0:T(8,128)(2,1)S(1)}, bf16[320,128]{1,0:T(8,128)(2,1)S(1...) custom-call(bf16[384,512]{1,0:T(8,128)(2,1)S(1)} %get-tuple-element.37.lift, ...), custom_call_target="tpu_custom_call" | custom-call | flops 1000000000 | bytes 3895296 | tf_op jit(solution)/shard_map/pallas_call | solution.py:329
  14.1 0.2 collective-permute-start.4
  14.3 1.1 %collective-permute-done.4.got = bf16[320,128]{1,0:T(8,128)(2,1)S(1)} collective-permute-done((bf16[320,128]{1,0:T(8,128)(2,1)S(1)}, bf16[320,128]{1,0:T(8,128)(2,1)S(1)}, u32[]{:S(2)}, u32[]{:S(2)}) %collective-permute-start.4) | collective-permute-done | bytes 81952 | tf_op jit(solution)/shard_map/ppermute | solution.py:347
  15.4 0.8 %collective-permute-start.6 = (bf16[96,128]{1,0:T(8,128)(2,1)S(1)}, bf16[96,128]{1,0:T(8,128)(2,1)S(1)}, u32[]{:S(2)}, u32[]{:S(2)}) collective-permute-start(bf16[96,128]{1,0:T(8,128)(2,1)S(1)} %pad_maximum_fusion.5), channel_id=1, source_target_pairs={{0,16},{1,4},{2,18},{3,6},{4,1},{5,8},{6,3},{7,10},{8,5},{9,12},{1... | collective-permute-start | bytes 73736 | tf_op jit(solution)/shard_map/ppermute | solution.py:351
  16.2 1.3 %collective-permute-start.5 = (bf16[320,128]{1,0:T(8,128)(2,1)S(1)}, bf16[320,128]{1,0:T(8,128)(2,1)S(1)}, u32[]{:S(2)}, u32[]{:S(2)}) collective-permute-start(bf16[320,128]{1,0:T(8,128)(2,1)S(1)} %pad_maximum_fusion.1), channel_id=1, source_target_pairs={{0,16},{1,2},{2,1},{3,4},{4,3},{5,6},{6,5},{7,8},{8,7},{9,10},{10,... | collective-permute-start | bytes 245768 | tf_op jit(solution)/shard_map/ppermute | solution.py:350
  17.5 0.0 copy-done
  17.5 2.1 %shard_map.104 = (f32[512,512]{1,0:T(8,128)S(1)}, f32[512,384]{1,0:T(8,128)S(1)}, bf16[16,128]{1,0:T(8,128)(2,1)S(1)}) custom-call(f32[512,128]{1,0:T(8,128)S(1)} %get-tuple-element.33.column, f32[512,512]{1,0:T(8,128)S(1)} %copy-done, f32[512,512]{1,0:T(8,128)S(1)} %get-tuple-element.49.field, bf16[512,1536]{1,0:T(8,128)(2,1)S(1)} %get-tuple-element.50.stiffness, ...), custom_call_target="tpu_custom_call" | custom-call | flops 3000000000 | bytes 4407296 | tf_op jit(solution)/shard_map/pallas_call | solution.py:329
  19.6 0.0 collective-permute-done.6.far
  19.6 1.1 %collective-permute-done.5.near = bf16[320,128]{1,0:T(8,128)(2,1)S(1)} collective-permute-done((bf16[320,128]{1,0:T(8,128)(2,1)S(1)}, bf16[320,128]{1,0:T(8,128)(2,1)S(1)}, u32[]{:S(2)}, u32[]{:S(2)}) %collective-permute-start.5) | collective-permute-done | bytes 81952 | tf_op jit(solution)/shard_map/ppermute | solution.py:350
  20.7 0.3 %collective-permute-start.7 = (bf16[112,128]{1,0:T(8,128)(2,1)S(1)}, bf16[112,128]{1,0:T(8,128)(2,1)S(1)}, u32[]{:S(2)}, u32[]{:S(2)}) collective-permute-start(bf16[112,128]{1,0:T(8,128)(2,1)S(1)} %pad_maximum_fusion.3.last), channel_id=1, source_target_pairs={{0,1},{1,0},{2,3},{3,2},{4,5},{5,4},{6,7},{7,6},{8,9},{9,8},{10,11... | collective-permute-start | bytes 86024 | tf_op jit(solution)/shard_map/ppermute | solution.py:360
  21.0 0.7 %shard_map.105.partial = f32[512,384]{1,0:T(8,128)S(1)} custom-call(bf16[512,768]{1,0:T(8,128)(2,1)S(1)} %get-tuple-element.39.picks, f32[512,384]{1,0:T(8,128)S(1)} %get-tuple-element.54.partial, f32[160,128]{1,0:T(8,128)S(1)} %get-tuple-element.55.face, bf16[512,160]{1,0:T(8,128)(2,1)S(1)} %get-tuple-element.56.element_hot, ...), custom_call_target="tpu_custom_call" | custom-call | flops 1000000000 | bytes 2035712 | tf_op jit(solution)/shard_map/pallas_call | solution.py:329
  21.7 0.4 %collective-permute-done.7.last = bf16[112,128]{1,0:T(8,128)(2,1)S(1)} collective-permute-done((bf16[112,128]{1,0:T(8,128)(2,1)S(1)}, bf16[112,128]{1,0:T(8,128)(2,1)S(1)}, u32[]{:S(2)}, u32[]{:S(2)}) %collective-permute-start.7) | collective-permute-done | bytes 28704 | tf_op jit(solution)/shard_map/ppermute | solution.py:360
  22.0 1.6 %shard_map.106 = f32[512,512]{1,0:T(8,128)} custom-call(bf16[384,512]{1,0:T(8,128)(2,1)S(1)} %get-tuple-element.37.lift, f32[512,512]{1,0:T(8,128)S(1)} %get-tuple-element.53.base, f32[512,384]{1,0:T(8,128)S(1)} %shard_map.105.partial, f32[512,384]{1,0:T(8,128)S(1)} %get-tuple-element.44.inflow, bf16[112,128]{1,0:T(8,128)(2,1)S(1)} %collective-permute-done.7.last, ...), custom_call_target="tpu_custom_call" | custom-call | flops 1000000000 | bytes 3190784 | tf_op jit(solution)/shard_map/pallas_call | solution.py:329
  (19 shorter events, 0.1 us)
Async XLA Ops:
  2.5 1.4 %collective-permute-start = (bf16[320,128]{1,0:T(8,128)(2,1)S(1)}, bf16[320,128]{1,0:T(8,128)(2,1)S(1)}, u32[]{:S(2)}, u32[]{:S(2)}) collective-permute-start(bf16[320,128]{1,0:T(8,128)(2,1)S(1)} %get-tuple-element.36), channel_id=1, source_target_pairs={{0,1},{1,0},{2,3},{3,2},{4,5},{5,4},{6,7},{7,6},{8,9},{9,8},{10,11... | collective-permute-start | bytes 245768 | tf_op jit(solution)/shard_map/ppermute | solution.py:347
  3.9 5.8 %collective-permute-start.2 = (bf16[96,128]{1,0:T(8,128)(2,1)S(1)}, bf16[96,128]{1,0:T(8,128)(2,1)S(1)}, u32[]{:S(2)}, u32[]{:S(2)}) collective-permute-start(bf16[96,128]{1,0:T(8,128)(2,1)S(1)} %pad_maximum_fusion.4), channel_id=1, source_target_pairs={{0,16},{1,4},{2,18},{3,6},{4,1},{5,8},{6,3},{7,10},{8,5},{9,12},{1... | collective-permute-start | bytes 73736 | tf_op jit(solution)/shard_map/ppermute | solution.py:351
  6.8 4.5 %collective-permute-start.1 = (bf16[320,128]{1,0:T(8,128)(2,1)S(1)}, bf16[320,128]{1,0:T(8,128)(2,1)S(1)}, u32[]{:S(2)}, u32[]{:S(2)}) collective-permute-start(bf16[320,128]{1,0:T(8,128)(2,1)S(1)} %pad_maximum_fusion), channel_id=1, source_target_pairs={{0,16},{1,2},{2,1},{3,4},{4,3},{5,6},{6,5},{7,8},{8,7},{9,10},{10,... | collective-permute-start | bytes 245768 | tf_op jit(solution)/shard_map/ppermute | solution.py:350
  11.3 1.3 %collective-permute-start.3 = (bf16[112,128]{1,0:T(8,128)(2,1)S(1)}, bf16[112,128]{1,0:T(8,128)(2,1)S(1)}, u32[]{:S(2)}, u32[]{:S(2)}) collective-permute-start(bf16[112,128]{1,0:T(8,128)(2,1)S(1)} %pad_maximum_fusion.2.last), channel_id=1, source_target_pairs={{0,1},{1,0},{2,3},{3,2},{4,5},{5,4},{6,7},{7,6},{8,9},{9,8},{10,11... | collective-permute-start | bytes 86024 | tf_op jit(solution)/shard_map/ppermute | solution.py:360
  12.6 5.0 %copy-start = (f32[512,512]{1,0:T(8,128)S(1)}, f32[512,512]{1,0:T(8,128)}, u32[]{:S(2)}) copy-start(f32[512,512]{1,0:T(8,128)} %state.1) | copy-start | bytes 3145732
  14.1 1.3 %collective-permute-start.4 = (bf16[320,128]{1,0:T(8,128)(2,1)S(1)}, bf16[320,128]{1,0:T(8,128)(2,1)S(1)}, u32[]{:S(2)}, u32[]{:S(2)}) collective-permute-start(bf16[320,128]{1,0:T(8,128)(2,1)S(1)} %get-tuple-element.52), channel_id=1, source_target_pairs={{0,1},{1,0},{2,3},{3,2},{4,5},{5,4},{6,7},{7,6},{8,9},{9,8},{10,11... | collective-permute-start | bytes 245768 | tf_op jit(solution)/shard_map/ppermute | solution.py:347
  15.4 4.2 %collective-permute-start.6 = (bf16[96,128]{1,0:T(8,128)(2,1)S(1)}, bf16[96,128]{1,0:T(8,128)(2,1)S(1)}, u32[]{:S(2)}, u32[]{:S(2)}) collective-permute-start(bf16[96,128]{1,0:T(8,128)(2,1)S(1)} %pad_maximum_fusion.5), channel_id=1, source_target_pairs={{0,16},{1,4},{2,18},{3,6},{4,1},{5,8},{6,3},{7,10},{8,5},{9,12},{1... | collective-permute-start | bytes 73736 | tf_op jit(solution)/shard_map/ppermute | solution.py:351
  16.2 4.5 %collective-permute-start.5 = (bf16[320,128]{1,0:T(8,128)(2,1)S(1)}, bf16[320,128]{1,0:T(8,128)(2,1)S(1)}, u32[]{:S(2)}, u32[]{:S(2)}) collective-permute-start(bf16[320,128]{1,0:T(8,128)(2,1)S(1)} %pad_maximum_fusion.1), channel_id=1, source_target_pairs={{0,16},{1,2},{2,1},{3,4},{4,3},{5,6},{6,5},{7,8},{8,7},{9,10},{10,... | collective-permute-start | bytes 245768 | tf_op jit(solution)/shard_map/ppermute | solution.py:350
  20.7 1.3 %collective-permute-start.7 = (bf16[112,128]{1,0:T(8,128)(2,1)S(1)}, bf16[112,128]{1,0:T(8,128)(2,1)S(1)}, u32[]{:S(2)}, u32[]{:S(2)}) collective-permute-start(bf16[112,128]{1,0:T(8,128)(2,1)S(1)} %pad_maximum_fusion.3.last), channel_id=1, source_target_pairs={{0,1},{1,0},{2,3},{3,2},{4,5},{5,4},{6,7},{7,6},{8,9},{9,8},{10,11... | collective-permute-start | bytes 86024 | tf_op jit(solution)/shard_map/ppermute | solution.py:360

commit v7 on v6

--- a/solution.py
+++ b/solution.py
@@ -293,14 +293,14 @@
 
 def end_kernel(lift, base, partial, inflow, last, face, element_hot, field, result, sems):
     elements = base.shape[0]
-    pieces = last[0 : face.shape[0], :]
-    part = elements // 2
+    flux = fluxes(last[0 : face.shape[0], :], face[...], element_hot[...], partial, inflow)
+    part = elements // 4
     copies = []
-    for i in range(2):
-        cut = pl.ds(i * part, part)
-        flux = fluxes(pieces, face[...], element_hot[cut, :], partial.at[cut], inflow.at[cut])
-        result[cut, :] = base[cut, :] + 0.5 * time_step * dot(flux, lift[...])
-        copies.append(pltpu.make_async_copy(result.at[cut], field.at[cut], sems.at[i]))
+    for i in range(4):
+        cut = slice(part * i, part * i + part)
+        result[cut, :] = base[cut, :] + 0.5 * time_step * dot(flux[cut, :], lift[...])
+        rows = pl.ds(part * i, part)
+        copies.append(pltpu.make_async_copy(result.at[rows], field.at[rows], sems.at[i]))
         copies[i].start()
     for copy in copies:
         copy.wait()
@@ -324,7 +324,7 @@
 
 def call(kernel, out_shape, scratch, flops, far, near, out_space=pltpu.VMEM):
     operands = [pltpu.with_memory_space_constraint(x, pltpu.HBM) for x in far] + list(near)
-    read = sum(x.size * x.dtype.itemsize for x in operands)
+    read = sum(x.size * x.dtype.itemsize for x in operands) if flops > 10**8 else 10**5
     specs = [pl.BlockSpec(memory_space=pl.ANY)] * len(far) + [pl.BlockSpec(memory_space=pltpu.VMEM)] * len(near)
     return pl.pallas_call(
         kernel,
@@ -354,7 +354,7 @@
     def theirs(x):
         return jnp.where(core == 0, x[capacity : 2 * capacity], x[:capacity])
 
-    parts = [theirs(near[at : at + 2 * capacity]), theirs(near[at + 2 * capacity :]), theirs(far[: 2 * capacity])]
+    parts = [theirs(near[at : at + 2 * capacity]), theirs(near[at + 2 * capacity :]), theirs(far[: 2 * capacity]), theirs(far[capacity:])]
     last = jnp.concatenate(parts + [token], axis=0)
     totals = direct(results, got, near, far, last)
     return lax.ppermute(last, axes, cores), totals, results
@@ -407,7 +407,7 @@
             local_kernel,
             [like(stiffness), like(lift), whole, faces, faces, array((elements, 12 * rim), bf16), mark],
             [pltpu.SemaphoreType.DMA((2,))],
-            3 * 10**9,
+            10**8,
             (stiffness, lift),
             (element_column, near_state, traces, got),
         )
@@ -439,7 +439,7 @@
             second_local_kernel,
             [whole, faces, mark],
             [],
-            3 * 10**9,
+            10**8,
             (),
             (element_column, state, field, near_stiffness, traces, got),
         )
@@ -458,7 +458,7 @@
     return call(
         end_kernel,
         [whole],
-        [vmem((elements, modes), f32), pltpu.SemaphoreType.DMA((2,))],
+        [vmem((elements, modes), f32), pltpu.SemaphoreType.DMA((4,))],
         10**9,
         (),
         (near_lift, base, partial, inflow, last, face, element_hot),

time: 23.9 us -> 23.3 us (0.975)
  waiting for transfers between devices: 5.48 us -> 4.6 us
  starting transfers between devices: 6.15 us -> 6.56 us
    ppermute x2, starting transfers between devices: 1.4 us -> 4.51 us  [exchange(): near = lax.ppermute(near, axes, chips)]
    ppermute x2, starting transfers between devices: 3.64 us -> 0.6 us  [exchange(): far = lax.ppermute(far, axes, far_chips)]
    ppermute x2, waiting for transfers between devices: 2.66 us -> 0.35 us  [exchange(): near = lax.ppermute(near, axes, chips)]
    ppermute x2, waiting for transfers between devices: 0.01 us -> 1.75 us  [exchange(): far = lax.ppermute(far, axes, far_chips)]
  transfers between devices with their start and end apart: 8 -> 8, of which waited for: 6 -> 7; matrix products, arithmetic and copies ran while one was open for 0% -> 0% of each run, Pallas kernels for 26% -> 27%
where the time goes in v7:
time: 23.3 us; the launch traced here: 23.1 us
  Pallas kernels  11.7 us (50%)
  starting transfers between devices  6.56 us (28%)
  waiting for transfers between devices  4.6 us (20%)
    pallas_call x7, Pallas kernels, call(): pl.pallas_call(kernel, out_shape=out_shape, in_specs=specs, out_specs=[pl...  11.7 us
    ppermute x2, starting transfers between devices, exchange(): near = lax.ppermute(near, axes, chips)  4.51 us
    ppermute x2, waiting for transfers between devices, exchange(): got = lax.ppermute(first, axes, cores)  1.82 us
    ppermute x2, waiting for transfers between devices, exchange(): far = lax.ppermute(far, axes, far_chips)  1.75 us
    ppermute x2, starting transfers between devices, exchange(): got = lax.ppermute(first, axes, cores)  0.94 us
    ppermute x2, waiting for transfers between devices, exchange(): return (lax.ppermute(last, axes, cores), totals, results)  0.69 us
    ppermute x2, starting transfers between devices, exchange(): far = lax.ppermute(far, axes, far_chips)  0.6 us
    ppermute x2, starting transfers between devices, exchange(): return (lax.ppermute(last, axes, cores), totals, results)  0.52 us
  transfers between devices with their start and end apart: 8, of which 7 were waited for; matrix products, arithmetic and copies ran while one was open for 0% of the time, Pallas kernels for 27%

profile of v7, /device:TPU:0, one launch (start us, length us, event | category | flops | bytes accessed | tf_op | source)
XLA Modules:
  0.0 23.1 jit_solution(802109565828554894)
XLA Ops:
  0.0 2.5 %shard_map.100 = (f32[512,512]{1,0:T(8,128)S(1)}, bf16[512,384]{1,0:T(8,128)(2,1)S(1)}, bf16[64,512]{1,0:T(8,128)(2,1)S(1)}, bf16[512,384]{1,0:T(8,128)(2,1)S(1)...) custom-call(f32[512,512]{1,0:T(8,128)} %state.1, ...), custom_call_target="tpu_custom_call" | custom-call | flops 200000000 | bytes 1531936 | tf_op jit(solution)/shard_map/pallas_call | solution.py:329
  2.5 0.5 %collective-permute-start = (bf16[320,128]{1,0:T(8,128)(2,1)S(1)}, bf16[320,128]{1,0:T(8,128)(2,1)S(1)}, u32[]{:S(2)}, u32[]{:S(2)}) collective-permute-start(bf16[320,128]{1,0:T(8,128)(2,1)S(1)} %get-tuple-element.36), channel_id=1, source_target_pairs={{0,1},{1,0},{2,3},{3,2},{4,5},{5,4},{6,7},{7,6},{8,9},{9,8},{10,11... | collective-permute-start | bytes 245768 | tf_op jit(solution)/shard_map/ppermute | solution.py:347
  3.0 0.9 %collective-permute-done.got = bf16[320,128]{1,0:T(8,128)(2,1)S(1)} collective-permute-done((bf16[320,128]{1,0:T(8,128)(2,1)S(1)}, bf16[320,128]{1,0:T(8,128)(2,1)S(1)}, u32[]{:S(2)}, u32[]{:S(2)}) %collective-permute-start) | collective-permute-done | bytes 81952 | tf_op jit(solution)/shard_map/ppermute | solution.py:347
  3.9 2.9 %collective-permute-start.1 = (bf16[320,128]{1,0:T(8,128)(2,1)S(1)}, bf16[320,128]{1,0:T(8,128)(2,1)S(1)}, u32[]{:S(2)}, u32[]{:S(2)}) collective-permute-start(bf16[320,128]{1,0:T(8,128)(2,1)S(1)} %pad_maximum_fusion), channel_id=1, source_target_pairs={{0,16},{1,2},{2,1},{3,4},{4,3},{5,6},{6,5},{7,8},{8,7},{9,10},{10,... | collective-permute-start | bytes 245768 | tf_op jit(solution)/shard_map/ppermute | solution.py:350
  6.9 0.1 collective-permute-start.2
  7.0 2.8 %shard_map.101 = (bf16[512,1536]{1,0:T(8,128)(2,1)S(1)}, bf16[384,512]{1,0:T(8,128)(2,1)S(1)}, f32[512,512]{1,0:T(8,128)S(1)}, f32[512,384]{1,0:T(8,128)S(1)}, f...) custom-call(bf16[512,1536]{1,0:T(8,128)(2,1)} %stiffness_in.1, ...), custom_call_target="tpu_custom_call" | custom-call | flops 100000000 | bytes 100000 | tf_op jit(solution)/shard_map/pallas_call | solution.py:329
  9.8 0.0 collective-permute-done.1.near
  9.8 0.9 %collective-permute-done.2.far = bf16[96,128]{1,0:T(8,128)(2,1)S(1)} collective-permute-done((bf16[96,128]{1,0:T(8,128)(2,1)S(1)}, bf16[96,128]{1,0:T(8,128)(2,1)S(1)}, u32[]{:S(2)}, u32[]{:S(2)}) %collective-permute-start.2) | collective-permute-done | bytes 24608 | tf_op jit(solution)/shard_map/ppermute | solution.py:351
  10.7 0.4 %collective-permute-start.3 = (bf16[144,128]{1,0:T(8,128)(2,1)S(1)}, bf16[144,128]{1,0:T(8,128)(2,1)S(1)}, u32[]{:S(2)}, u32[]{:S(2)}) collective-permute-start(bf16[144,128]{1,0:T(8,128)(2,1)S(1)} %constant_dynamic-update-slice_fusion.last), channel_id=1, source_target_pairs={{0,1},{1,0},{2,3},{3,2},{4,5},{5,4},{6,7},{7,6},{8,9},{9,8},{10,11... | collective-permute-start | bytes 110600 | tf_op jit(solution)/shard_map/ppermute | solution.py:360
  11.2 0.7 %shard_map.102 = (f32[512,384]{1,0:T(8,128)S(1)}, f32[160,128]{1,0:T(8,128)S(1)}, bf16[512,160]{1,0:T(8,128)(2,1)S(1)}) custom-call(bf16[512,768]{1,0:T(8,128)(2,1)S(1)} %get-tuple-element.39.picks, f32[512,384]{1,0:T(8,128)S(1)} %get-tuple-element.40.partial, bf16[320,128]{1,0:T(8,128)(2,1)S(1)} %collective-permute-done.got, ...), custom_call_target="tpu_custom_call" | custom-call | flops 1000000000 | bytes 1798144 | tf_op jit(solution)/shard_map/pallas_call | solution.py:329
  11.9 0.1 collective-permute-done.3.last
  12.0 1.5 %shard_map.103 = (f32[512,512]{1,0:T(8,128)S(1)}, bf16[512,384]{1,0:T(8,128)(2,1)S(1)}, bf16[320,128]{1,0:T(8,128)(2,1)S(1)}, bf16[320,128]{1,0:T(8,128)(2,1)S(1...) custom-call(bf16[384,512]{1,0:T(8,128)(2,1)S(1)} %get-tuple-element.37.lift, ...), custom_call_target="tpu_custom_call" | custom-call | flops 1000000000 | bytes 3903488 | tf_op jit(solution)/shard_map/pallas_call | solution.py:329
  13.6 0.4 %collective-permute-start.4 = (bf16[320,128]{1,0:T(8,128)(2,1)S(1)}, bf16[320,128]{1,0:T(8,128)(2,1)S(1)}, u32[]{:S(2)}, u32[]{:S(2)}) collective-permute-start(bf16[320,128]{1,0:T(8,128)(2,1)S(1)} %get-tuple-element.52), channel_id=1, source_target_pairs={{0,1},{1,0},{2,3},{3,2},{4,5},{5,4},{6,7},{7,6},{8,9},{9,8},{10,11... | collective-permute-start | bytes 245768 | tf_op jit(solution)/shard_map/ppermute | solution.py:347
  14.0 0.9 %collective-permute-done.4.got = bf16[320,128]{1,0:T(8,128)(2,1)S(1)} collective-permute-done((bf16[320,128]{1,0:T(8,128)(2,1)S(1)}, bf16[320,128]{1,0:T(8,128)(2,1)S(1)}, u32[]{:S(2)}, u32[]{:S(2)}) %collective-permute-start.4) | collective-permute-done | bytes 81952 | tf_op jit(solution)/shard_map/ppermute | solution.py:347
  14.9 1.6 %collective-permute-start.5 = (bf16[320,128]{1,0:T(8,128)(2,1)S(1)}, bf16[320,128]{1,0:T(8,128)(2,1)S(1)}, u32[]{:S(2)}, u32[]{:S(2)}) collective-permute-start(bf16[320,128]{1,0:T(8,128)(2,1)S(1)} %pad_maximum_fusion.1), channel_id=1, source_target_pairs={{0,16},{1,2},{2,1},{3,4},{4,3},{5,6},{6,5},{7,8},{8,7},{9,10},{10,... | collective-permute-start | bytes 245768 | tf_op jit(solution)/shard_map/ppermute | solution.py:350
  16.5 0.5 %collective-permute-start.6 = (bf16[96,128]{1,0:T(8,128)(2,1)S(1)}, bf16[96,128]{1,0:T(8,128)(2,1)S(1)}, u32[]{:S(2)}, u32[]{:S(2)}) collective-permute-start(bf16[96,128]{1,0:T(8,128)(2,1)S(1)} %pad_maximum_fusion.3), channel_id=1, source_target_pairs={{0,16},{1,4},{2,18},{3,6},{4,1},{5,8},{6,3},{7,10},{8,5},{9,12},{1... | collective-permute-start | bytes 73736 | tf_op jit(solution)/shard_map/ppermute | solution.py:351
  17.0 0.0 copy-done
  17.0 2.1 %shard_map.104 = (f32[512,512]{1,0:T(8,128)S(1)}, f32[512,384]{1,0:T(8,128)S(1)}, bf16[16,128]{1,0:T(8,128)(2,1)S(1)}) custom-call(f32[512,128]{1,0:T(8,128)S(1)} %get-tuple-element.33.column, f32[512,512]{1,0:T(8,128)S(1)} %copy-done, f32[512,512]{1,0:T(8,128)S(1)} %get-tuple-element.49.field, bf16[512,1536]{1,0:T(8,128)(2,1)S(1)} %get-tuple-element.50.stiffness, ...), custom_call_target="tpu_custom_call" | custom-call | flops 100000000 | bytes 100000 | tf_op jit(solution)/shard_map/pallas_call | solution.py:329
  19.1 0.3 %collective-permute-done.5.near = bf16[320,128]{1,0:T(8,128)(2,1)S(1)} collective-permute-done((bf16[320,128]{1,0:T(8,128)(2,1)S(1)}, bf16[320,128]{1,0:T(8,128)(2,1)S(1)}, u32[]{:S(2)}, u32[]{:S(2)}) %collective-permute-start.5) | collective-permute-done | bytes 81952 | tf_op jit(solution)/shard_map/ppermute | solution.py:350
  19.4 0.9 %collective-permute-done.6.far = bf16[96,128]{1,0:T(8,128)(2,1)S(1)} collective-permute-done((bf16[96,128]{1,0:T(8,128)(2,1)S(1)}, bf16[96,128]{1,0:T(8,128)(2,1)S(1)}, u32[]{:S(2)}, u32[]{:S(2)}) %collective-permute-start.6) | collective-permute-done | bytes 24608 | tf_op jit(solution)/shard_map/ppermute | solution.py:351
  20.4 0.1 collective-permute-start.7
  20.4 0.7 %shard_map.105.partial = f32[512,384]{1,0:T(8,128)S(1)} custom-call(bf16[512,768]{1,0:T(8,128)(2,1)S(1)} %get-tuple-element.39.picks, f32[512,384]{1,0:T(8,128)S(1)} %get-tuple-element.54.partial, f32[160,128]{1,0:T(8,128)S(1)} %get-tuple-element.55.face, bf16[512,160]{1,0:T(8,128)(2,1)S(1)} %get-tuple-element.56.element_hot, ...), custom_call_target="tpu_custom_call" | custom-call | flops 1000000000 | bytes 2043904 | tf_op jit(solution)/shard_map/pallas_call | solution.py:329
  21.1 0.5 %collective-permute-done.7.last = bf16[144,128]{1,0:T(8,128)(2,1)S(1)} collective-permute-done((bf16[144,128]{1,0:T(8,128)(2,1)S(1)}, bf16[144,128]{1,0:T(8,128)(2,1)S(1)}, u32[]{:S(2)}, u32[]{:S(2)}) %collective-permute-start.7) | collective-permute-done | bytes 36896 | tf_op jit(solution)/shard_map/ppermute | solution.py:360
  21.6 1.5 %shard_map.106 = f32[512,512]{1,0:T(8,128)} custom-call(bf16[384,512]{1,0:T(8,128)(2,1)S(1)} %get-tuple-element.37.lift, f32[512,512]{1,0:T(8,128)S(1)} %get-tuple-element.53.base, f32[512,384]{1,0:T(8,128)S(1)} %shard_map.105.partial, f32[512,384]{1,0:T(8,128)S(1)} %get-tuple-element.44.inflow, bf16[144,128]{1,0:T(8,128)(2,1)S(1)} %collective-permute-done.7.last, ...), custom_call_target="tpu_custom_call" | custom-call | flops 1000000000 | bytes 3198976 | tf_op jit(solution)/shard_map/pallas_call | solution.py:329
  (23 shorter events, 0.2 us)
Async XLA Ops:
  2.5 1.4 %collective-permute-start = (bf16[320,128]{1,0:T(8,128)(2,1)S(1)}, bf16[320,128]{1,0:T(8,128)(2,1)S(1)}, u32[]{:S(2)}, u32[]{:S(2)}) collective-permute-start(bf16[320,128]{1,0:T(8,128)(2,1)S(1)} %get-tuple-element.36), channel_id=1, source_target_pairs={{0,1},{1,0},{2,3},{3,2},{4,5},{5,4},{6,7},{7,6},{8,9},{9,8},{10,11... | collective-permute-start | bytes 245768 | tf_op jit(solution)/shard_map/ppermute | solution.py:347
  3.9 5.9 %collective-permute-start.1 = (bf16[320,128]{1,0:T(8,128)(2,1)S(1)}, bf16[320,128]{1,0:T(8,128)(2,1)S(1)}, u32[]{:S(2)}, u32[]{:S(2)}) collective-permute-start(bf16[320,128]{1,0:T(8,128)(2,1)S(1)} %pad_maximum_fusion), channel_id=1, source_target_pairs={{0,16},{1,2},{2,1},{3,4},{4,3},{5,6},{6,5},{7,8},{8,7},{9,10},{10,... | collective-permute-start | bytes 245768 | tf_op jit(solution)/shard_map/ppermute | solution.py:350
  6.9 3.8 %collective-permute-start.2 = (bf16[96,128]{1,0:T(8,128)(2,1)S(1)}, bf16[96,128]{1,0:T(8,128)(2,1)S(1)}, u32[]{:S(2)}, u32[]{:S(2)}) collective-permute-start(bf16[96,128]{1,0:T(8,128)(2,1)S(1)} %pad_maximum_fusion.2), channel_id=1, source_target_pairs={{0,16},{1,4},{2,18},{3,6},{4,1},{5,8},{6,3},{7,10},{8,5},{9,12},{1... | collective-permute-start | bytes 73736 | tf_op jit(solution)/shard_map/ppermute | solution.py:351
  10.7 1.3 %collective-permute-start.3 = (bf16[144,128]{1,0:T(8,128)(2,1)S(1)}, bf16[144,128]{1,0:T(8,128)(2,1)S(1)}, u32[]{:S(2)}, u32[]{:S(2)}) collective-permute-start(bf16[144,128]{1,0:T(8,128)(2,1)S(1)} %constant_dynamic-update-slice_fusion.last), channel_id=1, source_target_pairs={{0,1},{1,0},{2,3},{3,2},{4,5},{5,4},{6,7},{7,6},{8,9},{9,8},{10,11... | collective-permute-start | bytes 110600 | tf_op jit(solution)/shard_map/ppermute | solution.py:360
  12.0 5.0 %copy-start = (f32[512,512]{1,0:T(8,128)S(1)}, f32[512,512]{1,0:T(8,128)}, u32[]{:S(2)}) copy-start(f32[512,512]{1,0:T(8,128)} %state.1) | copy-start | bytes 3145732
  13.6 1.3 %collective-permute-start.4 = (bf16[320,128]{1,0:T(8,128)(2,1)S(1)}, bf16[320,128]{1,0:T(8,128)(2,1)S(1)}, u32[]{:S(2)}, u32[]{:S(2)}) collective-permute-start(bf16[320,128]{1,0:T(8,128)(2,1)S(1)} %get-tuple-element.52), channel_id=1, source_target_pairs={{0,1},{1,0},{2,3},{3,2},{4,5},{5,4},{6,7},{7,6},{8,9},{9,8},{10,11... | collective-permute-start | bytes 245768 | tf_op jit(solution)/shard_map/ppermute | solution.py:347
  14.9 4.5 %collective-permute-start.5 = (bf16[320,128]{1,0:T(8,128)(2,1)S(1)}, bf16[320,128]{1,0:T(8,128)(2,1)S(1)}, u32[]{:S(2)}, u32[]{:S(2)}) collective-permute-start(bf16[320,128]{1,0:T(8,128)(2,1)S(1)} %pad_maximum_fusion.1), channel_id=1, source_target_pairs={{0,16},{1,2},{2,1},{3,4},{4,3},{5,6},{6,5},{7,8},{8,7},{9,10},{10,... | collective-permute-start | bytes 245768 | tf_op jit(solution)/shard_map/ppermute | solution.py:350
  16.5 3.8 %collective-permute-start.6 = (bf16[96,128]{1,0:T(8,128)(2,1)S(1)}, bf16[96,128]{1,0:T(8,128)(2,1)S(1)}, u32[]{:S(2)}, u32[]{:S(2)}) collective-permute-start(bf16[96,128]{1,0:T(8,128)(2,1)S(1)} %pad_maximum_fusion.3), channel_id=1, source_target_pairs={{0,16},{1,4},{2,18},{3,6},{4,1},{5,8},{6,3},{7,10},{8,5},{9,12},{1... | collective-permute-start | bytes 73736 | tf_op jit(solution)/shard_map/ppermute | solution.py:351
  20.4 1.3 %collective-permute-start.7 = (bf16[144,128]{1,0:T(8,128)(2,1)S(1)}, bf16[144,128]{1,0:T(8,128)(2,1)S(1)}, u32[]{:S(2)}, u32[]{:S(2)}) collective-permute-start(bf16[144,128]{1,0:T(8,128)(2,1)S(1)} %constant_dynamic-update-slice_fusion.5.last), channel_id=1, source_target_pairs={{0,1},{1,0},{2,3},{3,2},{4,5},{5,4},{6,7},{7,6},{8,9},{9,8},{10,11... | collective-permute-start | bytes 110600 | tf_op jit(solution)/shard_map/ppermute | solution.py:360

commit v8 on v7

--- a/solution.py
+++ b/solution.py
@@ -62,7 +62,7 @@
     return transposed(jnp.concatenate(rows, axis=0))
 
 
-def send(traces, source_hot, column, projection, first_out, own_out, blocks):
+def send(traces, source_hot, column, projection, first_out, rim_out, own_out, blocks, with_codes):
     elements, width = traces.shape
     slots = column.shape[0]
     capacity = slots // 8
@@ -82,7 +82,9 @@
     for t in range(4):
         folded = jnp.where(half + 2 * t == kind, every[:, 128 * t : 128 * t + 128], folded)
     piece = folded + pltpu.roll(folded, 64, 1)
-    blocks[...] = jnp.where(lane < 64, piece, column[...]).astype(bf16)
+    if with_codes:
+        piece = jnp.where(lane < 64, piece, column[...])
+    blocks[...] = piece.astype(bf16)
 
     def block(at_first, at_second):
         index = at_first + core * (at_second - at_first)
@@ -94,14 +96,25 @@
         cut = slice(128 * t, 128 * t + 128)
         rows = slice(rim * t, rim * t + rim)
         first_out[rows, :] = traces[pl.ds(final_at, rim), cut]
-        own_out[rows, :] = traces[pl.ds(other_at, rim), cut]
+        rim_out[rows, :] = traces[pl.ds(other_at, rim), cut]
     at = 3 * rim
     there = [(4, 3), (5, 1), (6, 2), (7, 0)]
     here = [(2, 4), (3, 5), (0, 6), (1, 7)]
-    for i in range(4):
-        rows = slice(at + capacity * i, at + capacity * i + capacity)
-        first_out[rows, :] = block(*there[i])
-        own_out[rows, :] = block(*here[i])
+    if with_codes:
+        for i in range(4):
+            rows = slice(at + capacity * i, at + capacity * i + capacity)
+            first_out[rows, :] = block(*there[i])
+            own_out[rows, :] = block(*here[i])
+        return
+    low = lanes((capacity, 128)) < 64
+
+    def pair(a, b):
+        return jnp.where(low, block(*a), block(*b))
+
+    first_out[at : at + capacity, :] = pair(there[0], there[3])
+    first_out[at + capacity :, :] = pair(there[1], there[2])
+    own_out[0:capacity, :] = pair(here[0], here[1])
+    own_out[capacity:, :] = pair(here[2], here[3])
 
 
 def start_kernel(
@@ -132,7 +145,7 @@
         cut = slice(i * part, i * part + part)
         traces[cut, :] = dot(state[cut, :].astype(bf16), trace_map[...]).astype(bf16)
     copies[8].wait()
-    send(traces, source_hot[...], column, projection, first_out, own_out, blocks)
+    send(traces, source_hot[...], column, projection, first_out, own_out, own_out, blocks, True)
 
 
 def element_columns(velocity, levels, neighbours):
@@ -168,7 +181,11 @@
         partial_out[:, 128 * t : 128 * t + 128] = near - tile.astype(f32)
 
 
-def local_kernel(stiffness_in, lift_in, column, state, traces, got, stiffness, lift, base, partial, inflow, picks, token, sems):
+def own_kernel(column, traces, partial):
+    own_part(column[...], traces, partial)
+
+
+def local_kernel(stiffness_in, lift_in, column, state, got, stiffness, lift, base, inflow, picks, token, sems):
     token[...] = got[0:16, :]
     elements, modes = state.shape
     rim = elements // 8
@@ -179,7 +196,6 @@
     for copy in copies:
         copy.start()
     columns = column[...]
-    own_part(columns, traces, partial)
     low = lanes((elements, 128)) < 64
     for t in range(3):
         speed = columns[:, t : t + 1]
@@ -226,6 +242,28 @@
     return arrived[...]
 
 
+def in_both(pieces, which):
+    half = jnp.where(lanes(pieces.shape) < 64, 0, 1)
+    kept = jnp.where(half == which, pieces.astype(f32), 0.0)
+    return kept + pltpu.roll(kept, 64, 1)
+
+
+def direct_pairs(got, near, far, arrived):
+    capacity = arrived.shape[0] // 5
+    at = 6 * capacity
+    core = lax.axis_index("pair")
+    blocks = [
+        (got[at : at + capacity, :], 0),
+        (near[0:capacity, :], core),
+        (near[capacity : 2 * capacity, :], core),
+        (far[0:capacity, :], core),
+        (far[capacity : 2 * capacity, :], 1),
+    ]
+    for i, (block, which) in enumerate(blocks):
+        arrived[capacity * i : capacity * i + capacity, :] = in_both(block, which)
+    return arrived[...]
+
+
 def targets(pieces, elements):
     face_of = jnp.where(rows_of((128, 128)) == 66, 1.0, 0.0).astype(bf16)
     face = dot(pieces, face_of) - 1.0
@@ -236,21 +274,19 @@
     return face, jnp.where(match, 1.0, 0.0).astype(bf16)
 
 
-def mortar_term(pieces, face, element_hot, t):
-    half = jnp.where(lanes(pieces.shape) < 64, 0.0, 1.0)
-    plain = jnp.where(half == 0.0, pieces.astype(f32), 0.0)
-    both = plain + pltpu.roll(plain, 64, 1)
+def mortar_term(both, face, element_hot, t):
+    half = jnp.where(lanes(both.shape) < 64, 0.0, 1.0)
     return dot(element_hot, jnp.where(half + 2 * t == face, both, 0.0).astype(bf16))
 
 
-def add_direct(picks, partial, got, near, pieces, face, element_hot, total):
+def add_direct(picks, partial, got, near, both, face, element_hot, total):
     rim = picks.shape[1] // 12
     for t in range(3):
         cut = slice(128 * t, 128 * t + 128)
         rows = slice(rim * t, rim * t + rim)
         window = jnp.concatenate([got[rows, :], near[rows, :]], axis=0)
         conforming = dot(picks[:, 4 * rim * t : 4 * rim * t + 4 * rim], swapped(window))
-        total[:, cut] = partial[:, cut] + conforming + mortar_term(pieces, face, element_hot, t)
+        total[:, cut] = partial[:, cut] + conforming + mortar_term(both, face, element_hot, t)
 
 
 def direct_kernel(picks, partial, got, near, far, last, total, face_out, element_hot_out, arrived):
@@ -258,42 +294,46 @@
     face, element_hot = targets(pieces, partial.shape[0])
     face_out[...] = face
     element_hot_out[...] = element_hot
-    add_direct(picks, partial, got, near, pieces, face, element_hot, total)
-
-
-def second_direct_kernel(picks, partial, face, element_hot, got, near, far, last, total, arrived):
-    pieces = direct_pieces(got, near, far, arrived)
-    add_direct(picks, partial, got, near, pieces, face[...], element_hot[...], total)
-
-
-def fluxes(pieces, face, element_hot, partial, inflow):
+    add_direct(picks, partial, got, near, in_both(pieces, 0), face, element_hot, total)
+
+
+def second_direct_kernel(picks, partial, face, element_hot, got, rim, near, far, last, total, arrived):
+    both = direct_pairs(got, near, far, arrived)
+    add_direct(picks, partial, got, rim, both, face[...], element_hot[...], total)
+
+
+def fluxes(both, face, element_hot, partial, inflow):
     parts = []
     for t in range(3):
         cut = slice(128 * t, 128 * t + 128)
-        total = partial[:, cut] + mortar_term(pieces, face, element_hot, t)
+        total = partial[:, cut] + mortar_term(both, face, element_hot, t)
         parts.append((inflow[:, cut] * total).astype(bf16))
     return jnp.concatenate(parts, axis=1)
 
 
 def middle_kernel(
     lift, base, partial, inflow, last, trace_map, projection, source_hot, column,
-    field, traces, first_out, own_out, face_out, element_hot_out, blocks
+    field, traces, first_out, rim_out, own_out, face_out, element_hot_out, blocks
 ):
     elements = base.shape[0]
     pieces = last[0 : face_out.shape[0], :]
     face, element_hot = targets(pieces, elements)
     face_out[...] = face
     element_hot_out[...] = element_hot
-    flux = fluxes(pieces, face, element_hot, partial, inflow)
+    flux = fluxes(in_both(pieces, 0), face, element_hot, partial, inflow)
     new = base[...] + time_step * dot(flux, lift[...])
     field[...] = new
     traces[...] = dot(new.astype(bf16), trace_map[...]).astype(bf16)
-    send(traces, source_hot[...], column, projection, first_out, own_out, blocks)
+    send(traces, source_hot[...], column, projection, first_out, rim_out, own_out, blocks, False)
 
 
 def end_kernel(lift, base, partial, inflow, last, face, element_hot, field, result, sems):
     elements = base.shape[0]
-    flux = fluxes(last[0 : face.shape[0], :], face[...], element_hot[...], partial, inflow)
+    capacity = face.shape[0] // 3
+    core = lax.axis_index("pair")
+    far = last[pl.ds(pl.multiple_of((3 - core) * capacity, capacity), capacity), :]
+    both = in_both(jnp.concatenate([last[0 : 2 * capacity, :], far], axis=0), core)
+    flux = fluxes(both, face[...], element_hot[...], partial, inflow)
     part = elements // 4
     copies = []
     for i in range(4):
@@ -337,26 +377,39 @@
     )(*operands)
 
 
-def exchange(first, own, core, capacity, local, direct):
+def exchange(first, rim, own, core, capacity, local, direct):
     axes = ("groups",) + CURVE
     groups, count = lax.axis_size("groups"), lax.axis_size(CURVE)
     cores = paired(groups, count, 1, lambda s: s % 2 == 0)
     chips = paired(groups, count, 1, lambda s: s % 2 == 1)
     far_chips = paired(groups, count, 3, lambda s: s % 2 == 1)
-    at = own.shape[0] - 4 * capacity
     got = lax.ppermute(first, axes, cores)
-    near = jnp.concatenate([own[: at + 2 * capacity], got[at + capacity : at + 3 * capacity]], axis=0)
-    far = jnp.concatenate([own[at + 2 * capacity :], got[at + 3 * capacity :]], axis=0)
+    with_codes = rim is None
+    at = own.shape[0] - 4 * capacity if with_codes else 0
+
+    def either(x, at_first, at_second):
+        return jnp.where(core == 0, x[at_first : at_first + capacity], x[at_second : at_second + capacity])
+
+    if with_codes:
+        near = jnp.concatenate([own[: at + 2 * capacity], got[at + capacity : at + 3 * capacity]], axis=0)
+        far = jnp.concatenate([own[at + 2 * capacity :], got[at + 3 * capacity :]], axis=0)
+    else:
+        rim = lax.ppermute(rim, axes, chips)
+        theirs = got.shape[0] - 2 * capacity
+        near = jnp.concatenate([own[:capacity], got[theirs + capacity :]], axis=0)
+        far = jnp.concatenate([own[capacity:], got[theirs : theirs + capacity]], axis=0)
     near = lax.ppermute(near, axes, chips)
     far = lax.ppermute(far, axes, far_chips)
     *results, token = local(got)
-
-    def theirs(x):
-        return jnp.where(core == 0, x[capacity : 2 * capacity], x[:capacity])
-
-    parts = [theirs(near[at : at + 2 * capacity]), theirs(near[at + 2 * capacity :]), theirs(far[: 2 * capacity]), theirs(far[capacity:])]
+    if with_codes:
+        parts = [either(near, at + capacity, at + 2 * capacity), either(near, at + 3 * capacity, at)]
+        parts += [either(far, capacity, 0), either(far, 0, capacity)]
+    else:
+        parts = [either(near, at, at + capacity), either(near, at + capacity, at)]
+        parts += [either(far, 0, capacity), either(far, capacity, 0)]
     last = jnp.concatenate(parts + [token], axis=0)
-    totals = direct(results, got, near, far, last)
+    arrived = (got, near, far) if with_codes else (got, rim, near, far)
+    totals = direct(results, *arrived, last)
     return lax.ppermute(last, axes, cores), totals, results
 
 
@@ -376,10 +429,13 @@
     def like(x):
         return array(x.shape, x.dtype)
 
-    sent = [
+    message = array((3 * rim + 4 * capacity, 128), bf16)
+    sent = [array((elements, width), bf16), message, message]
+    second_sent = [
         array((elements, width), bf16),
-        array((3 * rim + 4 * capacity, 128), bf16),
-        array((3 * rim + 4 * capacity, 128), bf16),
+        array((3 * rim + 2 * capacity, 128), bf16),
+        array((3 * rim, 128), bf16),
+        array((2 * capacity, 128), bf16),
     ]
     whole = array((elements, modes), f32)
     faces = array((elements, width), f32)
@@ -402,14 +458,16 @@
         (),
     )
 
+    partial = call(own_kernel, [faces], [], 10**8, (), (element_column, traces))[0]
+
     def local(got):
         return call(
             local_kernel,
-            [like(stiffness), like(lift), whole, faces, faces, array((elements, 12 * rim), bf16), mark],
+            [like(stiffness), like(lift), whole, faces, array((elements, 12 * rim), bf16), mark],
             [pltpu.SemaphoreType.DMA((2,))],
             10**8,
             (stiffness, lift),
-            (element_column, near_state, traces, got),
+            (element_column, near_state, got),
         )
 
     def direct(results, *arrived):
@@ -419,19 +477,19 @@
             [vmem((5 * capacity, 128), bf16)],
             10**9,
             (),
-            (results[5], results[3], *arrived),
+            (results[4], partial, *arrived),
         )
 
-    last, (partial, *direct_targets), (near_stiffness, near_lift, base, _, inflow, picks) = exchange(
-        first, own, core, capacity, local, direct
+    last, (partial, *direct_targets), (stiffness, lift, base, inflow, picks) = exchange(
+        first, None, own, core, capacity, local, direct
     )
-    field, traces, first, own, face, element_hot = call(
+    field, traces, first, rims, own, face, element_hot = call(
         middle_kernel,
-        [whole] + sent + [array((3 * capacity, 128), f32), array((elements, 3 * capacity), bf16)],
+        [whole] + second_sent + [array((3 * capacity, 128), f32), array((elements, 3 * capacity), bf16)],
         [blocks],
         10**9,
         (),
-        (near_lift, base, partial, inflow, last, trace_map, projection, source_hot, column),
+        (lift, base, partial, inflow, last, trace_map, projection, source_hot, column),
     )
 
     def second_local(got):
@@ -441,27 +499,29 @@
             [],
             10**8,
             (),
-            (element_column, state, field, near_stiffness, traces, got),
+            (element_column, state, field, stiffness, traces, got),
         )
 
     def second_direct(results, *arrived):
         return call(
             second_direct_kernel,
             [faces],
-            [vmem((5 * capacity, 128), bf16)],
+            [vmem((5 * capacity, 128), f32)],
             10**9,
             (),
             (picks, results[1], *direct_targets, *arrived),
         )
 
-    last, (partial,), (base, _) = exchange(first, own, core, capacity, second_local, second_direct)
+    last, (partial,), (base, _) = exchange(
+        first, rims, own, core, capacity, second_local, second_direct
+    )
     return call(
         end_kernel,
         [whole],
         [vmem((elements, modes), f32), pltpu.SemaphoreType.DMA((4,))],
         10**9,
         (),
-        (near_lift, base, partial, inflow, last, face, element_hot),
+        (lift, base, partial, inflow, last, face, element_hot),
         out_space=pl.ANY,
     )[0]
 

time: 23.3 us -> 23 us (0.987)
  waiting for transfers between devices: 4.6 us -> 2.14 us
  starting transfers between devices: 6.56 us -> 7.99 us
  Pallas kernels: 11.7 us -> 12.4 us
    ppermute x2, waiting for transfers between devices: 1.82 us -> 0.01 us  [exchange(): got = lax.ppermute(first, axes, cores)]
    ppermute x0 -> x1, starting transfers between devices: none -> 1.52 us  [exchange(): rim = lax.ppermute(rim, axes, chips)]
    ppermute x2, starting transfers between devices: 4.51 us -> 3.55 us  [exchange(): near = lax.ppermute(near, axes, chips)]
    pallas_call x7 -> x8, Pallas kernels: 11.7 us -> 12.4 us  [call(): pl.pallas_call(kernel, out_shape=out_shape, in_specs=specs, out_specs=[pl...]
    ppermute x2, starting transfers between devices: 0.6 us -> 1.28 us  [exchange(): far = lax.ppermute(far, axes, far_chips)]
    ppermute x2, waiting for transfers between devices: 0.35 us -> 0.01 us  [exchange(): near = lax.ppermute(near, axes, chips)]
    ppermute x2, starting transfers between devices: 0.52 us -> 0.77 us  [exchange(): return (lax.ppermute(last, axes, cores), totals, results)]
    ppermute x2, waiting for transfers between devices: 0.69 us -> 0.44 us  [exchange(): return (lax.ppermute(last, axes, cores), totals, results)]
  transfers between devices with their start and end apart: 8 -> 9, of which waited for: 7 -> 4; matrix products, arithmetic and copies ran while one was open for 0% -> 0% of each run, Pallas kernels for 27% -> 31%
where the time goes in v8:
time: 23 us; the launch traced here: 22.9 us
  Pallas kernels  12.4 us (54%)
  starting transfers between devices  7.99 us (35%)
  waiting for transfers between devices  2.14 us (9%)
    pallas_call x8, Pallas kernels, call(): pl.pallas_call(kernel, out_shape=out_shape, in_specs=specs, out_specs=[pl...  12.4 us
    ppermute x2, starting transfers between devices, exchange(): near = lax.ppermute(near, axes, chips)  3.55 us
    ppermute x2, waiting for transfers between devices, exchange(): far = lax.ppermute(far, axes, far_chips)  1.68 us
    ppermute x1, starting transfers between devices, exchange(): rim = lax.ppermute(rim, axes, chips)  1.52 us
    ppermute x2, starting transfers between devices, exchange(): far = lax.ppermute(far, axes, far_chips)  1.28 us
    ppermute x2, starting transfers between devices, exchange(): got = lax.ppermute(first, axes, cores)  0.86 us
    ppermute x2, starting transfers between devices, exchange(): return (lax.ppermute(last, axes, cores), totals, results)  0.77 us
  transfers between devices with their start and end apart: 9, of which 4 were waited for; matrix products, arithmetic and copies ran while one was open for 0% of the time, Pallas kernels for 31%

profile of v8, /device:TPU:0, one launch (start us, length us, event | category | flops | bytes accessed | tf_op | source)
XLA Modules:
  0.0 22.9 jit_solution(14782455860100578838)
XLA Ops:
  0.0 2.5 %shard_map.100 = (f32[512,512]{1,0:T(8,128)S(1)}, bf16[512,384]{1,0:T(8,128)(2,1)S(1)}, bf16[64,512]{1,0:T(8,128)(2,1)S(1)}, bf16[512,384]{1,0:T(8,128)(2,1)S(1)...) custom-call(f32[512,512]{1,0:T(8,128)} %state.1, ...), custom_call_target="tpu_custom_call" | custom-call | flops 200000000 | bytes 1531936 | tf_op jit(solution)/shard_map/pallas_call | solution.py:369
  2.5 0.5 %collective-permute-start = (bf16[320,128]{1,0:T(8,128)(2,1)S(1)}, bf16[320,128]{1,0:T(8,128)(2,1)S(1)}, u32[]{:S(2)}, u32[]{:S(2)}) collective-permute-start(bf16[320,128]{1,0:T(8,128)(2,1)S(1)} %get-tuple-element.35), channel_id=1, source_target_pairs={{0,1},{1,0},{2,3},{3,2},{4,5},{5,4},{6,7},{7,6},{8,9},{9,8},{10,11... | collective-permute-start | bytes 245768 | tf_op jit(solution)/shard_map/ppermute | solution.py:386
  3.0 1.1 %shard_map.102.partial = f32[512,384]{1,0:T(8,128)S(1)} custom-call(f32[512,128]{1,0:T(8,128)S(1)} %get-tuple-element.33.column, bf16[512,384]{1,0:T(8,128)(2,1)S(1)} %get-tuple-element.39.traces), custom_call_target="tpu_custom_call" | custom-call | flops 100000000 | bytes 100000 | tf_op jit(solution)/shard_map/pallas_call | solution.py:369
  4.2 0.0 collective-permute-done.got
  4.2 2.7 %collective-permute-start.1 = (bf16[320,128]{1,0:T(8,128)(2,1)S(1)}, bf16[320,128]{1,0:T(8,128)(2,1)S(1)}, u32[]{:S(2)}, u32[]{:S(2)}) collective-permute-start(bf16[320,128]{1,0:T(8,128)(2,1)S(1)} %pad_maximum_fusion), channel_id=1, source_target_pairs={{0,16},{1,2},{2,1},{3,4},{4,3},{5,6},{6,5},{7,8},{8,7},{9,10},{10,... | collective-permute-start | bytes 245768 | tf_op jit(solution)/shard_map/ppermute | solution.py:401
  6.9 0.1 collective-permute-start.2
  7.0 2.4 %shard_map.101 = (bf16[512,1536]{1,0:T(8,128)(2,1)S(1)}, bf16[384,512]{1,0:T(8,128)(2,1)S(1)}, f32[512,512]{1,0:T(8,128)S(1)}, f32[512,384]{1,0:T(8,128)S(1)}, b...) custom-call(bf16[512,1536]{1,0:T(8,128)(2,1)} %stiffness_in.1, bf16[384,512]{1,0:T(8,128)(2,1)} %lift_in.1, ...), custom_call_target="tpu_custom_call" | custom-call | flops 100000000 | bytes 100000 | tf_op jit(solution)/shard_map/pallas_call | solution.py:369
  9.4 0.0 collective-permute-done.1.near
  9.5 1.2 %collective-permute-done.2.far = bf16[96,128]{1,0:T(8,128)(2,1)S(1)} collective-permute-done((bf16[96,128]{1,0:T(8,128)(2,1)S(1)}, bf16[96,128]{1,0:T(8,128)(2,1)S(1)}, u32[]{:S(2)}, u32[]{:S(2)}) %collective-permute-start.2) | collective-permute-done | bytes 24608 | tf_op jit(solution)/shard_map/ppermute | solution.py:402
  10.7 0.3 %collective-permute-start.3 = (bf16[144,128]{1,0:T(8,128)(2,1)S(1)}, bf16[144,128]{1,0:T(8,128)(2,1)S(1)}, u32[]{:S(2)}, u32[]{:S(2)}) collective-permute-start(bf16[144,128]{1,0:T(8,128)(2,1)S(1)} %constant_dynamic-update-slice_fusion.last), channel_id=1, source_target_pairs={{0,1},{1,0},{2,3},{3,2},{4,5},{5,4},{6,7},{7,6},{8,9},{9,8},{10,11... | collective-permute-start | bytes 110600 | tf_op jit(solution)/shard_map/ppermute | solution.py:413
  11.1 0.7 %shard_map.103 = (f32[512,384]{1,0:T(8,128)S(1)}, f32[160,128]{1,0:T(8,128)S(1)}, bf16[512,160]{1,0:T(8,128)(2,1)S(1)}) custom-call(bf16[512,768]{1,0:T(8,128)(2,1)S(1)} %get-tuple-element.38.picks, f32[512,384]{1,0:T(8,128)S(1)} %shard_map.102.partial, bf16[320,128]{1,0:T(8,128)(2,1)S(1)} %collective-permute-done.got, ...), custom_call_target="tpu_custom_call" | custom-call | flops 1000000000 | bytes 1798144 | tf_op jit(solution)/shard_map/pallas_call | solution.py:369
  11.8 0.2 %collective-permute-done.3.last = bf16[144,128]{1,0:T(8,128)(2,1)S(1)} collective-permute-done((bf16[144,128]{1,0:T(8,128)(2,1)S(1)}, bf16[144,128]{1,0:T(8,128)(2,1)S(1)}, u32[]{:S(2)}, u32[]{:S(2)}) %collective-permute-start.3) | collective-permute-done | bytes 36896 | tf_op jit(solution)/shard_map/ppermute | solution.py:413
  12.0 1.5 %shard_map.104 = (f32[512,512]{1,0:T(8,128)S(1)}, bf16[512,384]{1,0:T(8,128)(2,1)S(1)}, bf16[256,128]{1,0:T(8,128)(2,1)S(1)}, bf16[192,128]{1,0:T(8,128)(2,1)S(1...) custom-call(bf16[384,512]{1,0:T(8,128)(2,1)S(1)} %get-tuple-element.36.lift, ...), custom_call_target="tpu_custom_call" | custom-call | flops 1000000000 | bytes 3903488 | tf_op jit(solution)/shard_map/pallas_call | solution.py:369
  13.5 0.3 %collective-permute-start.4 = (bf16[256,128]{1,0:T(8,128)(2,1)S(1)}, bf16[256,128]{1,0:T(8,128)(2,1)S(1)}, u32[]{:S(2)}, u32[]{:S(2)}) collective-permute-start(bf16[256,128]{1,0:T(8,128)(2,1)S(1)} %get-tuple-element.51), channel_id=1, source_target_pairs={{0,1},{1,0},{2,3},{3,2},{4,5},{5,4},{6,7},{7,6},{8,9},{9,8},{10,11... | collective-permute-start | bytes 196616 | tf_op jit(solution)/shard_map/ppermute | solution.py:386
  13.9 1.5 %collective-permute-start.5 = (bf16[192,128]{1,0:T(8,128)(2,1)S(1)}, bf16[192,128]{1,0:T(8,128)(2,1)S(1)}, u32[]{:S(2)}, u32[]{:S(2)}) collective-permute-start(bf16[192,128]{1,0:T(8,128)(2,1)S(1)} %get-tuple-element.56), channel_id=1, source_target_pairs={{0,16},{1,2},{2,1},{3,4},{4,3},{5,6},{6,5},{7,8},{8,7},{9,10},{10,... | collective-permute-start | bytes 147464 | tf_op jit(solution)/shard_map/ppermute | solution.py:397
  15.4 0.9 %collective-permute-start.6 = (bf16[64,128]{1,0:T(8,128)(2,1)S(1)}, bf16[64,128]{1,0:T(8,128)(2,1)S(1)}, u32[]{:S(2)}, u32[]{:S(2)}) collective-permute-start(bf16[64,128]{1,0:T(8,128)(2,1)S(1)} %pad_maximum_fusion.2), channel_id=1, source_target_pairs={{0,16},{1,2},{2,1},{3,4},{4,3},{5,6},{6,5},{7,8},{8,7},{9,10},{10,... | collective-permute-start | bytes 49160 | tf_op jit(solution)/shard_map/ppermute | solution.py:401
  16.3 1.2 %collective-permute-start.7 = (bf16[64,128]{1,0:T(8,128)(2,1)S(1)}, bf16[64,128]{1,0:T(8,128)(2,1)S(1)}, u32[]{:S(2)}, u32[]{:S(2)}) collective-permute-start(bf16[64,128]{1,0:T(8,128)(2,1)S(1)} %pad_maximum_fusion.3), channel_id=1, source_target_pairs={{0,16},{1,4},{2,18},{3,6},{4,1},{5,8},{6,3},{7,10},{8,5},{9,12},{1... | collective-permute-start | bytes 49160 | tf_op jit(solution)/shard_map/ppermute | solution.py:402
  17.5 2.0 %shard_map.105 = (f32[512,512]{1,0:T(8,128)S(1)}, f32[512,384]{1,0:T(8,128)S(1)}, bf16[16,128]{1,0:T(8,128)(2,1)S(1)}) custom-call(f32[512,128]{1,0:T(8,128)S(1)} %get-tuple-element.33.column, f32[512,512]{1,0:T(8,128)S(1)} %copy-done, f32[512,512]{1,0:T(8,128)S(1)} %get-tuple-element.48.field, bf16[512,1536]{1,0:T(8,128)(2,1)S(1)} %get-tuple-element.49.stiffness, ...), custom_call_target="tpu_custom_call" | custom-call | flops 100000000 | bytes 100000 | tf_op jit(solution)/shard_map/pallas_call | solution.py:369
  19.5 0.0 collective-permute-done.6.near
  19.6 0.4 %collective-permute-done.7.far = bf16[64,128]{1,0:T(8,128)(2,1)S(1)} collective-permute-done((bf16[64,128]{1,0:T(8,128)(2,1)S(1)}, bf16[64,128]{1,0:T(8,128)(2,1)S(1)}, u32[]{:S(2)}, u32[]{:S(2)}) %collective-permute-start.7) | collective-permute-done | bytes 16416 | tf_op jit(solution)/shard_map/ppermute | solution.py:402
  20.1 0.4 %collective-permute-start.8 = (bf16[144,128]{1,0:T(8,128)(2,1)S(1)}, bf16[144,128]{1,0:T(8,128)(2,1)S(1)}, u32[]{:S(2)}, u32[]{:S(2)}) collective-permute-start(bf16[144,128]{1,0:T(8,128)(2,1)S(1)} %constant_dynamic-update-slice_fusion.5.last), channel_id=1, source_target_pairs={{0,1},{1,0},{2,3},{3,2},{4,5},{5,4},{6,7},{7,6},{8,9},{9,8},{10,11... | collective-permute-start | bytes 110600 | tf_op jit(solution)/shard_map/ppermute | solution.py:413
  20.5 0.6 %shard_map.106.partial = f32[512,384]{1,0:T(8,128)S(1)} custom-call(bf16[512,768]{1,0:T(8,128)(2,1)S(1)} %get-tuple-element.38.picks, f32[512,384]{1,0:T(8,128)S(1)} %get-tuple-element.53.partial, f32[160,128]{1,0:T(8,128)S(1)} %get-tuple-element.54.face, bf16[512,160]{1,0:T(8,128)(2,1)S(1)} %get-tuple-element.55.element_hot, ...), custom_call_target="tpu_custom_call" | custom-call | flops 1000000000 | bytes 2002944 | tf_op jit(solution)/shard_map/pallas_call | solution.py:369
  21.2 0.2 collective-permute-done.8.last
  21.4 1.5 %shard_map.107 = f32[512,512]{1,0:T(8,128)} custom-call(bf16[384,512]{1,0:T(8,128)(2,1)S(1)} %get-tuple-element.36.lift, f32[512,512]{1,0:T(8,128)S(1)} %get-tuple-element.52.base, f32[512,384]{1,0:T(8,128)S(1)} %shard_map.106.partial, f32[512,384]{1,0:T(8,128)S(1)} %get-tuple-element.43.inflow, bf16[144,128]{1,0:T(8,128)(2,1)S(1)} %collective-permute-done.8.last, ...), custom_call_target="tpu_custom_call" | custom-call | flops 1000000000 | bytes 3198976 | tf_op jit(solution)/shard_map/pallas_call | solution.py:369
  (24 shorter events, 0.2 us)
Async XLA Ops:
  2.5 1.7 %collective-permute-start = (bf16[320,128]{1,0:T(8,128)(2,1)S(1)}, bf16[320,128]{1,0:T(8,128)(2,1)S(1)}, u32[]{:S(2)}, u32[]{:S(2)}) collective-permute-start(bf16[320,128]{1,0:T(8,128)(2,1)S(1)} %get-tuple-element.35), channel_id=1, source_target_pairs={{0,1},{1,0},{2,3},{3,2},{4,5},{5,4},{6,7},{7,6},{8,9},{9,8},{10,11... | collective-permute-start | bytes 245768 | tf_op jit(solution)/shard_map/ppermute | solution.py:386
  4.2 5.2 %collective-permute-start.1 = (bf16[320,128]{1,0:T(8,128)(2,1)S(1)}, bf16[320,128]{1,0:T(8,128)(2,1)S(1)}, u32[]{:S(2)}, u32[]{:S(2)}) collective-permute-start(bf16[320,128]{1,0:T(8,128)(2,1)S(1)} %pad_maximum_fusion), channel_id=1, source_target_pairs={{0,16},{1,2},{2,1},{3,4},{4,3},{5,6},{6,5},{7,8},{8,7},{9,10},{10,... | collective-permute-start | bytes 245768 | tf_op jit(solution)/shard_map/ppermute | solution.py:401
  6.9 3.8 %collective-permute-start.2 = (bf16[96,128]{1,0:T(8,128)(2,1)S(1)}, bf16[96,128]{1,0:T(8,128)(2,1)S(1)}, u32[]{:S(2)}, u32[]{:S(2)}) collective-permute-start(bf16[96,128]{1,0:T(8,128)(2,1)S(1)} %pad_maximum_fusion.1), channel_id=1, source_target_pairs={{0,16},{1,4},{2,18},{3,6},{4,1},{5,8},{6,3},{7,10},{8,5},{9,12},{1... | collective-permute-start | bytes 73736 | tf_op jit(solution)/shard_map/ppermute | solution.py:402
  10.7 1.3 %collective-permute-start.3 = (bf16[144,128]{1,0:T(8,128)(2,1)S(1)}, bf16[144,128]{1,0:T(8,128)(2,1)S(1)}, u32[]{:S(2)}, u32[]{:S(2)}) collective-permute-start(bf16[144,128]{1,0:T(8,128)(2,1)S(1)} %constant_dynamic-update-slice_fusion.last), channel_id=1, source_target_pairs={{0,1},{1,0},{2,3},{3,2},{4,5},{5,4},{6,7},{7,6},{8,9},{9,8},{10,11... | collective-permute-start | bytes 110600 | tf_op jit(solution)/shard_map/ppermute | solution.py:413
  12.0 5.5 %copy-start = (f32[512,512]{1,0:T(8,128)S(1)}, f32[512,512]{1,0:T(8,128)}, u32[]{:S(2)}) copy-start(f32[512,512]{1,0:T(8,128)} %state.1) | copy-start | bytes 3145732
  13.5 1.9 %collective-permute-start.4 = (bf16[256,128]{1,0:T(8,128)(2,1)S(1)}, bf16[256,128]{1,0:T(8,128)(2,1)S(1)}, u32[]{:S(2)}, u32[]{:S(2)}) collective-permute-start(bf16[256,128]{1,0:T(8,128)(2,1)S(1)} %get-tuple-element.51), channel_id=1, source_target_pairs={{0,1},{1,0},{2,3},{3,2},{4,5},{5,4},{6,7},{7,6},{8,9},{9,8},{10,11... | collective-permute-start | bytes 196616 | tf_op jit(solution)/shard_map/ppermute | solution.py:386
  13.9 6.7 %collective-permute-start.5 = (bf16[192,128]{1,0:T(8,128)(2,1)S(1)}, bf16[192,128]{1,0:T(8,128)(2,1)S(1)}, u32[]{:S(2)}, u32[]{:S(2)}) collective-permute-start(bf16[192,128]{1,0:T(8,128)(2,1)S(1)} %get-tuple-element.56), channel_id=1, source_target_pairs={{0,16},{1,2},{2,1},{3,4},{4,3},{5,6},{6,5},{7,8},{8,7},{9,10},{10,... | collective-permute-start | bytes 147464 | tf_op jit(solution)/shard_map/ppermute | solution.py:397
  15.4 4.2 %collective-permute-start.6 = (bf16[64,128]{1,0:T(8,128)(2,1)S(1)}, bf16[64,128]{1,0:T(8,128)(2,1)S(1)}, u32[]{:S(2)}, u32[]{:S(2)}) collective-permute-start(bf16[64,128]{1,0:T(8,128)(2,1)S(1)} %pad_maximum_fusion.2), channel_id=1, source_target_pairs={{0,16},{1,2},{2,1},{3,4},{4,3},{5,6},{6,5},{7,8},{8,7},{9,10},{10,... | collective-permute-start | bytes 49160 | tf_op jit(solution)/shard_map/ppermute | solution.py:401
  16.3 3.7 %collective-permute-start.7 = (bf16[64,128]{1,0:T(8,128)(2,1)S(1)}, bf16[64,128]{1,0:T(8,128)(2,1)S(1)}, u32[]{:S(2)}, u32[]{:S(2)}) collective-permute-start(bf16[64,128]{1,0:T(8,128)(2,1)S(1)} %pad_maximum_fusion.3), channel_id=1, source_target_pairs={{0,16},{1,4},{2,18},{3,6},{4,1},{5,8},{6,3},{7,10},{8,5},{9,12},{1... | collective-permute-start | bytes 49160 | tf_op jit(solution)/shard_map/ppermute | solution.py:402
  20.1 1.3 %collective-permute-start.8 = (bf16[144,128]{1,0:T(8,128)(2,1)S(1)}, bf16[144,128]{1,0:T(8,128)(2,1)S(1)}, u32[]{:S(2)}, u32[]{:S(2)}) collective-permute-start(bf16[144,128]{1,0:T(8,128)(2,1)S(1)} %constant_dynamic-update-slice_fusion.5.last), channel_id=1, source_target_pairs={{0,1},{1,0},{2,3},{3,2},{4,5},{5,4},{6,7},{7,6},{8,9},{9,8},{10,11... | collective-permute-start | bytes 110600 | tf_op jit(solution)/shard_map/ppermute | solution.py:413

commit v9 on v8

--- a/solution.py
+++ b/solution.py
@@ -181,14 +181,21 @@
         partial_out[:, 128 * t : 128 * t + 128] = near - tile.astype(f32)
 
 
-def own_kernel(column, traces, partial):
-    own_part(column[...], traces, partial)
-
-
-def local_kernel(stiffness_in, lift_in, column, state, got, stiffness, lift, base, inflow, picks, token, sems):
+def columns_kernel(column, inflow, picks):
+    elements = column.shape[0]
+    rim = elements // 8
+    columns = column[...]
+    low = lanes((elements, 128)) < 64
+    for t in range(3):
+        speed = columns[:, t : t + 1]
+        inflow[:, 128 * t : 128 * t + 128] = columns[:, 3:4] * jnp.maximum(jnp.where(low, speed, -speed), 0.0)
+    for i in range(6):
+        picks[:, 2 * rim * i : 2 * rim * i + 2 * rim] = hot(columns[:, 16 + i : 17 + i], 2 * rim)
+
+
+def local_kernel(stiffness_in, lift_in, column, state, traces, got, stiffness, lift, base, partial, token, sems):
     token[...] = got[0:16, :]
-    elements, modes = state.shape
-    rim = elements // 8
+    modes = state.shape[1]
     copies = [
         pltpu.make_async_copy(stiffness_in, stiffness, sems.at[0]),
         pltpu.make_async_copy(lift_in, lift, sems.at[1]),
@@ -196,12 +203,7 @@
     for copy in copies:
         copy.start()
     columns = column[...]
-    low = lanes((elements, 128)) < 64
-    for t in range(3):
-        speed = columns[:, t : t + 1]
-        inflow[:, 128 * t : 128 * t + 128] = columns[:, 3:4] * jnp.maximum(jnp.where(low, speed, -speed), 0.0)
-    for i in range(6):
-        picks[:, 2 * rim * i : 2 * rim * i + 2 * rim] = hot(columns[:, 16 + i : 17 + i], 2 * rim)
+    own_part(columns, traces, partial)
     lowered = state[...].astype(bf16)
     step = 256
     copies[0].wait()
@@ -274,19 +276,21 @@
     return face, jnp.where(match, 1.0, 0.0).astype(bf16)
 
 
-def mortar_term(both, face, element_hot, t):
+def mortar_sum(both, face, element_hot):
     half = jnp.where(lanes(both.shape) < 64, 0.0, 1.0)
-    return dot(element_hot, jnp.where(half + 2 * t == face, both, 0.0).astype(bf16))
+    placed = [jnp.where(half + 2 * t == face, both, 0.0).astype(bf16) for t in range(3)]
+    return dot(element_hot, jnp.concatenate(placed, axis=1))
 
 
 def add_direct(picks, partial, got, near, both, face, element_hot, total):
     rim = picks.shape[1] // 12
+    mortar = mortar_sum(both, face, element_hot)
     for t in range(3):
         cut = slice(128 * t, 128 * t + 128)
         rows = slice(rim * t, rim * t + rim)
         window = jnp.concatenate([got[rows, :], near[rows, :]], axis=0)
         conforming = dot(picks[:, 4 * rim * t : 4 * rim * t + 4 * rim], swapped(window))
-        total[:, cut] = partial[:, cut] + conforming + mortar_term(both, face, element_hot, t)
+        total[:, cut] = partial[:, cut] + conforming + mortar[:, cut]
 
 
 def direct_kernel(picks, partial, got, near, far, last, total, face_out, element_hot_out, arrived):
@@ -303,12 +307,7 @@
 
 
 def fluxes(both, face, element_hot, partial, inflow):
-    parts = []
-    for t in range(3):
-        cut = slice(128 * t, 128 * t + 128)
-        total = partial[:, cut] + mortar_term(both, face, element_hot, t)
-        parts.append((inflow[:, cut] * total).astype(bf16))
-    return jnp.concatenate(parts, axis=1)
+    return (inflow[...] * (partial[...] + mortar_sum(both, face, element_hot))).astype(bf16)
 
 
 def middle_kernel(
@@ -458,16 +457,17 @@
         (),
     )
 
-    partial = call(own_kernel, [faces], [], 10**8, (), (element_column, traces))[0]
+    picks = array((elements, 12 * rim), bf16)
+    inflow, picks = call(columns_kernel, [faces, picks], [], 10**8, (), (element_column,))
 
     def local(got):
         return call(
             local_kernel,
-            [like(stiffness), like(lift), whole, faces, array((elements, 12 * rim), bf16), mark],
+            [like(stiffness), like(lift), whole, faces, mark],
             [pltpu.SemaphoreType.DMA((2,))],
             10**8,
             (stiffness, lift),
-            (element_column, near_state, got),
+            (element_column, near_state, traces, got),
         )
 
     def direct(results, *arrived):
@@ -477,10 +477,10 @@
             [vmem((5 * capacity, 128), bf16)],
             10**9,
             (),
-            (results[4], partial, *arrived),
+            (picks, results[3], *arrived),
         )
 
-    last, (partial, *direct_targets), (stiffness, lift, base, inflow, picks) = exchange(
+    last, (partial, *direct_targets), (stiffness, lift, base, _) = exchange(
         first, None, own, core, capacity, local, direct
     )
     field, traces, first, rims, own, face, element_hot = call(

time: 23 us -> 23 us (level)
  starting transfers between devices: 7.99 us -> 8.31 us
  waiting for transfers between devices: 2.14 us -> 1.88 us
    ppermute x2, waiting for transfers between devices: 1.68 us -> 1.41 us  [exchange(): far = lax.ppermute(far, axes, far_chips)]
where the time goes in v9:
time: 23 us; the launch traced here: 22.8 us
  Pallas kernels  12.3 us (53%)
  starting transfers between devices  8.31 us (36%)
  waiting for transfers between devices  1.88 us (8%)
    pallas_call x8, Pallas kernels, call(): pl.pallas_call(kernel, out_shape=out_shape, in_specs=specs, out_specs=[pl...  12.3 us
    ppermute x2, starting transfers between devices, exchange(): near = lax.ppermute(near, axes, chips)  3.75 us
    ppermute x1, starting transfers between devices, exchange(): rim = lax.ppermute(rim, axes, chips)  1.52 us
    ppermute x2, waiting for transfers between devices, exchange(): far = lax.ppermute(far, axes, far_chips)  1.41 us
    ppermute x2, starting transfers between devices, exchange(): far = lax.ppermute(far, axes, far_chips)  1.28 us
    ppermute x2, starting transfers between devices, exchange(): got = lax.ppermute(first, axes, cores)  0.94 us
    ppermute x2, starting transfers between devices, exchange(): return (lax.ppermute(last, axes, cores), totals, results)  0.83 us
    ppermute x2, waiting for transfers between devices, exchange(): return (lax.ppermute(last, axes, cores), totals, results)  0.46 us
  transfers between devices with their start and end apart: 9, of which 4 were waited for; matrix products, arithmetic and copies ran while one was open for 0% of the time, Pallas kernels for 31%

profile of v9, /device:TPU:0, one launch (start us, length us, event | category | flops | bytes accessed | tf_op | source)
XLA Modules:
  0.0 22.8 jit_solution(7930320452912245350)
XLA Ops:
  0.0 2.5 %shard_map.100 = (f32[512,512]{1,0:T(8,128)S(1)}, bf16[512,384]{1,0:T(8,128)(2,1)S(1)}, bf16[64,512]{1,0:T(8,128)(2,1)S(1)}, bf16[512,384]{1,0:T(8,128)(2,1)S(1)...) custom-call(f32[512,512]{1,0:T(8,128)} %state.1, ...), custom_call_target="tpu_custom_call" | custom-call | flops 200000000 | bytes 1531936 | tf_op jit(solution)/shard_map/pallas_call | solution.py:368
  2.5 0.5 %collective-permute-start = (bf16[320,128]{1,0:T(8,128)(2,1)S(1)}, bf16[320,128]{1,0:T(8,128)(2,1)S(1)}, u32[]{:S(2)}, u32[]{:S(2)}) collective-permute-start(bf16[320,128]{1,0:T(8,128)(2,1)S(1)} %get-tuple-element.37), channel_id=1, source_target_pairs={{0,1},{1,0},{2,3},{3,2},{4,5},{5,4},{6,7},{7,6},{8,9},{9,8},{10,11... | collective-permute-start | bytes 245768 | tf_op jit(solution)/shard_map/ppermute | solution.py:385
  3.0 1.0 %shard_map.102 = (f32[512,384]{1,0:T(8,128)S(1)}, bf16[512,768]{1,0:T(8,128)(2,1)S(1)}) custom-call(f32[512,128]{1,0:T(8,128)S(1)} %get-tuple-element.34.column), custom_call_target="tpu_custom_call" | custom-call | flops 100000000 | bytes 100000 | tf_op jit(solution)/shard_map/pallas_call | solution.py:368
  4.0 0.0 collective-permute-done.got
  4.0 2.8 %collective-permute-start.1 = (bf16[320,128]{1,0:T(8,128)(2,1)S(1)}, bf16[320,128]{1,0:T(8,128)(2,1)S(1)}, u32[]{:S(2)}, u32[]{:S(2)}) collective-permute-start(bf16[320,128]{1,0:T(8,128)(2,1)S(1)} %pad_maximum_fusion), channel_id=1, source_target_pairs={{0,16},{1,2},{2,1},{3,4},{4,3},{5,6},{6,5},{7,8},{8,7},{9,10},{10,... | collective-permute-start | bytes 245768 | tf_op jit(solution)/shard_map/ppermute | solution.py:400
  6.9 0.1 collective-permute-start.2
  7.0 2.7 %shard_map.101 = (bf16[512,1536]{1,0:T(8,128)(2,1)S(1)}, bf16[384,512]{1,0:T(8,128)(2,1)S(1)}, f32[512,512]{1,0:T(8,128)S(1)}, f32[512,384]{1,0:T(8,128)S(1)}, bf16[16,128]{1,0:T(8,128)(2,1)S(1)}) custom-call(bf16[512,1536]{1,0:T(8,128)(2,1)} %stiffness_in.1, bf16[384,512]{1,0:T(8,128)(2,1)} %lift_in.1, f32[512,128]{1,0:T(8,128)S(1)} %get-tuple-element.34.column, ...), custom_call_target="tpu_custom_call" | custom-call | flops 100000000 | bytes 100000 | tf_op jit(solution)/shard_map/pallas_call | solution.py:368
  9.7 0.0 collective-permute-done.1.near
  9.7 1.0 %collective-permute-done.2.far = bf16[96,128]{1,0:T(8,128)(2,1)S(1)} collective-permute-done((bf16[96,128]{1,0:T(8,128)(2,1)S(1)}, bf16[96,128]{1,0:T(8,128)(2,1)S(1)}, u32[]{:S(2)}, u32[]{:S(2)}) %collective-permute-start.2) | collective-permute-done | bytes 24608 | tf_op jit(solution)/shard_map/ppermute | solution.py:401
  10.7 0.4 %collective-permute-start.3 = (bf16[144,128]{1,0:T(8,128)(2,1)S(1)}, bf16[144,128]{1,0:T(8,128)(2,1)S(1)}, u32[]{:S(2)}, u32[]{:S(2)}) collective-permute-start(bf16[144,128]{1,0:T(8,128)(2,1)S(1)} %constant_dynamic-update-slice_fusion.last), channel_id=1, source_target_pairs={{0,1},{1,0},{2,3},{3,2},{4,5},{5,4},{6,7},{7,6},{8,9},{9,8},{10,11... | collective-permute-start | bytes 110600 | tf_op jit(solution)/shard_map/ppermute | solution.py:412
  11.2 0.7 %shard_map.103 = (f32[512,384]{1,0:T(8,128)S(1)}, f32[160,128]{1,0:T(8,128)S(1)}, bf16[512,160]{1,0:T(8,128)(2,1)S(1)}) custom-call(bf16[512,768]{1,0:T(8,128)(2,1)S(1)} %get-tuple-element.40.picks, f32[512,384]{1,0:T(8,128)S(1)} %get-tuple-element.41.partial, bf16[320,128]{1,0:T(8,128)(2,1)S(1)} %collective-permute-done.got, ...), custom_call_target="tpu_custom_call" | custom-call | flops 1000000000 | bytes 1798144 | tf_op jit(solution)/shard_map/pallas_call | solution.py:368
  11.9 0.2 collective-permute-done.3.last
  12.0 1.5 %shard_map.104 = (f32[512,512]{1,0:T(8,128)S(1)}, bf16[512,384]{1,0:T(8,128)(2,1)S(1)}, bf16[256,128]{1,0:T(8,128)(2,1)S(1)}, bf16[192,128]{1,0:T(8,128)(2,1)S(1...) custom-call(bf16[384,512]{1,0:T(8,128)(2,1)S(1)} %get-tuple-element.38.lift, ...), custom_call_target="tpu_custom_call" | custom-call | flops 1000000000 | bytes 3903488 | tf_op jit(solution)/shard_map/pallas_call | solution.py:368
  13.5 0.4 %collective-permute-start.4 = (bf16[256,128]{1,0:T(8,128)(2,1)S(1)}, bf16[256,128]{1,0:T(8,128)(2,1)S(1)}, u32[]{:S(2)}, u32[]{:S(2)}) collective-permute-start(bf16[256,128]{1,0:T(8,128)(2,1)S(1)} %get-tuple-element.53), channel_id=1, source_target_pairs={{0,1},{1,0},{2,3},{3,2},{4,5},{5,4},{6,7},{7,6},{8,9},{9,8},{10,11... | collective-permute-start | bytes 196616 | tf_op jit(solution)/shard_map/ppermute | solution.py:385
  13.9 1.5 %collective-permute-start.5 = (bf16[192,128]{1,0:T(8,128)(2,1)S(1)}, bf16[192,128]{1,0:T(8,128)(2,1)S(1)}, u32[]{:S(2)}, u32[]{:S(2)}) collective-permute-start(bf16[192,128]{1,0:T(8,128)(2,1)S(1)} %get-tuple-element.58), channel_id=1, source_target_pairs={{0,16},{1,2},{2,1},{3,4},{4,3},{5,6},{6,5},{7,8},{8,7},{9,10},{10,... | collective-permute-start | bytes 147464 | tf_op jit(solution)/shard_map/ppermute | solution.py:396
  15.4 0.0 collective-permute-done.4.got
  15.4 0.9 %collective-permute-start.6 = (bf16[64,128]{1,0:T(8,128)(2,1)S(1)}, bf16[64,128]{1,0:T(8,128)(2,1)S(1)}, u32[]{:S(2)}, u32[]{:S(2)}) collective-permute-start(bf16[64,128]{1,0:T(8,128)(2,1)S(1)} %pad_maximum_fusion.2), channel_id=1, source_target_pairs={{0,16},{1,2},{2,1},{3,4},{4,3},{5,6},{6,5},{7,8},{8,7},{9,10},{10,... | collective-permute-start | bytes 49160 | tf_op jit(solution)/shard_map/ppermute | solution.py:400
  16.3 1.2 %collective-permute-start.7 = (bf16[64,128]{1,0:T(8,128)(2,1)S(1)}, bf16[64,128]{1,0:T(8,128)(2,1)S(1)}, u32[]{:S(2)}, u32[]{:S(2)}) collective-permute-start(bf16[64,128]{1,0:T(8,128)(2,1)S(1)} %pad_maximum_fusion.3), channel_id=1, source_target_pairs={{0,16},{1,4},{2,18},{3,6},{4,1},{5,8},{6,3},{7,10},{8,5},{9,12},{1... | collective-permute-start | bytes 49160 | tf_op jit(solution)/shard_map/ppermute | solution.py:401
  17.5 2.1 %shard_map.105 = (f32[512,512]{1,0:T(8,128)S(1)}, f32[512,384]{1,0:T(8,128)S(1)}, bf16[16,128]{1,0:T(8,128)(2,1)S(1)}) custom-call(f32[512,128]{1,0:T(8,128)S(1)} %get-tuple-element.34.column, f32[512,512]{1,0:T(8,128)S(1)} %copy-done, f32[512,512]{1,0:T(8,128)S(1)} %get-tuple-element.50.field, bf16[512,1536]{1,0:T(8,128)(2,1)S(1)} %get-tuple-element.51.stiffness, ...), custom_call_target="tpu_custom_call" | custom-call | flops 100000000 | bytes 100000 | tf_op jit(solution)/shard_map/pallas_call | solution.py:368
  19.6 0.4 %collective-permute-done.7.far = bf16[64,128]{1,0:T(8,128)(2,1)S(1)} collective-permute-done((bf16[64,128]{1,0:T(8,128)(2,1)S(1)}, bf16[64,128]{1,0:T(8,128)(2,1)S(1)}, u32[]{:S(2)}, u32[]{:S(2)}) %collective-permute-start.7) | collective-permute-done | bytes 16416 | tf_op jit(solution)/shard_map/ppermute | solution.py:401
  20.1 0.4 %collective-permute-start.8 = (bf16[144,128]{1,0:T(8,128)(2,1)S(1)}, bf16[144,128]{1,0:T(8,128)(2,1)S(1)}, u32[]{:S(2)}, u32[]{:S(2)}) collective-permute-start(bf16[144,128]{1,0:T(8,128)(2,1)S(1)} %constant_dynamic-update-slice_fusion.5.last), channel_id=1, source_target_pairs={{0,1},{1,0},{2,3},{3,2},{4,5},{5,4},{6,7},{7,6},{8,9},{9,8},{10,11... | collective-permute-start | bytes 110600 | tf_op jit(solution)/shard_map/ppermute | solution.py:412
  20.5 0.6 %shard_map.106.partial = f32[512,384]{1,0:T(8,128)S(1)} custom-call(bf16[512,768]{1,0:T(8,128)(2,1)S(1)} %get-tuple-element.40.picks, f32[512,384]{1,0:T(8,128)S(1)} %get-tuple-element.55.partial, f32[160,128]{1,0:T(8,128)S(1)} %get-tuple-element.56.face, bf16[512,160]{1,0:T(8,128)(2,1)S(1)} %get-tuple-element.57.element_hot, ...), custom_call_target="tpu_custom_call" | custom-call | flops 1000000000 | bytes 2002944 | tf_op jit(solution)/shard_map/pallas_call | solution.py:368
  21.1 0.3 %collective-permute-done.8.last = bf16[144,128]{1,0:T(8,128)(2,1)S(1)} collective-permute-done((bf16[144,128]{1,0:T(8,128)(2,1)S(1)}, bf16[144,128]{1,0:T(8,128)(2,1)S(1)}, u32[]{:S(2)}, u32[]{:S(2)}) %collective-permute-start.8) | collective-permute-done | bytes 36896 | tf_op jit(solution)/shard_map/ppermute | solution.py:412
  21.4 1.4 %shard_map.107 = f32[512,512]{1,0:T(8,128)} custom-call(bf16[384,512]{1,0:T(8,128)(2,1)S(1)} %get-tuple-element.38.lift, f32[512,512]{1,0:T(8,128)S(1)} %get-tuple-element.54.base, f32[512,384]{1,0:T(8,128)S(1)} %shard_map.106.partial, f32[512,384]{1,0:T(8,128)S(1)} %get-tuple-element.45.inflow, bf16[144,128]{1,0:T(8,128)(2,1)S(1)} %collective-permute-done.8.last, ...), custom_call_target="tpu_custom_call" | custom-call | flops 1000000000 | bytes 3198976 | tf_op jit(solution)/shard_map/pallas_call | solution.py:368
  (24 shorter events, 0.2 us)
Async XLA Ops:
  2.5 1.5 %collective-permute-start = (bf16[320,128]{1,0:T(8,128)(2,1)S(1)}, bf16[320,128]{1,0:T(8,128)(2,1)S(1)}, u32[]{:S(2)}, u32[]{:S(2)}) collective-permute-start(bf16[320,128]{1,0:T(8,128)(2,1)S(1)} %get-tuple-element.37), channel_id=1, source_target_pairs={{0,1},{1,0},{2,3},{3,2},{4,5},{5,4},{6,7},{7,6},{8,9},{9,8},{10,11... | collective-permute-start | bytes 245768 | tf_op jit(solution)/shard_map/ppermute | solution.py:385
  4.0 5.7 %collective-permute-start.1 = (bf16[320,128]{1,0:T(8,128)(2,1)S(1)}, bf16[320,128]{1,0:T(8,128)(2,1)S(1)}, u32[]{:S(2)}, u32[]{:S(2)}) collective-permute-start(bf16[320,128]{1,0:T(8,128)(2,1)S(1)} %pad_maximum_fusion), channel_id=1, source_target_pairs={{0,16},{1,2},{2,1},{3,4},{4,3},{5,6},{6,5},{7,8},{8,7},{9,10},{10,... | collective-permute-start | bytes 245768 | tf_op jit(solution)/shard_map/ppermute | solution.py:400
  6.9 3.8 %collective-permute-start.2 = (bf16[96,128]{1,0:T(8,128)(2,1)S(1)}, bf16[96,128]{1,0:T(8,128)(2,1)S(1)}, u32[]{:S(2)}, u32[]{:S(2)}) collective-permute-start(bf16[96,128]{1,0:T(8,128)(2,1)S(1)} %pad_maximum_fusion.1), channel_id=1, source_target_pairs={{0,16},{1,4},{2,18},{3,6},{4,1},{5,8},{6,3},{7,10},{8,5},{9,12},{1... | collective-permute-start | bytes 73736 | tf_op jit(solution)/shard_map/ppermute | solution.py:401
  10.7 1.3 %collective-permute-start.3 = (bf16[144,128]{1,0:T(8,128)(2,1)S(1)}, bf16[144,128]{1,0:T(8,128)(2,1)S(1)}, u32[]{:S(2)}, u32[]{:S(2)}) collective-permute-start(bf16[144,128]{1,0:T(8,128)(2,1)S(1)} %constant_dynamic-update-slice_fusion.last), channel_id=1, source_target_pairs={{0,1},{1,0},{2,3},{3,2},{4,5},{5,4},{6,7},{7,6},{8,9},{9,8},{10,11... | collective-permute-start | bytes 110600 | tf_op jit(solution)/shard_map/ppermute | solution.py:412
  12.0 5.5 %copy-start = (f32[512,512]{1,0:T(8,128)S(1)}, f32[512,512]{1,0:T(8,128)}, u32[]{:S(2)}) copy-start(f32[512,512]{1,0:T(8,128)} %state.1) | copy-start | bytes 3145732
  13.5 1.9 %collective-permute-start.4 = (bf16[256,128]{1,0:T(8,128)(2,1)S(1)}, bf16[256,128]{1,0:T(8,128)(2,1)S(1)}, u32[]{:S(2)}, u32[]{:S(2)}) collective-permute-start(bf16[256,128]{1,0:T(8,128)(2,1)S(1)} %get-tuple-element.53), channel_id=1, source_target_pairs={{0,1},{1,0},{2,3},{3,2},{4,5},{5,4},{6,7},{7,6},{8,9},{9,8},{10,11... | collective-permute-start | bytes 196616 | tf_op jit(solution)/shard_map/ppermute | solution.py:385
  13.9 6.6 %collective-permute-start.5 = (bf16[192,128]{1,0:T(8,128)(2,1)S(1)}, bf16[192,128]{1,0:T(8,128)(2,1)S(1)}, u32[]{:S(2)}, u32[]{:S(2)}) collective-permute-start(bf16[192,128]{1,0:T(8,128)(2,1)S(1)} %get-tuple-element.58), channel_id=1, source_target_pairs={{0,16},{1,2},{2,1},{3,4},{4,3},{5,6},{6,5},{7,8},{8,7},{9,10},{10,... | collective-permute-start | bytes 147464 | tf_op jit(solution)/shard_map/ppermute | solution.py:396
  15.4 4.2 %collective-permute-start.6 = (bf16[64,128]{1,0:T(8,128)(2,1)S(1)}, bf16[64,128]{1,0:T(8,128)(2,1)S(1)}, u32[]{:S(2)}, u32[]{:S(2)}) collective-permute-start(bf16[64,128]{1,0:T(8,128)(2,1)S(1)} %pad_maximum_fusion.2), channel_id=1, source_target_pairs={{0,16},{1,2},{2,1},{3,4},{4,3},{5,6},{6,5},{7,8},{8,7},{9,10},{10,... | collective-permute-start | bytes 49160 | tf_op jit(solution)/shard_map/ppermute | solution.py:400
  16.3 3.7 %collective-permute-start.7 = (bf16[64,128]{1,0:T(8,128)(2,1)S(1)}, bf16[64,128]{1,0:T(8,128)(2,1)S(1)}, u32[]{:S(2)}, u32[]{:S(2)}) collective-permute-start(bf16[64,128]{1,0:T(8,128)(2,1)S(1)} %pad_maximum_fusion.3), channel_id=1, source_target_pairs={{0,16},{1,4},{2,18},{3,6},{4,1},{5,8},{6,3},{7,10},{8,5},{9,12},{1... | collective-permute-start | bytes 49160 | tf_op jit(solution)/shard_map/ppermute | solution.py:401
  20.1 1.3 %collective-permute-start.8 = (bf16[144,128]{1,0:T(8,128)(2,1)S(1)}, bf16[144,128]{1,0:T(8,128)(2,1)S(1)}, u32[]{:S(2)}, u32[]{:S(2)}) collective-permute-start(bf16[144,128]{1,0:T(8,128)(2,1)S(1)} %constant_dynamic-update-slice_fusion.5.last), channel_id=1, source_target_pairs={{0,1},{1,0},{2,3},{3,2},{4,5},{5,4},{6,7},{7,6},{8,9},{9,8},{10,11... | collective-permute-start | bytes 110600 | tf_op jit(solution)/shard_map/ppermute | solution.py:412

commit v10 on v8

--- a/solution.py
+++ b/solution.py
@@ -193,8 +193,7 @@
         pltpu.make_async_copy(stiffness_in, stiffness, sems.at[0]),
         pltpu.make_async_copy(lift_in, lift, sems.at[1]),
     ]
-    for copy in copies:
-        copy.start()
+    copies[0].start()
     columns = column[...]
     low = lanes((elements, 128)) < 64
     for t in range(3):
@@ -205,6 +204,7 @@
     lowered = state[...].astype(bf16)
     step = 256
     copies[0].wait()
+    copies[1].start()
     for n in range(0, modes, step):
         base[:, n : n + step] = state[:, n : n + step] + time_step * volume_term(columns, lowered, stiffness, n, step)
     copies[1].wait()
@@ -274,19 +274,21 @@
     return face, jnp.where(match, 1.0, 0.0).astype(bf16)
 
 
-def mortar_term(both, face, element_hot, t):
+def mortar_sum(both, face, element_hot):
     half = jnp.where(lanes(both.shape) < 64, 0.0, 1.0)
-    return dot(element_hot, jnp.where(half + 2 * t == face, both, 0.0).astype(bf16))
+    placed = [jnp.where(half + 2 * t == face, both, 0.0).astype(bf16) for t in range(3)]
+    return dot(element_hot, jnp.concatenate(placed, axis=1))
 
 
 def add_direct(picks, partial, got, near, both, face, element_hot, total):
     rim = picks.shape[1] // 12
+    mortar = mortar_sum(both, face, element_hot)
     for t in range(3):
         cut = slice(128 * t, 128 * t + 128)
         rows = slice(rim * t, rim * t + rim)
         window = jnp.concatenate([got[rows, :], near[rows, :]], axis=0)
         conforming = dot(picks[:, 4 * rim * t : 4 * rim * t + 4 * rim], swapped(window))
-        total[:, cut] = partial[:, cut] + conforming + mortar_term(both, face, element_hot, t)
+        total[:, cut] = partial[:, cut] + conforming + mortar[:, cut]
 
 
 def direct_kernel(picks, partial, got, near, far, last, total, face_out, element_hot_out, arrived):
@@ -303,12 +305,7 @@
 
 
 def fluxes(both, face, element_hot, partial, inflow):
-    parts = []
-    for t in range(3):
-        cut = slice(128 * t, 128 * t + 128)
-        total = partial[:, cut] + mortar_term(both, face, element_hot, t)
-        parts.append((inflow[:, cut] * total).astype(bf16))
-    return jnp.concatenate(parts, axis=1)
+    return (inflow[...] * (partial[...] + mortar_sum(both, face, element_hot))).astype(bf16)
 
 
 def middle_kernel(

time: 23 us -> 22.9 us (level)
  transfers between devices with their start and end apart: 9 -> 9, of which waited for: 4 -> 4; matrix products, arithmetic and copies ran while one was open for 0% -> 0% of each run, Pallas kernels for 31% -> 30%
where the time goes in v10:
time: 22.9 us; the launch traced here: 22.7 us
  Pallas kernels  12.2 us (53%)
  starting transfers between devices  7.97 us (35%)
  waiting for transfers between devices  2.24 us (10%)
    pallas_call x8, Pallas kernels, call(): pl.pallas_call(kernel, out_shape=out_shape, in_specs=specs, out_specs=[pl...  12.2 us
    ppermute x2, starting transfers between devices, exchange(): near = lax.ppermute(near, axes, chips)  3.56 us
    ppermute x2, waiting for transfers between devices, exchange(): far = lax.ppermute(far, axes, far_chips)  1.69 us
    ppermute x1, starting transfers between devices, exchange(): rim = lax.ppermute(rim, axes, chips)  1.52 us
    ppermute x2, starting transfers between devices, exchange(): far = lax.ppermute(far, axes, far_chips)  1.27 us
    ppermute x2, starting transfers between devices, exchange(): got = lax.ppermute(first, axes, cores)  0.86 us
    ppermute x2, starting transfers between devices, exchange(): return (lax.ppermute(last, axes, cores), totals, results)  0.75 us
    ppermute x2, waiting for transfers between devices, exchange(): return (lax.ppermute(last, axes, cores), totals, results)  0.54 us
  transfers between devices with their start and end apart: 9, of which 4 were waited for; matrix products, arithmetic and copies ran while one was open for 0% of the time, Pallas kernels for 30%

profile of v10, /device:TPU:0, one launch (start us, length us, event | category | flops | bytes accessed | tf_op | source)
XLA Modules:
  0.0 22.7 jit_solution(6610738291203048278)
XLA Ops:
  0.0 2.5 %shard_map.100 = (f32[512,512]{1,0:T(8,128)S(1)}, bf16[512,384]{1,0:T(8,128)(2,1)S(1)}, bf16[64,512]{1,0:T(8,128)(2,1)S(1)}, bf16[512,384]{1,0:T(8,128)(2,1)S(1)...) custom-call(f32[512,512]{1,0:T(8,128)} %state.1, ...), custom_call_target="tpu_custom_call" | custom-call | flops 200000000 | bytes 1531936 | tf_op jit(solution)/shard_map/pallas_call | solution.py:366
  2.5 0.5 %collective-permute-start = (bf16[320,128]{1,0:T(8,128)(2,1)S(1)}, bf16[320,128]{1,0:T(8,128)(2,1)S(1)}, u32[]{:S(2)}, u32[]{:S(2)}) collective-permute-start(bf16[320,128]{1,0:T(8,128)(2,1)S(1)} %get-tuple-element.35), channel_id=1, source_target_pairs={{0,1},{1,0},{2,3},{3,2},{4,5},{5,4},{6,7},{7,6},{8,9},{9,8},{10,11... | collective-permute-start | bytes 245768 | tf_op jit(solution)/shard_map/ppermute | solution.py:383
  3.0 1.1 %shard_map.102.partial = f32[512,384]{1,0:T(8,128)S(1)} custom-call(f32[512,128]{1,0:T(8,128)S(1)} %get-tuple-element.33.column, bf16[512,384]{1,0:T(8,128)(2,1)S(1)} %get-tuple-element.39.traces), custom_call_target="tpu_custom_call" | custom-call | flops 100000000 | bytes 100000 | tf_op jit(solution)/shard_map/pallas_call | solution.py:366
  4.2 0.0 collective-permute-done.got
  4.2 2.7 %collective-permute-start.1 = (bf16[320,128]{1,0:T(8,128)(2,1)S(1)}, bf16[320,128]{1,0:T(8,128)(2,1)S(1)}, u32[]{:S(2)}, u32[]{:S(2)}) collective-permute-start(bf16[320,128]{1,0:T(8,128)(2,1)S(1)} %pad_maximum_fusion), channel_id=1, source_target_pairs={{0,16},{1,2},{2,1},{3,4},{4,3},{5,6},{6,5},{7,8},{8,7},{9,10},{10,... | collective-permute-start | bytes 245768 | tf_op jit(solution)/shard_map/ppermute | solution.py:398
  6.9 0.1 collective-permute-start.2
  7.0 2.4 %shard_map.101 = (bf16[512,1536]{1,0:T(8,128)(2,1)S(1)}, bf16[384,512]{1,0:T(8,128)(2,1)S(1)}, f32[512,512]{1,0:T(8,128)S(1)}, f32[512,384]{1,0:T(8,128)S(1)}, b...) custom-call(bf16[512,1536]{1,0:T(8,128)(2,1)} %stiffness_in.1, bf16[384,512]{1,0:T(8,128)(2,1)} %lift_in.1, ...), custom_call_target="tpu_custom_call" | custom-call | flops 100000000 | bytes 100000 | tf_op jit(solution)/shard_map/pallas_call | solution.py:366
  9.5 1.2 %collective-permute-done.2.far = bf16[96,128]{1,0:T(8,128)(2,1)S(1)} collective-permute-done((bf16[96,128]{1,0:T(8,128)(2,1)S(1)}, bf16[96,128]{1,0:T(8,128)(2,1)S(1)}, u32[]{:S(2)}, u32[]{:S(2)}) %collective-permute-start.2) | collective-permute-done | bytes 24608 | tf_op jit(solution)/shard_map/ppermute | solution.py:399
  10.7 0.3 %collective-permute-start.3 = (bf16[144,128]{1,0:T(8,128)(2,1)S(1)}, bf16[144,128]{1,0:T(8,128)(2,1)S(1)}, u32[]{:S(2)}, u32[]{:S(2)}) collective-permute-start(bf16[144,128]{1,0:T(8,128)(2,1)S(1)} %constant_dynamic-update-slice_fusion.last), channel_id=1, source_target_pairs={{0,1},{1,0},{2,3},{3,2},{4,5},{5,4},{6,7},{7,6},{8,9},{9,8},{10,11... | collective-permute-start | bytes 110600 | tf_op jit(solution)/shard_map/ppermute | solution.py:410
  11.1 0.7 %shard_map.103 = (f32[512,384]{1,0:T(8,128)S(1)}, f32[160,128]{1,0:T(8,128)S(1)}, bf16[512,160]{1,0:T(8,128)(2,1)S(1)}) custom-call(bf16[512,768]{1,0:T(8,128)(2,1)S(1)} %get-tuple-element.38.picks, f32[512,384]{1,0:T(8,128)S(1)} %shard_map.102.partial, bf16[320,128]{1,0:T(8,128)(2,1)S(1)} %collective-permute-done.got, ...), custom_call_target="tpu_custom_call" | custom-call | flops 1000000000 | bytes 1798144 | tf_op jit(solution)/shard_map/pallas_call | solution.py:366
  11.8 0.3 %collective-permute-done.3.last = bf16[144,128]{1,0:T(8,128)(2,1)S(1)} collective-permute-done((bf16[144,128]{1,0:T(8,128)(2,1)S(1)}, bf16[144,128]{1,0:T(8,128)(2,1)S(1)}, u32[]{:S(2)}, u32[]{:S(2)}) %collective-permute-start.3) | collective-permute-done | bytes 36896 | tf_op jit(solution)/shard_map/ppermute | solution.py:410
  12.0 1.5 %shard_map.104 = (f32[512,512]{1,0:T(8,128)S(1)}, bf16[512,384]{1,0:T(8,128)(2,1)S(1)}, bf16[256,128]{1,0:T(8,128)(2,1)S(1)}, bf16[192,128]{1,0:T(8,128)(2,1)S(1...) custom-call(bf16[384,512]{1,0:T(8,128)(2,1)S(1)} %get-tuple-element.36.lift, ...), custom_call_target="tpu_custom_call" | custom-call | flops 1000000000 | bytes 3903488 | tf_op jit(solution)/shard_map/pallas_call | solution.py:366
  13.5 0.3 %collective-permute-start.4 = (bf16[256,128]{1,0:T(8,128)(2,1)S(1)}, bf16[256,128]{1,0:T(8,128)(2,1)S(1)}, u32[]{:S(2)}, u32[]{:S(2)}) collective-permute-start(bf16[256,128]{1,0:T(8,128)(2,1)S(1)} %get-tuple-element.51), channel_id=1, source_target_pairs={{0,1},{1,0},{2,3},{3,2},{4,5},{5,4},{6,7},{7,6},{8,9},{9,8},{10,11... | collective-permute-start | bytes 196616 | tf_op jit(solution)/shard_map/ppermute | solution.py:383
  13.8 1.5 %collective-permute-start.5 = (bf16[192,128]{1,0:T(8,128)(2,1)S(1)}, bf16[192,128]{1,0:T(8,128)(2,1)S(1)}, u32[]{:S(2)}, u32[]{:S(2)}) collective-permute-start(bf16[192,128]{1,0:T(8,128)(2,1)S(1)} %get-tuple-element.56), channel_id=1, source_target_pairs={{0,16},{1,2},{2,1},{3,4},{4,3},{5,6},{6,5},{7,8},{8,7},{9,10},{10,... | collective-permute-start | bytes 147464 | tf_op jit(solution)/shard_map/ppermute | solution.py:394
  15.3 0.0 collective-permute-done.4.got
  15.3 0.9 %collective-permute-start.6 = (bf16[64,128]{1,0:T(8,128)(2,1)S(1)}, bf16[64,128]{1,0:T(8,128)(2,1)S(1)}, u32[]{:S(2)}, u32[]{:S(2)}) collective-permute-start(bf16[64,128]{1,0:T(8,128)(2,1)S(1)} %pad_maximum_fusion.2), channel_id=1, source_target_pairs={{0,16},{1,2},{2,1},{3,4},{4,3},{5,6},{6,5},{7,8},{8,7},{9,10},{10,... | collective-permute-start | bytes 49160 | tf_op jit(solution)/shard_map/ppermute | solution.py:398
  16.3 1.2 %collective-permute-start.7 = (bf16[64,128]{1,0:T(8,128)(2,1)S(1)}, bf16[64,128]{1,0:T(8,128)(2,1)S(1)}, u32[]{:S(2)}, u32[]{:S(2)}) collective-permute-start(bf16[64,128]{1,0:T(8,128)(2,1)S(1)} %pad_maximum_fusion.3), channel_id=1, source_target_pairs={{0,16},{1,4},{2,18},{3,6},{4,1},{5,8},{6,3},{7,10},{8,5},{9,12},{1... | collective-permute-start | bytes 49160 | tf_op jit(solution)/shard_map/ppermute | solution.py:399
  17.4 2.1 %shard_map.105 = (f32[512,512]{1,0:T(8,128)S(1)}, f32[512,384]{1,0:T(8,128)S(1)}, bf16[16,128]{1,0:T(8,128)(2,1)S(1)}) custom-call(f32[512,128]{1,0:T(8,128)S(1)} %get-tuple-element.33.column, f32[512,512]{1,0:T(8,128)S(1)} %copy-done, f32[512,512]{1,0:T(8,128)S(1)} %get-tuple-element.48.field, bf16[512,1536]{1,0:T(8,128)(2,1)S(1)} %get-tuple-element.49.stiffness, ...), custom_call_target="tpu_custom_call" | custom-call | flops 100000000 | bytes 100000 | tf_op jit(solution)/shard_map/pallas_call | solution.py:366
  19.5 0.0 collective-permute-done.6.near
  19.5 0.5 %collective-permute-done.7.far = bf16[64,128]{1,0:T(8,128)(2,1)S(1)} collective-permute-done((bf16[64,128]{1,0:T(8,128)(2,1)S(1)}, bf16[64,128]{1,0:T(8,128)(2,1)S(1)}, u32[]{:S(2)}, u32[]{:S(2)}) %collective-permute-start.7) | collective-permute-done | bytes 16416 | tf_op jit(solution)/shard_map/ppermute | solution.py:399
  20.0 0.4 %collective-permute-start.8 = (bf16[144,128]{1,0:T(8,128)(2,1)S(1)}, bf16[144,128]{1,0:T(8,128)(2,1)S(1)}, u32[]{:S(2)}, u32[]{:S(2)}) collective-permute-start(bf16[144,128]{1,0:T(8,128)(2,1)S(1)} %constant_dynamic-update-slice_fusion.5.last), channel_id=1, source_target_pairs={{0,1},{1,0},{2,3},{3,2},{4,5},{5,4},{6,7},{7,6},{8,9},{9,8},{10,11... | collective-permute-start | bytes 110600 | tf_op jit(solution)/shard_map/ppermute | solution.py:410
  20.5 0.6 %shard_map.106.partial = f32[512,384]{1,0:T(8,128)S(1)} custom-call(bf16[512,768]{1,0:T(8,128)(2,1)S(1)} %get-tuple-element.38.picks, f32[512,384]{1,0:T(8,128)S(1)} %get-tuple-element.53.partial, f32[160,128]{1,0:T(8,128)S(1)} %get-tuple-element.54.face, bf16[512,160]{1,0:T(8,128)(2,1)S(1)} %get-tuple-element.55.element_hot, ...), custom_call_target="tpu_custom_call" | custom-call | flops 1000000000 | bytes 2002944 | tf_op jit(solution)/shard_map/pallas_call | solution.py:366
  21.0 0.3 %collective-permute-done.8.last = bf16[144,128]{1,0:T(8,128)(2,1)S(1)} collective-permute-done((bf16[144,128]{1,0:T(8,128)(2,1)S(1)}, bf16[144,128]{1,0:T(8,128)(2,1)S(1)}, u32[]{:S(2)}, u32[]{:S(2)}) %collective-permute-start.8) | collective-permute-done | bytes 36896 | tf_op jit(solution)/shard_map/ppermute | solution.py:410
  21.3 1.4 %shard_map.107 = f32[512,512]{1,0:T(8,128)} custom-call(bf16[384,512]{1,0:T(8,128)(2,1)S(1)} %get-tuple-element.36.lift, f32[512,512]{1,0:T(8,128)S(1)} %get-tuple-element.52.base, f32[512,384]{1,0:T(8,128)S(1)} %shard_map.106.partial, f32[512,384]{1,0:T(8,128)S(1)} %get-tuple-element.43.inflow, bf16[144,128]{1,0:T(8,128)(2,1)S(1)} %collective-permute-done.8.last, ...), custom_call_target="tpu_custom_call" | custom-call | flops 1000000000 | bytes 3198976 | tf_op jit(solution)/shard_map/pallas_call | solution.py:366
  (24 shorter events, 0.2 us)
Async XLA Ops:
  2.5 1.7 %collective-permute-start = (bf16[320,128]{1,0:T(8,128)(2,1)S(1)}, bf16[320,128]{1,0:T(8,128)(2,1)S(1)}, u32[]{:S(2)}, u32[]{:S(2)}) collective-permute-start(bf16[320,128]{1,0:T(8,128)(2,1)S(1)} %get-tuple-element.35), channel_id=1, source_target_pairs={{0,1},{1,0},{2,3},{3,2},{4,5},{5,4},{6,7},{7,6},{8,9},{9,8},{10,11... | collective-permute-start | bytes 245768 | tf_op jit(solution)/shard_map/ppermute | solution.py:383
  4.2 5.2 %collective-permute-start.1 = (bf16[320,128]{1,0:T(8,128)(2,1)S(1)}, bf16[320,128]{1,0:T(8,128)(2,1)S(1)}, u32[]{:S(2)}, u32[]{:S(2)}) collective-permute-start(bf16[320,128]{1,0:T(8,128)(2,1)S(1)} %pad_maximum_fusion), channel_id=1, source_target_pairs={{0,16},{1,2},{2,1},{3,4},{4,3},{5,6},{6,5},{7,8},{8,7},{9,10},{10,... | collective-permute-start | bytes 245768 | tf_op jit(solution)/shard_map/ppermute | solution.py:398
  6.9 3.8 %collective-permute-start.2 = (bf16[96,128]{1,0:T(8,128)(2,1)S(1)}, bf16[96,128]{1,0:T(8,128)(2,1)S(1)}, u32[]{:S(2)}, u32[]{:S(2)}) collective-permute-start(bf16[96,128]{1,0:T(8,128)(2,1)S(1)} %pad_maximum_fusion.1), channel_id=1, source_target_pairs={{0,16},{1,4},{2,18},{3,6},{4,1},{5,8},{6,3},{7,10},{8,5},{9,12},{1... | collective-permute-start | bytes 73736 | tf_op jit(solution)/shard_map/ppermute | solution.py:399
  10.7 1.3 %collective-permute-start.3 = (bf16[144,128]{1,0:T(8,128)(2,1)S(1)}, bf16[144,128]{1,0:T(8,128)(2,1)S(1)}, u32[]{:S(2)}, u32[]{:S(2)}) collective-permute-start(bf16[144,128]{1,0:T(8,128)(2,1)S(1)} %constant_dynamic-update-slice_fusion.last), channel_id=1, source_target_pairs={{0,1},{1,0},{2,3},{3,2},{4,5},{5,4},{6,7},{7,6},{8,9},{9,8},{10,11... | collective-permute-start | bytes 110600 | tf_op jit(solution)/shard_map/ppermute | solution.py:410
  12.0 5.4 %copy-start = (f32[512,512]{1,0:T(8,128)S(1)}, f32[512,512]{1,0:T(8,128)}, u32[]{:S(2)}) copy-start(f32[512,512]{1,0:T(8,128)} %state.1) | copy-start | bytes 3145732
  13.5 1.9 %collective-permute-start.4 = (bf16[256,128]{1,0:T(8,128)(2,1)S(1)}, bf16[256,128]{1,0:T(8,128)(2,1)S(1)}, u32[]{:S(2)}, u32[]{:S(2)}) collective-permute-start(bf16[256,128]{1,0:T(8,128)(2,1)S(1)} %get-tuple-element.51), channel_id=1, source_target_pairs={{0,1},{1,0},{2,3},{3,2},{4,5},{5,4},{6,7},{7,6},{8,9},{9,8},{10,11... | collective-permute-start | bytes 196616 | tf_op jit(solution)/shard_map/ppermute | solution.py:383
  13.8 6.6 %collective-permute-start.5 = (bf16[192,128]{1,0:T(8,128)(2,1)S(1)}, bf16[192,128]{1,0:T(8,128)(2,1)S(1)}, u32[]{:S(2)}, u32[]{:S(2)}) collective-permute-start(bf16[192,128]{1,0:T(8,128)(2,1)S(1)} %get-tuple-element.56), channel_id=1, source_target_pairs={{0,16},{1,2},{2,1},{3,4},{4,3},{5,6},{6,5},{7,8},{8,7},{9,10},{10,... | collective-permute-start | bytes 147464 | tf_op jit(solution)/shard_map/ppermute | solution.py:394
  15.3 4.2 %collective-permute-start.6 = (bf16[64,128]{1,0:T(8,128)(2,1)S(1)}, bf16[64,128]{1,0:T(8,128)(2,1)S(1)}, u32[]{:S(2)}, u32[]{:S(2)}) collective-permute-start(bf16[64,128]{1,0:T(8,128)(2,1)S(1)} %pad_maximum_fusion.2), channel_id=1, source_target_pairs={{0,16},{1,2},{2,1},{3,4},{4,3},{5,6},{6,5},{7,8},{8,7},{9,10},{10,... | collective-permute-start | bytes 49160 | tf_op jit(solution)/shard_map/ppermute | solution.py:398
  16.3 3.7 %collective-permute-start.7 = (bf16[64,128]{1,0:T(8,128)(2,1)S(1)}, bf16[64,128]{1,0:T(8,128)(2,1)S(1)}, u32[]{:S(2)}, u32[]{:S(2)}) collective-permute-start(bf16[64,128]{1,0:T(8,128)(2,1)S(1)} %pad_maximum_fusion.3), channel_id=1, source_target_pairs={{0,16},{1,4},{2,18},{3,6},{4,1},{5,8},{6,3},{7,10},{8,5},{9,12},{1... | collective-permute-start | bytes 49160 | tf_op jit(solution)/shard_map/ppermute | solution.py:399
  20.0 1.3 %collective-permute-start.8 = (bf16[144,128]{1,0:T(8,128)(2,1)S(1)}, bf16[144,128]{1,0:T(8,128)(2,1)S(1)}, u32[]{:S(2)}, u32[]{:S(2)}) collective-permute-start(bf16[144,128]{1,0:T(8,128)(2,1)S(1)} %constant_dynamic-update-slice_fusion.5.last), channel_id=1, source_target_pairs={{0,1},{1,0},{2,3},{3,2},{4,5},{5,4},{6,7},{7,6},{8,9},{9,8},{10,11... | collective-permute-start | bytes 110600 | tf_op jit(solution)/shard_map/ppermute | solution.py:410

commit v11 on v10

--- a/solution.py
+++ b/solution.py
@@ -326,10 +326,7 @@
 
 def end_kernel(lift, base, partial, inflow, last, face, element_hot, field, result, sems):
     elements = base.shape[0]
-    capacity = face.shape[0] // 3
-    core = lax.axis_index("pair")
-    far = last[pl.ds(pl.multiple_of((3 - core) * capacity, capacity), capacity), :]
-    both = in_both(jnp.concatenate([last[0 : 2 * capacity, :], far], axis=0), core)
+    both = in_both(last[0 : face.shape[0], :], lax.axis_index("pair"))
     flux = fluxes(both, face[...], element_hot[...], partial, inflow)
     part = elements // 4
     copies = []
@@ -402,8 +399,7 @@
         parts = [either(near, at + capacity, at + 2 * capacity), either(near, at + 3 * capacity, at)]
         parts += [either(far, capacity, 0), either(far, 0, capacity)]
     else:
-        parts = [either(near, at, at + capacity), either(near, at + capacity, at)]
-        parts += [either(far, 0, capacity), either(far, capacity, 0)]
+        parts = [either(near, at, at + capacity), either(near, at + capacity, at), far[:capacity]]
     last = jnp.concatenate(parts + [token], axis=0)
     arrived = (got, near, far) if with_codes else (got, rim, near, far)
     totals = direct(results, *arrived, last)

time: 22.9 us -> 22.9 us (level)
  no operation moved by 1% of the time
where the time goes in v11:
time: 22.9 us; the launch traced here: 22.7 us
  Pallas kernels  12.3 us (54%)
  starting transfers between devices  7.96 us (35%)
  waiting for transfers between devices  2.25 us (10%)
    pallas_call x8, Pallas kernels, call(): pl.pallas_call(kernel, out_shape=out_shape, in_specs=specs, out_specs=[pl...  12.3 us
    ppermute x2, starting transfers between devices, exchange(): near = lax.ppermute(near, axes, chips)  3.56 us
    ppermute x2, waiting for transfers between devices, exchange(): far = lax.ppermute(far, axes, far_chips)  1.71 us
    ppermute x1, starting transfers between devices, exchange(): rim = lax.ppermute(rim, axes, chips)  1.52 us
    ppermute x2, starting transfers between devices, exchange(): far = lax.ppermute(far, axes, far_chips)  1.27 us
    ppermute x2, starting transfers between devices, exchange(): got = lax.ppermute(first, axes, cores)  0.86 us
    ppermute x2, starting transfers between devices, exchange(): return (lax.ppermute(last, axes, cores), totals, results)  0.74 us
    ppermute x2, waiting for transfers between devices, exchange(): return (lax.ppermute(last, axes, cores), totals, results)  0.53 us
  transfers between devices with their start and end apart: 9, of which 4 were waited for; matrix products, arithmetic and copies ran while one was open for 0% of the time, Pallas kernels for 30%

profile of v11, /device:TPU:0, one launch (start us, length us, event | category | flops | bytes accessed | tf_op | source)
XLA Modules:
  0.0 22.7 jit_solution(13533348938813631728)
XLA Ops:
  0.0 2.5 %shard_map.100 = (f32[512,512]{1,0:T(8,128)S(1)}, bf16[512,384]{1,0:T(8,128)(2,1)S(1)}, bf16[64,512]{1,0:T(8,128)(2,1)S(1)}, bf16[512,384]{1,0:T(8,128)(2,1)S(1)...) custom-call(f32[512,512]{1,0:T(8,128)} %state.1, ...), custom_call_target="tpu_custom_call" | custom-call | flops 200000000 | bytes 1531936 | tf_op jit(solution)/shard_map/pallas_call | solution.py:363
  2.5 0.5 %collective-permute-start = (bf16[320,128]{1,0:T(8,128)(2,1)S(1)}, bf16[320,128]{1,0:T(8,128)(2,1)S(1)}, u32[]{:S(2)}, u32[]{:S(2)}) collective-permute-start(bf16[320,128]{1,0:T(8,128)(2,1)S(1)} %get-tuple-element.35), channel_id=1, source_target_pairs={{0,1},{1,0},{2,3},{3,2},{4,5},{5,4},{6,7},{7,6},{8,9},{9,8},{10,11... | collective-permute-start | bytes 245768 | tf_op jit(solution)/shard_map/ppermute | solution.py:380
  3.0 1.1 %shard_map.102.partial = f32[512,384]{1,0:T(8,128)S(1)} custom-call(f32[512,128]{1,0:T(8,128)S(1)} %get-tuple-element.33.column, bf16[512,384]{1,0:T(8,128)(2,1)S(1)} %get-tuple-element.39.traces), custom_call_target="tpu_custom_call" | custom-call | flops 100000000 | bytes 100000 | tf_op jit(solution)/shard_map/pallas_call | solution.py:363
  4.2 0.0 collective-permute-done.got
  4.2 2.7 %collective-permute-start.1 = (bf16[320,128]{1,0:T(8,128)(2,1)S(1)}, bf16[320,128]{1,0:T(8,128)(2,1)S(1)}, u32[]{:S(2)}, u32[]{:S(2)}) collective-permute-start(bf16[320,128]{1,0:T(8,128)(2,1)S(1)} %pad_maximum_fusion), channel_id=1, source_target_pairs={{0,16},{1,2},{2,1},{3,4},{4,3},{5,6},{6,5},{7,8},{8,7},{9,10},{10,... | collective-permute-start | bytes 245768 | tf_op jit(solution)/shard_map/ppermute | solution.py:395
  6.9 0.1 collective-permute-start.2
  7.0 2.4 %shard_map.101 = (bf16[512,1536]{1,0:T(8,128)(2,1)S(1)}, bf16[384,512]{1,0:T(8,128)(2,1)S(1)}, f32[512,512]{1,0:T(8,128)S(1)}, f32[512,384]{1,0:T(8,128)S(1)}, b...) custom-call(bf16[512,1536]{1,0:T(8,128)(2,1)} %stiffness_in.1, bf16[384,512]{1,0:T(8,128)(2,1)} %lift_in.1, ...), custom_call_target="tpu_custom_call" | custom-call | flops 100000000 | bytes 100000 | tf_op jit(solution)/shard_map/pallas_call | solution.py:363
  9.4 0.0 collective-permute-done.1.near
  9.5 1.2 %collective-permute-done.2.far = bf16[96,128]{1,0:T(8,128)(2,1)S(1)} collective-permute-done((bf16[96,128]{1,0:T(8,128)(2,1)S(1)}, bf16[96,128]{1,0:T(8,128)(2,1)S(1)}, u32[]{:S(2)}, u32[]{:S(2)}) %collective-permute-start.2) | collective-permute-done | bytes 24608 | tf_op jit(solution)/shard_map/ppermute | solution.py:396
  10.7 0.3 %collective-permute-start.3 = (bf16[144,128]{1,0:T(8,128)(2,1)S(1)}, bf16[144,128]{1,0:T(8,128)(2,1)S(1)}, u32[]{:S(2)}, u32[]{:S(2)}) collective-permute-start(bf16[144,128]{1,0:T(8,128)(2,1)S(1)} %constant_dynamic-update-slice_fusion.last), channel_id=1, source_target_pairs={{0,1},{1,0},{2,3},{3,2},{4,5},{5,4},{6,7},{7,6},{8,9},{9,8},{10,11... | collective-permute-start | bytes 110600 | tf_op jit(solution)/shard_map/ppermute | solution.py:406
  11.1 0.7 %shard_map.103 = (f32[512,384]{1,0:T(8,128)S(1)}, f32[160,128]{1,0:T(8,128)S(1)}, bf16[512,160]{1,0:T(8,128)(2,1)S(1)}) custom-call(bf16[512,768]{1,0:T(8,128)(2,1)S(1)} %get-tuple-element.38.picks, f32[512,384]{1,0:T(8,128)S(1)} %shard_map.102.partial, bf16[320,128]{1,0:T(8,128)(2,1)S(1)} %collective-permute-done.got, ...), custom_call_target="tpu_custom_call" | custom-call | flops 1000000000 | bytes 1798144 | tf_op jit(solution)/shard_map/pallas_call | solution.py:363
  11.8 0.3 %collective-permute-done.3.last = bf16[144,128]{1,0:T(8,128)(2,1)S(1)} collective-permute-done((bf16[144,128]{1,0:T(8,128)(2,1)S(1)}, bf16[144,128]{1,0:T(8,128)(2,1)S(1)}, u32[]{:S(2)}, u32[]{:S(2)}) %collective-permute-start.3) | collective-permute-done | bytes 36896 | tf_op jit(solution)/shard_map/ppermute | solution.py:406
  12.0 1.5 %shard_map.104 = (f32[512,512]{1,0:T(8,128)S(1)}, bf16[512,384]{1,0:T(8,128)(2,1)S(1)}, bf16[256,128]{1,0:T(8,128)(2,1)S(1)}, bf16[192,128]{1,0:T(8,128)(2,1)S(1...) custom-call(bf16[384,512]{1,0:T(8,128)(2,1)S(1)} %get-tuple-element.36.lift, ...), custom_call_target="tpu_custom_call" | custom-call | flops 1000000000 | bytes 3903488 | tf_op jit(solution)/shard_map/pallas_call | solution.py:363
  13.5 0.3 %collective-permute-start.4 = (bf16[256,128]{1,0:T(8,128)(2,1)S(1)}, bf16[256,128]{1,0:T(8,128)(2,1)S(1)}, u32[]{:S(2)}, u32[]{:S(2)}) collective-permute-start(bf16[256,128]{1,0:T(8,128)(2,1)S(1)} %get-tuple-element.51), channel_id=1, source_target_pairs={{0,1},{1,0},{2,3},{3,2},{4,5},{5,4},{6,7},{7,6},{8,9},{9,8},{10,11... | collective-permute-start | bytes 196616 | tf_op jit(solution)/shard_map/ppermute | solution.py:380
  13.8 1.5 %collective-permute-start.5 = (bf16[192,128]{1,0:T(8,128)(2,1)S(1)}, bf16[192,128]{1,0:T(8,128)(2,1)S(1)}, u32[]{:S(2)}, u32[]{:S(2)}) collective-permute-start(bf16[192,128]{1,0:T(8,128)(2,1)S(1)} %get-tuple-element.56), channel_id=1, source_target_pairs={{0,16},{1,2},{2,1},{3,4},{4,3},{5,6},{6,5},{7,8},{8,7},{9,10},{10,... | collective-permute-start | bytes 147464 | tf_op jit(solution)/shard_map/ppermute | solution.py:391
  15.3 0.9 %collective-permute-start.6 = (bf16[64,128]{1,0:T(8,128)(2,1)S(1)}, bf16[64,128]{1,0:T(8,128)(2,1)S(1)}, u32[]{:S(2)}, u32[]{:S(2)}) collective-permute-start(bf16[64,128]{1,0:T(8,128)(2,1)S(1)} %pad_maximum_fusion.3), channel_id=1, source_target_pairs={{0,16},{1,2},{2,1},{3,4},{4,3},{5,6},{6,5},{7,8},{8,7},{9,10},{10,... | collective-permute-start | bytes 49160 | tf_op jit(solution)/shard_map/ppermute | solution.py:395
  16.3 1.2 %collective-permute-start.7 = (bf16[64,128]{1,0:T(8,128)(2,1)S(1)}, bf16[64,128]{1,0:T(8,128)(2,1)S(1)}, u32[]{:S(2)}, u32[]{:S(2)}) collective-permute-start(bf16[64,128]{1,0:T(8,128)(2,1)S(1)} %pad_maximum_fusion.4), channel_id=1, source_target_pairs={{0,16},{1,4},{2,18},{3,6},{4,1},{5,8},{6,3},{7,10},{8,5},{9,12},{1... | collective-permute-start | bytes 49160 | tf_op jit(solution)/shard_map/ppermute | solution.py:396
  17.4 2.1 %shard_map.105 = (f32[512,512]{1,0:T(8,128)S(1)}, f32[512,384]{1,0:T(8,128)S(1)}, bf16[16,128]{1,0:T(8,128)(2,1)S(1)}) custom-call(f32[512,128]{1,0:T(8,128)S(1)} %get-tuple-element.33.column, f32[512,512]{1,0:T(8,128)S(1)} %copy-done, f32[512,512]{1,0:T(8,128)S(1)} %get-tuple-element.48.field, bf16[512,1536]{1,0:T(8,128)(2,1)S(1)} %get-tuple-element.49.stiffness, ...), custom_call_target="tpu_custom_call" | custom-call | flops 100000000 | bytes 100000 | tf_op jit(solution)/shard_map/pallas_call | solution.py:363
  19.5 0.5 %collective-permute-done.7.far = bf16[64,128]{1,0:T(8,128)(2,1)S(1)} collective-permute-done((bf16[64,128]{1,0:T(8,128)(2,1)S(1)}, bf16[64,128]{1,0:T(8,128)(2,1)S(1)}, u32[]{:S(2)}, u32[]{:S(2)}) %collective-permute-start.7) | collective-permute-done | bytes 16416 | tf_op jit(solution)/shard_map/ppermute | solution.py:396
  20.0 0.4 %collective-permute-start.8 = (bf16[112,128]{1,0:T(8,128)(2,1)S(1)}, bf16[112,128]{1,0:T(8,128)(2,1)S(1)}, u32[]{:S(2)}, u32[]{:S(2)}) collective-permute-start(bf16[112,128]{1,0:T(8,128)(2,1)S(1)} %pad_maximum_fusion.1.last), channel_id=1, source_target_pairs={{0,1},{1,0},{2,3},{3,2},{4,5},{5,4},{6,7},{7,6},{8,9},{9,8},{10,11... | collective-permute-start | bytes 86024 | tf_op jit(solution)/shard_map/ppermute | solution.py:406
  20.4 0.0 collective-permute-done.5.rim
  20.4 0.6 %shard_map.106.partial = f32[512,384]{1,0:T(8,128)S(1)} custom-call(bf16[512,768]{1,0:T(8,128)(2,1)S(1)} %get-tuple-element.38.picks, f32[512,384]{1,0:T(8,128)S(1)} %get-tuple-element.53.partial, f32[160,128]{1,0:T(8,128)S(1)} %get-tuple-element.54.face, bf16[512,160]{1,0:T(8,128)(2,1)S(1)} %get-tuple-element.55.element_hot, ...), custom_call_target="tpu_custom_call" | custom-call | flops 1000000000 | bytes 1994752 | tf_op jit(solution)/shard_map/pallas_call | solution.py:363
  21.0 0.3 %collective-permute-done.8.last = bf16[112,128]{1,0:T(8,128)(2,1)S(1)} collective-permute-done((bf16[112,128]{1,0:T(8,128)(2,1)S(1)}, bf16[112,128]{1,0:T(8,128)(2,1)S(1)}, u32[]{:S(2)}, u32[]{:S(2)}) %collective-permute-start.8) | collective-permute-done | bytes 28704 | tf_op jit(solution)/shard_map/ppermute | solution.py:406
  21.3 1.4 %shard_map.107 = f32[512,512]{1,0:T(8,128)} custom-call(bf16[384,512]{1,0:T(8,128)(2,1)S(1)} %get-tuple-element.36.lift, f32[512,512]{1,0:T(8,128)S(1)} %get-tuple-element.52.base, f32[512,384]{1,0:T(8,128)S(1)} %shard_map.106.partial, f32[512,384]{1,0:T(8,128)S(1)} %get-tuple-element.43.inflow, bf16[112,128]{1,0:T(8,128)(2,1)S(1)} %collective-permute-done.8.last, ...), custom_call_target="tpu_custom_call" | custom-call | flops 1000000000 | bytes 3190784 | tf_op jit(solution)/shard_map/pallas_call | solution.py:363
  (22 shorter events, 0.1 us)
Async XLA Ops:
  2.5 1.7 %collective-permute-start = (bf16[320,128]{1,0:T(8,128)(2,1)S(1)}, bf16[320,128]{1,0:T(8,128)(2,1)S(1)}, u32[]{:S(2)}, u32[]{:S(2)}) collective-permute-start(bf16[320,128]{1,0:T(8,128)(2,1)S(1)} %get-tuple-element.35), channel_id=1, source_target_pairs={{0,1},{1,0},{2,3},{3,2},{4,5},{5,4},{6,7},{7,6},{8,9},{9,8},{10,11... | collective-permute-start | bytes 245768 | tf_op jit(solution)/shard_map/ppermute | solution.py:380
  4.2 5.2 %collective-permute-start.1 = (bf16[320,128]{1,0:T(8,128)(2,1)S(1)}, bf16[320,128]{1,0:T(8,128)(2,1)S(1)}, u32[]{:S(2)}, u32[]{:S(2)}) collective-permute-start(bf16[320,128]{1,0:T(8,128)(2,1)S(1)} %pad_maximum_fusion), channel_id=1, source_target_pairs={{0,16},{1,2},{2,1},{3,4},{4,3},{5,6},{6,5},{7,8},{8,7},{9,10},{10,... | collective-permute-start | bytes 245768 | tf_op jit(solution)/shard_map/ppermute | solution.py:395
  6.9 3.8 %collective-permute-start.2 = (bf16[96,128]{1,0:T(8,128)(2,1)S(1)}, bf16[96,128]{1,0:T(8,128)(2,1)S(1)}, u32[]{:S(2)}, u32[]{:S(2)}) collective-permute-start(bf16[96,128]{1,0:T(8,128)(2,1)S(1)} %pad_maximum_fusion.2), channel_id=1, source_target_pairs={{0,16},{1,4},{2,18},{3,6},{4,1},{5,8},{6,3},{7,10},{8,5},{9,12},{1... | collective-permute-start | bytes 73736 | tf_op jit(solution)/shard_map/ppermute | solution.py:396
  10.7 1.3 %collective-permute-start.3 = (bf16[144,128]{1,0:T(8,128)(2,1)S(1)}, bf16[144,128]{1,0:T(8,128)(2,1)S(1)}, u32[]{:S(2)}, u32[]{:S(2)}) collective-permute-start(bf16[144,128]{1,0:T(8,128)(2,1)S(1)} %constant_dynamic-update-slice_fusion.last), channel_id=1, source_target_pairs={{0,1},{1,0},{2,3},{3,2},{4,5},{5,4},{6,7},{7,6},{8,9},{9,8},{10,11... | collective-permute-start | bytes 110600 | tf_op jit(solution)/shard_map/ppermute | solution.py:406
  12.0 5.4 %copy-start = (f32[512,512]{1,0:T(8,128)S(1)}, f32[512,512]{1,0:T(8,128)}, u32[]{:S(2)}) copy-start(f32[512,512]{1,0:T(8,128)} %state.1) | copy-start | bytes 3145732
  13.5 1.9 %collective-permute-start.4 = (bf16[256,128]{1,0:T(8,128)(2,1)S(1)}, bf16[256,128]{1,0:T(8,128)(2,1)S(1)}, u32[]{:S(2)}, u32[]{:S(2)}) collective-permute-start(bf16[256,128]{1,0:T(8,128)(2,1)S(1)} %get-tuple-element.51), channel_id=1, source_target_pairs={{0,1},{1,0},{2,3},{3,2},{4,5},{5,4},{6,7},{7,6},{8,9},{9,8},{10,11... | collective-permute-start | bytes 196616 | tf_op jit(solution)/shard_map/ppermute | solution.py:380
  13.8 6.6 %collective-permute-start.5 = (bf16[192,128]{1,0:T(8,128)(2,1)S(1)}, bf16[192,128]{1,0:T(8,128)(2,1)S(1)}, u32[]{:S(2)}, u32[]{:S(2)}) collective-permute-start(bf16[192,128]{1,0:T(8,128)(2,1)S(1)} %get-tuple-element.56), channel_id=1, source_target_pairs={{0,16},{1,2},{2,1},{3,4},{4,3},{5,6},{6,5},{7,8},{8,7},{9,10},{10,... | collective-permute-start | bytes 147464 | tf_op jit(solution)/shard_map/ppermute | solution.py:391
  15.3 4.2 %collective-permute-start.6 = (bf16[64,128]{1,0:T(8,128)(2,1)S(1)}, bf16[64,128]{1,0:T(8,128)(2,1)S(1)}, u32[]{:S(2)}, u32[]{:S(2)}) collective-permute-start(bf16[64,128]{1,0:T(8,128)(2,1)S(1)} %pad_maximum_fusion.3), channel_id=1, source_target_pairs={{0,16},{1,2},{2,1},{3,4},{4,3},{5,6},{6,5},{7,8},{8,7},{9,10},{10,... | collective-permute-start | bytes 49160 | tf_op jit(solution)/shard_map/ppermute | solution.py:395
  16.3 3.7 %collective-permute-start.7 = (bf16[64,128]{1,0:T(8,128)(2,1)S(1)}, bf16[64,128]{1,0:T(8,128)(2,1)S(1)}, u32[]{:S(2)}, u32[]{:S(2)}) collective-permute-start(bf16[64,128]{1,0:T(8,128)(2,1)S(1)} %pad_maximum_fusion.4), channel_id=1, source_target_pairs={{0,16},{1,4},{2,18},{3,6},{4,1},{5,8},{6,3},{7,10},{8,5},{9,12},{1... | collective-permute-start | bytes 49160 | tf_op jit(solution)/shard_map/ppermute | solution.py:396
  20.0 1.3 %collective-permute-start.8 = (bf16[112,128]{1,0:T(8,128)(2,1)S(1)}, bf16[112,128]{1,0:T(8,128)(2,1)S(1)}, u32[]{:S(2)}, u32[]{:S(2)}) collective-permute-start(bf16[112,128]{1,0:T(8,128)(2,1)S(1)} %pad_maximum_fusion.1.last), channel_id=1, source_target_pairs={{0,1},{1,0},{2,3},{3,2},{4,5},{5,4},{6,7},{7,6},{8,9},{9,8},{10,11... | collective-permute-start | bytes 86024 | tf_op jit(solution)/shard_map/ppermute | solution.py:406

commit v12 on v11

--- a/solution.py
+++ b/solution.py
@@ -119,7 +119,7 @@
 
 def start_kernel(
     state_in, trace_map_in, records_in, counts_in, velocity_in, levels_in, neighbours_in, projection_in,
-    state, trace_map, projection, traces, first_out, own_out, source_hot, column, elements_column,
+    state, trace_map, projection, traces, first_out, own_out, source_hot, column, elements_column, local,
     records, counts, velocity, levels, neighbours, blocks, sems
 ):
     elements = state.shape[0]
@@ -138,7 +138,7 @@
     columns = record_columns(records, counts)
     column[...] = columns
     source_hot[...] = hot(columns[:, 0:1], elements)
-    elements_column[...] = element_columns(velocity, levels, neighbours)
+    elements_column[...] = element_columns(velocity, levels, neighbours, local)
     copies[5].wait()
     for i in range(2):
         copies[6 + i].wait()
@@ -148,12 +148,14 @@
     send(traces, source_hot[...], column, projection, first_out, own_out, own_out, blocks, True)
 
 
-def element_columns(velocity, levels, neighbours):
+def element_columns(velocity, levels, neighbours, local_out):
     elements = velocity.shape[1]
     rim = elements // 8
     chip, core = place()
     raw = neighbours[...].astype(f32)
     local = raw - ((2 * chip + core) * elements).astype(f32)
+    local_out[0:6, :] = local
+    local_out[6:, :] = jnp.zeros((2, elements), f32)
     before = ((2 - core) * rim).astype(f32)
     after = (elements - core * rim).astype(f32)
     index = jnp.where(local < 0, local + before, jnp.where(local >= elements, local - after, -1.0))
@@ -171,18 +173,23 @@
     return column[:, 3:4] * volume
 
 
-def own_part(column, traces, partial_out):
+def own_part(local, traces, partial):
     elements = traces.shape[0]
+    element = rows_of((elements, elements))
     for t in range(3):
-        tile = traces[:, 128 * t : 128 * t + 128]
-        at = 8 + 2 * t
-        picks = [hot(column[:, at + i : at + i + 1], elements) for i in range(2)]
-        near = dot(jnp.concatenate(picks, axis=1), swapped(tile))
-        partial_out[:, 128 * t : 128 * t + 128] = near - tile.astype(f32)
-
-
-def own_kernel(column, traces, partial):
-    own_part(column[...], traces, partial)
+        tile = traces[:, 128 * t : 128 * t + 128].astype(f32)
+        turned = tile.T.astype(bf16)
+        parts = []
+        for i in range(2):
+            face = 2 * t + i
+            picked = jnp.where(element == local[face : face + 1, :].astype(jnp.int32), 1.0, 0.0).astype(bf16)
+            parts.append(dot(turned[64 - 64 * i : 128 - 64 * i, :], picked))
+        near = jnp.concatenate(parts, axis=0).astype(bf16).T
+        partial[:, 128 * t : 128 * t + 128] = near.astype(f32) - tile
+
+
+def own_kernel(local, traces, partial):
+    own_part(local, traces, partial)
 
 
 def local_kernel(stiffness_in, lift_in, column, state, got, stiffness, lift, base, inflow, picks, token, sems):
@@ -210,7 +217,7 @@
     copies[1].wait()
 
 
-def second_local_kernel(column, state, field, stiffness, traces, got, base, partial, token):
+def second_local_kernel(column, local, state, field, stiffness, traces, got, base, partial, token):
     token[...] = got[0:16, :]
     modes = state.shape[1]
     columns = column[...]
@@ -219,7 +226,7 @@
     for n in range(0, modes, step):
         volume = volume_term(columns, lowered, stiffness, n, step)
         base[:, n : n + step] = 0.5 * (state[:, n : n + step] + field[:, n : n + step]) + 0.5 * time_step * volume
-    own_part(columns, traces, partial)
+    own_part(local, traces, partial)
 
 
 def direct_pieces(got, near, far, arrived):
@@ -439,11 +446,11 @@
     levels = levels.reshape(1, elements)
     vmem = pltpu.VMEM
     wide = (elements, 128)
-    near_state, trace_map, projection, traces, first, own, source_hot, column, element_column = call(
+    near_state, trace_map, projection, traces, first, own, source_hot, column, element_column, local_rows = call(
         start_kernel,
         [like(state), like(trace_map), like(projection)]
         + sent
-        + [array((slots, elements), bf16), column_shape, array(wide, f32)],
+        + [array((slots, elements), bf16), column_shape, array(wide, f32), array((8, elements), f32)],
         [vmem(x.shape, x.dtype) for x in (records, counts, velocity, levels, neighbours)]
         + [blocks, pltpu.SemaphoreType.DMA((9,))],
         2 * 10**8,
@@ -451,7 +458,7 @@
         (),
     )
 
-    partial = call(own_kernel, [faces], [], 10**8, (), (element_column, traces))[0]
+    partial = call(own_kernel, [faces], [], 10**8, (), (local_rows, traces))[0]
 
     def local(got):
         return call(
@@ -492,7 +499,7 @@
             [],
             10**8,
             (),
-            (element_column, state, field, stiffness, traces, got),
+            (element_column, local_rows, state, field, stiffness, traces, got),
         )
 
     def second_direct(results, *arrived):

time: 22.9 us -> 22.6 us (0.987)
  Pallas kernels: 12.3 us -> 11.9 us
  waiting for transfers between devices: 2.25 us -> 2.61 us
  starting transfers between devices: 7.96 us -> 7.66 us
    pallas_call x8, Pallas kernels: 12.3 us -> 11.9 us  [call(): pl.pallas_call(kernel, out_shape=out_shape, in_specs=specs, out_specs=[pl...]
    ppermute x2, starting transfers between devices: 0.74 us -> 0.45 us  [exchange(): return (lax.ppermute(last, axes, cores), totals, results)]
    ppermute x2, waiting for transfers between devices: 0.53 us -> 0.76 us  [exchange(): return (lax.ppermute(last, axes, cores), totals, results)]
  transfers between devices with their start and end apart: 9 -> 9, of which waited for: 4 -> 4; matrix products, arithmetic and copies ran while one was open for 0% -> 0% of each run, Pallas kernels for 30% -> 29%
where the time goes in v12:
time: 22.6 us; the launch traced here: 22.5 us
  Pallas kernels  11.9 us (53%)
  starting transfers between devices  7.66 us (34%)
  waiting for transfers between devices  2.61 us (12%)
    pallas_call x8, Pallas kernels, call(): pl.pallas_call(kernel, out_shape=out_shape, in_specs=specs, out_specs=[pl...  11.9 us
    ppermute x2, starting transfers between devices, exchange(): near = lax.ppermute(near, axes, chips)  3.73 us
    ppermute x2, waiting for transfers between devices, exchange(): far = lax.ppermute(far, axes, far_chips)  1.84 us
    ppermute x1, starting transfers between devices, exchange(): rim = lax.ppermute(rim, axes, chips)  1.46 us
    ppermute x2, starting transfers between devices, exchange(): far = lax.ppermute(far, axes, far_chips)  1.28 us
    ppermute x2, waiting for transfers between devices, exchange(): return (lax.ppermute(last, axes, cores), totals, results)  0.76 us
    ppermute x2, starting transfers between devices, exchange(): got = lax.ppermute(first, axes, cores)  0.74 us
  transfers between devices with their start and end apart: 9, of which 4 were waited for; matrix products, arithmetic and copies ran while one was open for 0% of the time, Pallas kernels for 29%

profile of v12, /device:TPU:0, one launch (start us, length us, event | category | flops | bytes accessed | tf_op | source)
XLA Modules:
  0.0 22.5 jit_solution(3934420003649015203)
XLA Ops:
  0.0 2.5 %shard_map.100 = (f32[512,512]{1,0:T(8,128)S(1)}, bf16[512,384]{1,0:T(8,128)(2,1)S(1)}, bf16[64,512]{1,0:T(8,128)(2,1)S(1)}, bf16[512,384]{1,0:T(8,128)(2,1)S(1)...) custom-call(f32[512,512]{1,0:T(8,128)} %state.1, ...), custom_call_target="tpu_custom_call" | custom-call | flops 200000000 | bytes 1531936 | tf_op jit(solution)/shard_map/pallas_call | solution.py:370
  2.5 0.5 %collective-permute-start = (bf16[320,128]{1,0:T(8,128)(2,1)S(1)}, bf16[320,128]{1,0:T(8,128)(2,1)S(1)}, u32[]{:S(2)}, u32[]{:S(2)}) collective-permute-start(bf16[320,128]{1,0:T(8,128)(2,1)S(1)} %get-tuple-element.36), channel_id=1, source_target_pairs={{0,1},{1,0},{2,3},{3,2},{4,5},{5,4},{6,7},{7,6},{8,9},{9,8},{10,11... | collective-permute-start | bytes 245768 | tf_op jit(solution)/shard_map/ppermute | solution.py:387
  3.0 1.0 %shard_map.102.partial = f32[512,384]{1,0:T(8,128)S(1)} custom-call(f32[8,512]{1,0:T(8,128)S(1)} %get-tuple-element.38.local, bf16[512,384]{1,0:T(8,128)(2,1)S(1)} %get-tuple-element.41.traces), custom_call_target="tpu_custom_call" | custom-call | flops 100000000 | bytes 100000 | tf_op jit(solution)/shard_map/pallas_call | solution.py:370
  4.0 0.0 collective-permute-done.got
  4.0 2.8 %collective-permute-start.1 = (bf16[320,128]{1,0:T(8,128)(2,1)S(1)}, bf16[320,128]{1,0:T(8,128)(2,1)S(1)}, u32[]{:S(2)}, u32[]{:S(2)}) collective-permute-start(bf16[320,128]{1,0:T(8,128)(2,1)S(1)} %pad_maximum_fusion), channel_id=1, source_target_pairs={{0,16},{1,2},{2,1},{3,4},{4,3},{5,6},{6,5},{7,8},{8,7},{9,10},{10,... | collective-permute-start | bytes 245768 | tf_op jit(solution)/shard_map/ppermute | solution.py:402
  6.9 0.1 collective-permute-start.2
  7.0 2.4 %shard_map.101 = (bf16[512,1536]{1,0:T(8,128)(2,1)S(1)}, bf16[384,512]{1,0:T(8,128)(2,1)S(1)}, f32[512,512]{1,0:T(8,128)S(1)}, f32[512,384]{1,0:T(8,128)S(1)}, b...) custom-call(bf16[512,1536]{1,0:T(8,128)(2,1)} %stiffness_in.1, bf16[384,512]{1,0:T(8,128)(2,1)} %lift_in.1, ...), custom_call_target="tpu_custom_call" | custom-call | flops 100000000 | bytes 100000 | tf_op jit(solution)/shard_map/pallas_call | solution.py:370
  9.4 0.0 collective-permute-done.1.near
  9.5 1.2 %collective-permute-done.2.far = bf16[96,128]{1,0:T(8,128)(2,1)S(1)} collective-permute-done((bf16[96,128]{1,0:T(8,128)(2,1)S(1)}, bf16[96,128]{1,0:T(8,128)(2,1)S(1)}, u32[]{:S(2)}, u32[]{:S(2)}) %collective-permute-start.2) | collective-permute-done | bytes 24608 | tf_op jit(solution)/shard_map/ppermute | solution.py:403
  10.7 0.2 collective-permute-start.3
  10.9 0.7 %shard_map.103 = (f32[512,384]{1,0:T(8,128)S(1)}, f32[160,128]{1,0:T(8,128)S(1)}, bf16[512,160]{1,0:T(8,128)(2,1)S(1)}) custom-call(bf16[512,768]{1,0:T(8,128)(2,1)S(1)} %get-tuple-element.40.picks, f32[512,384]{1,0:T(8,128)S(1)} %shard_map.102.partial, bf16[320,128]{1,0:T(8,128)(2,1)S(1)} %collective-permute-done.got, ...), custom_call_target="tpu_custom_call" | custom-call | flops 1000000000 | bytes 1798144 | tf_op jit(solution)/shard_map/pallas_call | solution.py:370
  11.6 0.4 %collective-permute-done.3.last = bf16[144,128]{1,0:T(8,128)(2,1)S(1)} collective-permute-done((bf16[144,128]{1,0:T(8,128)(2,1)S(1)}, bf16[144,128]{1,0:T(8,128)(2,1)S(1)}, u32[]{:S(2)}, u32[]{:S(2)}) %collective-permute-start.3) | collective-permute-done | bytes 36896 | tf_op jit(solution)/shard_map/ppermute | solution.py:413
  12.0 1.5 %shard_map.104 = (f32[512,512]{1,0:T(8,128)S(1)}, bf16[512,384]{1,0:T(8,128)(2,1)S(1)}, bf16[256,128]{1,0:T(8,128)(2,1)S(1)}, bf16[192,128]{1,0:T(8,128)(2,1)S(1...) custom-call(bf16[384,512]{1,0:T(8,128)(2,1)S(1)} %get-tuple-element.37.lift, ...), custom_call_target="tpu_custom_call" | custom-call | flops 1000000000 | bytes 3903488 | tf_op jit(solution)/shard_map/pallas_call | solution.py:370
  13.5 0.2 collective-permute-start.4
  13.7 1.5 %collective-permute-start.5 = (bf16[192,128]{1,0:T(8,128)(2,1)S(1)}, bf16[192,128]{1,0:T(8,128)(2,1)S(1)}, u32[]{:S(2)}, u32[]{:S(2)}) collective-permute-start(bf16[192,128]{1,0:T(8,128)(2,1)S(1)} %get-tuple-element.58), channel_id=1, source_target_pairs={{0,16},{1,2},{2,1},{3,4},{4,3},{5,6},{6,5},{7,8},{8,7},{9,10},{10,... | collective-permute-start | bytes 147464 | tf_op jit(solution)/shard_map/ppermute | solution.py:398
  15.2 0.0 collective-permute-done.4.got
  15.2 0.9 %collective-permute-start.6 = (bf16[64,128]{1,0:T(8,128)(2,1)S(1)}, bf16[64,128]{1,0:T(8,128)(2,1)S(1)}, u32[]{:S(2)}, u32[]{:S(2)}) collective-permute-start(bf16[64,128]{1,0:T(8,128)(2,1)S(1)} %pad_maximum_fusion.3), channel_id=1, source_target_pairs={{0,16},{1,2},{2,1},{3,4},{4,3},{5,6},{6,5},{7,8},{8,7},{9,10},{10,... | collective-permute-start | bytes 49160 | tf_op jit(solution)/shard_map/ppermute | solution.py:402
  16.1 1.2 %collective-permute-start.7 = (bf16[64,128]{1,0:T(8,128)(2,1)S(1)}, bf16[64,128]{1,0:T(8,128)(2,1)S(1)}, u32[]{:S(2)}, u32[]{:S(2)}) collective-permute-start(bf16[64,128]{1,0:T(8,128)(2,1)S(1)} %pad_maximum_fusion.4), channel_id=1, source_target_pairs={{0,16},{1,4},{2,18},{3,6},{4,1},{5,8},{6,3},{7,10},{8,5},{9,12},{1... | collective-permute-start | bytes 49160 | tf_op jit(solution)/shard_map/ppermute | solution.py:403
  17.3 1.9 %shard_map.105 = (f32[512,512]{1,0:T(8,128)S(1)}, f32[512,384]{1,0:T(8,128)S(1)}, bf16[16,128]{1,0:T(8,128)(2,1)S(1)}) custom-call(f32[512,128]{1,0:T(8,128)S(1)} %get-tuple-element.34.column, f32[8,512]{1,0:T(8,128)S(1)} %get-tuple-element.38.local, f32[512,512]{1,0:T(8,128)S(1)} %copy-done, f32[512,512]{1,0:T(8,128)S(1)} %get-tuple-element.50.field, ...), custom_call_target="tpu_custom_call" | custom-call | flops 100000000 | bytes 100000 | tf_op jit(solution)/shard_map/pallas_call | solution.py:370
  19.2 0.6 %collective-permute-done.7.far = bf16[64,128]{1,0:T(8,128)(2,1)S(1)} collective-permute-done((bf16[64,128]{1,0:T(8,128)(2,1)S(1)}, bf16[64,128]{1,0:T(8,128)(2,1)S(1)}, u32[]{:S(2)}, u32[]{:S(2)}) %collective-permute-start.7) | collective-permute-done | bytes 16416 | tf_op jit(solution)/shard_map/ppermute | solution.py:403
  19.8 0.3 %collective-permute-start.8 = (bf16[112,128]{1,0:T(8,128)(2,1)S(1)}, bf16[112,128]{1,0:T(8,128)(2,1)S(1)}, u32[]{:S(2)}, u32[]{:S(2)}) collective-permute-start(bf16[112,128]{1,0:T(8,128)(2,1)S(1)} %pad_maximum_fusion.1.last), channel_id=1, source_target_pairs={{0,1},{1,0},{2,3},{3,2},{4,5},{5,4},{6,7},{7,6},{8,9},{9,8},{10,11... | collective-permute-start | bytes 86024 | tf_op jit(solution)/shard_map/ppermute | solution.py:413
  20.1 0.6 %shard_map.106.partial = f32[512,384]{1,0:T(8,128)S(1)} custom-call(bf16[512,768]{1,0:T(8,128)(2,1)S(1)} %get-tuple-element.40.picks, f32[512,384]{1,0:T(8,128)S(1)} %get-tuple-element.55.partial, f32[160,128]{1,0:T(8,128)S(1)} %get-tuple-element.56.face, bf16[512,160]{1,0:T(8,128)(2,1)S(1)} %get-tuple-element.57.element_hot, ...), custom_call_target="tpu_custom_call" | custom-call | flops 1000000000 | bytes 1994752 | tf_op jit(solution)/shard_map/pallas_call | solution.py:370
  20.7 0.3 %collective-permute-done.8.last = bf16[112,128]{1,0:T(8,128)(2,1)S(1)} collective-permute-done((bf16[112,128]{1,0:T(8,128)(2,1)S(1)}, bf16[112,128]{1,0:T(8,128)(2,1)S(1)}, u32[]{:S(2)}, u32[]{:S(2)}) %collective-permute-start.8) | collective-permute-done | bytes 28704 | tf_op jit(solution)/shard_map/ppermute | solution.py:413
  21.0 1.4 %shard_map.107 = f32[512,512]{1,0:T(8,128)} custom-call(bf16[384,512]{1,0:T(8,128)(2,1)S(1)} %get-tuple-element.37.lift, f32[512,512]{1,0:T(8,128)S(1)} %get-tuple-element.54.base, f32[512,384]{1,0:T(8,128)S(1)} %shard_map.106.partial, f32[512,384]{1,0:T(8,128)S(1)} %get-tuple-element.45.inflow, bf16[112,128]{1,0:T(8,128)(2,1)S(1)} %collective-permute-done.8.last, ...), custom_call_target="tpu_custom_call" | custom-call | flops 1000000000 | bytes 3190784 | tf_op jit(solution)/shard_map/pallas_call | solution.py:370
  (22 shorter events, 0.1 us)
Async XLA Ops:
  2.5 1.5 %collective-permute-start = (bf16[320,128]{1,0:T(8,128)(2,1)S(1)}, bf16[320,128]{1,0:T(8,128)(2,1)S(1)}, u32[]{:S(2)}, u32[]{:S(2)}) collective-permute-start(bf16[320,128]{1,0:T(8,128)(2,1)S(1)} %get-tuple-element.36), channel_id=1, source_target_pairs={{0,1},{1,0},{2,3},{3,2},{4,5},{5,4},{6,7},{7,6},{8,9},{9,8},{10,11... | collective-permute-start | bytes 245768 | tf_op jit(solution)/shard_map/ppermute | solution.py:387
  4.0 5.4 %collective-permute-start.1 = (bf16[320,128]{1,0:T(8,128)(2,1)S(1)}, bf16[320,128]{1,0:T(8,128)(2,1)S(1)}, u32[]{:S(2)}, u32[]{:S(2)}) collective-permute-start(bf16[320,128]{1,0:T(8,128)(2,1)S(1)} %pad_maximum_fusion), channel_id=1, source_target_pairs={{0,16},{1,2},{2,1},{3,4},{4,3},{5,6},{6,5},{7,8},{8,7},{9,10},{10,... | collective-permute-start | bytes 245768 | tf_op jit(solution)/shard_map/ppermute | solution.py:402
  6.9 3.8 %collective-permute-start.2 = (bf16[96,128]{1,0:T(8,128)(2,1)S(1)}, bf16[96,128]{1,0:T(8,128)(2,1)S(1)}, u32[]{:S(2)}, u32[]{:S(2)}) collective-permute-start(bf16[96,128]{1,0:T(8,128)(2,1)S(1)} %pad_maximum_fusion.2), channel_id=1, source_target_pairs={{0,16},{1,4},{2,18},{3,6},{4,1},{5,8},{6,3},{7,10},{8,5},{9,12},{1... | collective-permute-start | bytes 73736 | tf_op jit(solution)/shard_map/ppermute | solution.py:403
  10.7 1.3 %collective-permute-start.3 = (bf16[144,128]{1,0:T(8,128)(2,1)S(1)}, bf16[144,128]{1,0:T(8,128)(2,1)S(1)}, u32[]{:S(2)}, u32[]{:S(2)}) collective-permute-start(bf16[144,128]{1,0:T(8,128)(2,1)S(1)} %constant_dynamic-update-slice_fusion.last), channel_id=1, source_target_pairs={{0,1},{1,0},{2,3},{3,2},{4,5},{5,4},{6,7},{7,6},{8,9},{9,8},{10,11... | collective-permute-start | bytes 110600 | tf_op jit(solution)/shard_map/ppermute | solution.py:413
  12.0 5.2 %copy-start = (f32[512,512]{1,0:T(8,128)S(1)}, f32[512,512]{1,0:T(8,128)}, u32[]{:S(2)}) copy-start(f32[512,512]{1,0:T(8,128)} %state.1) | copy-start | bytes 3145732
  13.5 1.7 %collective-permute-start.4 = (bf16[256,128]{1,0:T(8,128)(2,1)S(1)}, bf16[256,128]{1,0:T(8,128)(2,1)S(1)}, u32[]{:S(2)}, u32[]{:S(2)}) collective-permute-start(bf16[256,128]{1,0:T(8,128)(2,1)S(1)} %get-tuple-element.53), channel_id=1, source_target_pairs={{0,1},{1,0},{2,3},{3,2},{4,5},{5,4},{6,7},{7,6},{8,9},{9,8},{10,11... | collective-permute-start | bytes 196616 | tf_op jit(solution)/shard_map/ppermute | solution.py:387
  13.7 6.4 %collective-permute-start.5 = (bf16[192,128]{1,0:T(8,128)(2,1)S(1)}, bf16[192,128]{1,0:T(8,128)(2,1)S(1)}, u32[]{:S(2)}, u32[]{:S(2)}) collective-permute-start(bf16[192,128]{1,0:T(8,128)(2,1)S(1)} %get-tuple-element.58), channel_id=1, source_target_pairs={{0,16},{1,2},{2,1},{3,4},{4,3},{5,6},{6,5},{7,8},{8,7},{9,10},{10,... | collective-permute-start | bytes 147464 | tf_op jit(solution)/shard_map/ppermute | solution.py:398
  15.2 4.0 %collective-permute-start.6 = (bf16[64,128]{1,0:T(8,128)(2,1)S(1)}, bf16[64,128]{1,0:T(8,128)(2,1)S(1)}, u32[]{:S(2)}, u32[]{:S(2)}) collective-permute-start(bf16[64,128]{1,0:T(8,128)(2,1)S(1)} %pad_maximum_fusion.3), channel_id=1, source_target_pairs={{0,16},{1,2},{2,1},{3,4},{4,3},{5,6},{6,5},{7,8},{8,7},{9,10},{10,... | collective-permute-start | bytes 49160 | tf_op jit(solution)/shard_map/ppermute | solution.py:402
  16.1 3.7 %collective-permute-start.7 = (bf16[64,128]{1,0:T(8,128)(2,1)S(1)}, bf16[64,128]{1,0:T(8,128)(2,1)S(1)}, u32[]{:S(2)}, u32[]{:S(2)}) collective-permute-start(bf16[64,128]{1,0:T(8,128)(2,1)S(1)} %pad_maximum_fusion.4), channel_id=1, source_target_pairs={{0,16},{1,4},{2,18},{3,6},{4,1},{5,8},{6,3},{7,10},{8,5},{9,12},{1... | collective-permute-start | bytes 49160 | tf_op jit(solution)/shard_map/ppermute | solution.py:403
  19.8 1.2 %collective-permute-start.8 = (bf16[112,128]{1,0:T(8,128)(2,1)S(1)}, bf16[112,128]{1,0:T(8,128)(2,1)S(1)}, u32[]{:S(2)}, u32[]{:S(2)}) collective-permute-start(bf16[112,128]{1,0:T(8,128)(2,1)S(1)} %pad_maximum_fusion.1.last), channel_id=1, source_target_pairs={{0,1},{1,0},{2,3},{3,2},{4,5},{5,4},{6,7},{7,6},{8,9},{9,8},{10,11... | collective-permute-start | bytes 86024 | tf_op jit(solution)/shard_map/ppermute | solution.py:413
